TPU v7x, 128 devices: a whole 4x4x4 slice. The times are simulated.
128 devices in a mesh: store: 32 (over x, z, core), batch: 4 (over y).
Axes of the slice: x: 4, y: 4, z: 4, core: 2. Of those that a mesh axis runs over, the one named last changes fastest.
Arguments:
- features: bfloat16 [524288, 768], P(('store', 'batch')), may hold values from -6 to 6
- source_part: int32 [131072], P(('store', 'batch')), may hold values from 0 to 127, as said below
- source_row: int32 [131072], P(('store', 'batch')), may hold values from 0 to 4095
- adj_tiles: bfloat16 [6144, 128, 128], P(('store', 'batch')), may hold values from -0.25 to 0.25
- tile_row: int32 [6144], P(('store', 'batch')), may hold values from 0 to 7, as said below
- tile_col: int32 [6144], P(('store', 'batch')), may hold values from 0 to 7, as said below
- tile_count: int32 [128], P(('store', 'batch')), may hold values from 24 to 48
- labels: int32 [131072], P(('store', 'batch')), may hold values from 0 to 152
- layer_one: bfloat16 [768, 1024], replicated, may hold values from -0.21875 to 0.21875
- layer_two: bfloat16 [1024, 153], replicated
Outputs:
- grad_one: float32 [768, 1024], replicated
- grad_two: float32 [1024, 153], replicated
- loss: float32 [], replicated
Inputs may be any that keep to these rules, and one draw needn't show every extreme that they name: `source_part`: within each batch no storage owner appears more than 16 times, and every batch takes exactly 16 nodes from the owner with its own index. Within each batch the first 1024 // 128 tiles are the diagonal ones; the live tiles of a batch have pairwise different (tile_row, tile_col) pairs; entries at and beyond the batch's tile_count are 0. `tile_col`: as tile_row.
All inputs are finite; a program needn't handle non-finite values.
Results may differ from a plain program's by a relative error of at most 0.0065.
Values may be sent and summed in bfloat16 or wider, within the bound.
No kernel may reach another device: no remote copies, remote signals or barrier semaphores. Data moves between devices by JAX's collectives and lax.ppermute only.
A program may use at most 64 MiB of HBM per device.

v0:
```python
from functools import partial

import jax
import jax.numpy as jnp
from jax import lax
from jax.sharding import PartitionSpec as P


def densify(adj_tiles, tile_row, tile_col, live_count, nodes):
    tile = adj_tiles.shape[1]
    blocks = nodes // tile
    live = jnp.arange(tile_row.shape[0], dtype=jnp.int32) < live_count
    masked = jnp.where(live[:, None, None], adj_tiles, jnp.zeros_like(adj_tiles))
    grid = jnp.zeros((blocks, blocks, tile, tile), jnp.bfloat16).at[tile_row, tile_col].add(masked)
    return grid.transpose(0, 2, 1, 3).reshape(nodes, nodes)


def forward_spread(dense, values):
    return jnp.dot(dense, values, preferred_element_type=jnp.float32)


def backward_spread(dense, values):
    return lax.dot_general(
        dense, values, (((0,), (0,)), ((), ())), preferred_element_type=jnp.float32
    )


def on_device(
    features,
    source_part,
    source_row,
    adj_tiles,
    tile_row,
    tile_col,
    tile_count,
    labels,
    layer_one,
    layer_two,
):
    devices = lax.axis_size(("store", "batch"))
    nodes = source_part.shape[0]
    capacity = max(2, 2 * nodes // devices)
    owners = (source_part[:, None] == jnp.arange(devices, dtype=jnp.int32)[None, :]).astype(
        jnp.int32
    )
    ranking = jnp.cumsum(owners, axis=0) - 1
    source_slot = jnp.sum(owners * ranking, axis=1)
    position = source_part * capacity + source_slot
    requests = (
        jnp.zeros((devices * capacity,), jnp.int32)
        .at[position]
        .set(source_row)
        .reshape(devices, capacity)
    )
    found = features[
        lax.all_to_all(requests, ("store", "batch"), split_axis=0, concat_axis=0, tiled=True)
    ]
    arrived = lax.all_to_all(found, ("store", "batch"), split_axis=0, concat_axis=0, tiled=True)
    inputs = arrived.reshape(devices * capacity, features.shape[1])[position]
    dense = densify(adj_tiles, tile_row, tile_col, tile_count[0], nodes)
    mixed = forward_spread(dense, inputs).astype(jnp.bfloat16)
    before = jnp.dot(mixed, layer_one, preferred_element_type=jnp.float32)
    hidden = jax.nn.gelu(before, approximate=True).astype(jnp.bfloat16)
    smooth = forward_spread(dense, hidden).astype(jnp.bfloat16)
    logits = jnp.dot(smooth, layer_two, preferred_element_type=jnp.float32)
    largest = jnp.max(logits, axis=1, keepdims=True)
    logsum = jnp.log(jnp.sum(jnp.exp(logits - largest), axis=1, keepdims=True)) + largest
    truth = (labels[:, None] == jnp.arange(logits.shape[1], dtype=jnp.int32)[None, :]).astype(
        jnp.float32
    )
    batch_loss = jnp.mean(logsum[:, 0] - jnp.sum(truth * logits, axis=1))
    upstream = ((jnp.exp(logits - logsum) - truth) / logits.shape[0]).astype(jnp.bfloat16)
    grad_two = jnp.dot(smooth.T, upstream, preferred_element_type=jnp.float32)
    back_smooth = jnp.dot(upstream, layer_two.T, preferred_element_type=jnp.float32).astype(
        jnp.bfloat16
    )
    back_hidden = backward_spread(dense, back_smooth)
    back_before = jax.vjp(partial(jax.nn.gelu, approximate=True), before)[1](back_hidden)[0].astype(
        jnp.bfloat16
    )
    grad_one = jnp.dot(mixed.T, back_before, preferred_element_type=jnp.float32)
    grad_one, grad_two, batch_loss = lax.psum((grad_one, grad_two, batch_loss), ("store", "batch"))
    return (grad_one, grad_two, batch_loss)


def solution(mesh):
    return jax.shard_map(
        on_device,
        mesh=mesh,
        in_specs=(
            P(("store", "batch"), None),
            P(("store", "batch")),
            P(("store", "batch")),
            P(("store", "batch"), None, None),
            P(("store", "batch")),
            P(("store", "batch")),
            P(("store", "batch")),
            P(("store", "batch")),
            P(),
            P(),
        ),
        out_specs=(P(), P(), P()),
        check_vma=False,
    )
```

profile of v0, /device:TPU:1, one launch (start us, length us, event | category | flops | bytes accessed | tf_op | source)
XLA Modules:
  0.0 291.4 jit_solution(13792978811416294298)
XLA Ops:
  7.2 0.0 copy-start
  7.2 0.0 copy-start.5
  7.2 0.9 copy.17
  8.1 0.2 fusion.32
  8.4 0.1 copy.18
  8.5 0.0 copy-done.5
  8.5 0.4 fusion.31
  8.9 4.5 %scatter_custom_fusion.1 = s32[2048]{0:T(1024)S(1)} fusion(s32[1024]{0:T(1024)S(1)} %get-tuple-element.10, s32[1024]{0:T(1024)} %param.12, s32[]{:T(128)} %constant.17.clone.1), kind=kCustom, calls=%fused_computation.50 | custom fusion | bytes 8704 | tf_op jit(solution)/shard_map/scatter | solution.py:52
  13.4 0.1 all_to_all.11
  13.5 21.2 %all_to_all.17 = s32[128,1,16]{2,1,0:T(1,128)S(1)} all-to-all(s32[128,1,16]{2,1,0:T(1,128)S(1)} %bitcast.61), channel_id=1, replica_groups=mesh['store'=32,'batch'=4] {'store','batch'}, dimensions={0} | all-to-all | bytes 16384 | tf_op jit(solution)/shard_map/all_to_all | solution.py:56
  34.7 0.1 reshape.81
  34.8 13.7 %gather_fusion = bf16[2048,768]{1,0:T(8,128)(2,1)} fusion(bf16[4096,768]{1,0:T(8,128)(2,1)} %param.10, s32[2048]{0:T(1024)S(1)} %broadcast_clamp_fusion), kind=kCustom, calls=%fused_computation | custom fusion | bytes 6299648 | tf_op jit(solution)/shard_map/gather | solution.py:55
  48.4 0.0 copy-start.7
  48.4 0.0 copy-start.8
  48.4 5.0 %all-to-all-start.1 = ((bf16[128,16,768]{2,1,0:T(8,128)(2,1)}), bf16[128,16,768]{2,1,0:T(8,128)(2,1)}, u32[]{:S(2)}, u32[]{:S(2)}) async-start(bf16[128,16,768]{2,1,0:T(8,128)(2,1)} %bitcast.57), calls=%async_computation.1 | async-start | bytes 6291456 | tf_op jit(solution)/shard_map/all_to_all | solution.py:58
  53.4 0.0 all-reduce.3.cloned.1.call-start
  54.1 0.0 copy-done.7
  54.1 0.0 copy-done.8
  54.1 1.6 broadcast_select_fusion
  55.7 1.9 broadcast_in_dim.20
  57.6 9.7 %scatter_fusion = bf16[8,8,128,128]{3,2,1,0:T(8,128)(2,1)} fusion(bf16[8,8,128,128]{3,2,1,0:T(8,128)(2,1)} %broadcast_in_dim.20, s32[48]{0:T(128)S(1)} %fusion.40, bf16[48,128,128]{2,1,0:T(8,128)(2,1)S(1)} %broadcast_select_fusion), kind=kCustom, calls=%fused_computation.2 | custom fusion | flops 786432 | bytes 4718976 | tf_op jit(solution)/shard_map/scatter-add | solution.py:14
  67.3 4.3 %copy.16 = bf16[8,128,8,128]{3,2,1,0:T(8,128)(2,1)} copy(bf16[8,128,8,128]{3,1,2,0:T(8,128)(2,1)} %bitcast.56) | data formatting | bytes 4194304 | tf_op jit(solution)/shard_map/transpose | solution.py:15
  71.6 23.9 %all-to-all-done.1 = bf16[128,16,768]{2,1,0:T(8,128)(2,1)} async-done(((bf16[128,16,768]{2,1,0:T(8,128)(2,1)}), bf16[128,16,768]{2,1,0:T(8,128)(2,1)}, u32[]{:S(2)}, u32[]{:S(2)}) %all-to-all-start.1) | async-done | bytes 3145760 | tf_op jit(solution)/shard_map/all_to_all | solution.py:58
  95.5 6.9 %gather_fusion.1 = bf16[1024,768]{1,0:T(8,128)(2,1)S(1)} fusion(bf16[2048,768]{1,0:T(8,128)(2,1)} %bitcast.12, s32[1024]{0:T(1024)S(1)} %get-tuple-element.9), kind=kCustom, calls=%fused_computation.1 | custom fusion | bytes 3149824 | tf_op jit(solution)/shard_map/gather | solution.py:59
  102.4 3.4 %fusion.25 = bf16[1024,768]{1,0:T(8,128)(2,1)S(1)} fusion(bf16[1024,768]{1,0:T(8,128)(2,1)S(1)} %gather_fusion.1, bf16[128,8,8,128]{3,2,1,0:T(8,128)(2,1)} %bitcast.58), kind=kOutput, calls=%fused_computation.27 | convolution fusion | flops 1611399168 | bytes 5242880 | tf_op jit(solution)/shard_map/dot_general | solution.py:19
  105.8 0.0 copy-start.2
  105.8 1.2 copy-done.2
  107.0 0.0 copy-done
  107.0 0.0 copy-start.1
  107.1 1.8 fusion.47
  108.9 0.0 copy-done.1
  108.9 0.0 copy-start.9
  108.9 0.0 copy-start.4
  108.9 2.5 fusion.22
  111.4 0.0 copy-done.9
  111.4 0.0 copy-done.4
  111.4 0.0 copy-start.6
  111.4 0.9 fusion.46
  112.3 0.0 copy-done.6
  112.3 0.2 select_reduce_fusion
  112.5 0.6 subtract_reduce_fusion
  113.1 1.4 fusion.45
  114.4 9.6 %fusion.6 = bf16[1024,1024]{1,0:T(8,128)(2,1)} fusion(f32[1024,1024]{1,0:T(8,128)} %copy-done.9, bf16[1024,153]{0,1:T(8,128)(2,1)S(1)} %copy-done.4, bf16[128,8,8,128]{3,2,1,0:T(8,128)(2,1)} %bitcast.59, f32[1024,153]{0,1:T(8,128)S(1)} %get-tuple-element.12, s32[1024]{0:T(1024)S(1)} %copy-done.6, f32[1024]{0:T(1024)S(1)} %get-tuple-element.8), kind=kOutput, calls=%fused_computation.12 | convolution fusion | flops 2491308032 | bytes 9336832 | tf_op jit(solution)/shard_map/dot_general | solution.py:23
  124.0 5.8 %fusion.48 = f32[768,1024]{1,0:T(8,128)} fusion(bf16[1024,768]{1,0:T(8,128)(2,1)} %copy-done.2, bf16[1024,1024]{1,0:T(8,128)(2,1)} %fusion.6), kind=kOutput, calls=%fused_computation.70 | convolution fusion | flops 1610612736 | bytes 6815744 | tf_op jit(solution)/shard_map/dot_general | solution.py:81
  129.8 0.0 all-reduce.3.cloned.1.call-update
  130.5 63.7 %psum.23 = f32[]{:T(128)} all-reduce(f32[]{:T(128)S(6)} %div.11), channel_id=1, replica_groups=mesh['store'=32,'batch'=4] {'store','batch'}, use_global_device_ids=true, to_apply=%region_11.12 | all-reduce | flops 1 | bytes 8 | tf_op jit(solution)/shard_map/psum | solution.py:82
  194.2 85.5 %all-reduce.3.cloned.1.call-done = (f32[768,1024]{1,0:T(8,128)}, f32[1024,153]{0,1:T(8,128)}) async-done(((f32[768,1024]{1,0:T(8,128)}, f32[1024,153]{0,1:T(8,128)}), (f32[768,1024]{1,0:T(8,128)}, f32[1024,153]{0,1:T(8,128)})) %all-reduce.3.cloned.1.call-update) | async-done | bytes 3772432 | tf_op jit(solution)/shard_map/psum | solution.py:82
  279.6 0.0 copy-start.3
  279.6 4.0 %copy.37 = f32[768,1024]{1,0:T(8,128)} copy(f32[768,1024]{1,0:T(8,128)} %get-tuple-element.13) | data formatting | bytes 6291456
  283.7 0.0 copy-done.3
  283.7 0.8 copy.38
  (9 shorter events, 0.1 us)
Async XLA Ops:
  7.2 99.9 %copy-start = (bf16[768,1024]{1,0:T(8,128)(2,1)S(1)}, bf16[768,1024]{1,0:T(8,128)(2,1)}, u32[]{:S(2)}) copy-start(bf16[768,1024]{1,0:T(8,128)(2,1)} %param.18) | copy-start | bytes 4718596
  7.2 1.3 copy-start.5
  48.4 5.7 %copy-start.7 = (s32[48]{0:T(128)S(1)}, s32[48]{0:T(128)}, u32[]{:S(2)}) copy-start(s32[48]{0:T(128)} %param.15) | copy-start | bytes 580
  48.4 5.7 %copy-start.8 = (s32[48]{0:T(128)S(1)}, s32[48]{0:T(128)}, u32[]{:S(2)}) copy-start(s32[48]{0:T(128)} %param.14) | copy-start | bytes 580
  48.4 47.0 %all-to-all-start.1 = ((bf16[128,16,768]{2,1,0:T(8,128)(2,1)}), bf16[128,16,768]{2,1,0:T(8,128)(2,1)}, u32[]{:S(2)}, u32[]{:S(2)}) async-start(bf16[128,16,768]{2,1,0:T(8,128)(2,1)} %bitcast.57), calls=%async_computation.1 | async-start | bytes 6291456 | tf_op jit(solution)/shard_map/all_to_all | solution.py:58
  53.4 226.2 %all-reduce.3.cloned.1.call-start = ((), (), s32[]{:S(2)}) async-start(), calls=%async_computation.2 | async-start | bytes 7602176 | tf_op jit(solution)/shard_map/psum | solution.py:82
  105.8 1.2 copy-start.2
  107.0 1.8 copy-start.1
  108.9 2.5 copy-start.9
  108.9 2.5 copy-start.4
  111.4 0.9 copy-start.6
  279.6 4.0 %copy-start.3 = (f32[1024,153]{0,1:T(8,128)S(1)}, f32[1024,153]{0,1:T(8,128)}, u32[]{:S(2)}) copy-start(f32[1024,153]{0,1:T(8,128)} %get-tuple-element.14) | copy-start | bytes 1880068
Sparse Core Ops, SparseCore 0:
  130.0 149.6 all-reduce.2
where the time goes:
time: 292 us; the launch traced here: 291 us
  waiting for transfers between devices  109 us (37%)
  blocking collectives  84.8 us (29%)
  local copies, waits for them, and re-layouts  38.5 us (13%)
  matrix products  25.3 us (9%)
  between operations  15.6 us (5%)
  other arithmetic  12.7 us (4%)
  starting transfers between devices  5.01 us (2%)
    psum x1, waiting for transfers between devices, on_device(): lax.psum((grad_one, grad_two, batch_loss), ('store', 'batch'))  85.5 us
    psum x1, blocking collectives, on_device(): lax.psum((grad_one, grad_two, batch_loss), ('store', 'batch'))  63.7 us
    all_to_all x1, waiting for transfers between devices, on_device(): lax.all_to_all(found, ('store', 'batch'), split_axis=0, concat_axis=0, ti...  23.9 us
    all_to_all x1, blocking collectives, on_device(): lax.all_to_all(requests, ('store', 'batch'), split_axis=0, concat_axis=0,...  21.2 us
    gather x1, local copies, waits for them, and re-layouts, on_device(): features[lax.all_to_all(requests, ('store', 'batch'), split_axis=0, conca...  13.7 us
    scatter-add x1, other arithmetic, densify(): jnp.zeros((blocks, blocks, tile, tile), jnp.bfloat16).at[tile_row, tile_col]  9.71 us
    dot_general x1, matrix products, backward_spread(): lax.dot_general(dense, values, (((0,), (0,)), ((), ())), preferred_elemen...  9.62 us
    gather x1, local copies, waits for them, and re-layouts, on_device(): inputs = arrived.reshape(devices * capacity, features.shape[1])[position]  6.95 us
  transfers between devices with their start and end apart: 2, of which 2 were waited for; matrix products, arithmetic and copies ran while one was open for 6% of the time, Pallas kernels for 0%

commit v1 on v0

--- a/solution.py
+++ b/solution.py
@@ -3,7 +3,150 @@
 import jax
 import jax.numpy as jnp
 from jax import lax
+from jax.experimental import pallas as pl
+from jax.experimental.pallas import tpu as pltpu
 from jax.sharding import PartitionSpec as P
+
+AXES = ("store", "batch")
+SIDE = 4
+WIDTH = 128
+LOSS_ROW = 921
+ROWS = 928
+
+
+def flat(x, y, z, core):
+    return ((x * SIDE + z) * 2 + core) * SIDE + y
+
+
+def shift_pairs(axes, offset):
+    pairs = []
+    for x in range(SIDE):
+        for y in range(SIDE):
+            for z in range(SIDE):
+                for core in range(2):
+                    place = [x, y, z]
+                    place[axes[core]] = (place[axes[core]] + offset) % SIDE
+                    pairs.append((flat(x, y, z, core), flat(*place, core)))
+    return pairs
+
+
+def swap_pairs():
+    return [
+        (flat(x, y, z, core), flat(x, y, z, 1 - core))
+        for x in range(SIDE)
+        for y in range(SIDE)
+        for z in range(SIDE)
+        for core in range(2)
+    ]
+
+
+FIRST, SECOND, THIRD = (0, 1), (1, 2), (2, 0)
+
+
+def split_loss(total):
+    tail = total[ROWS - 8 :, :]
+    row = lax.broadcasted_iota(jnp.int32, tail.shape, 0)
+    lane = lax.broadcasted_iota(jnp.int32, tail.shape, 1)
+    here = row == LOSS_ROW - (ROWS - 8)
+    loss = jnp.sum(jnp.where(here & (lane < 3), tail, 0.0), axis=1, keepdims=True)
+    high = loss.astype(jnp.bfloat16).astype(jnp.float32)
+    middle = (loss - high).astype(jnp.bfloat16).astype(jnp.float32)
+    low = (loss - high - middle).astype(jnp.bfloat16).astype(jnp.float32)
+    parts = jnp.where(lane == 0, high, jnp.where(lane == 1, middle, jnp.where(lane == 2, low, 0.0)))
+    return jnp.where(here, parts, tail)
+
+
+def store_total(out, columns, total):
+    out[: ROWS - 16, columns] = total[: ROWS - 16].astype(jnp.bfloat16)
+    last = jnp.concatenate([total[ROWS - 16 : ROWS - 8], split_loss(total)], axis=0)
+    out[ROWS - 16 :, columns] = last.astype(jnp.bfloat16)
+
+
+def first_add(place, own, arrived, keep, one, two, three):
+    for offset, out in ((1, one), (2, two), (3, three), (0, keep)):
+        block = lax.rem(place[0] + offset, SIDE)
+        columns = pl.ds(pl.multiple_of(block * WIDTH, WIDTH), WIDTH)
+        total = own[:, columns].astype(jnp.float32) + arrived[:, columns].astype(jnp.float32)
+        store_total(out, slice(None), total)
+
+
+def four_add(own, one, two, three, out):
+    total = (own[...].astype(jnp.float32) + two[...].astype(jnp.float32)) + (
+        one[...].astype(jnp.float32) + three[...].astype(jnp.float32)
+    )
+    store_total(out, slice(None), total)
+
+
+def place_blocks(place, own, one, two, three, out):
+    for offset, block in ((0, own), (1, one), (2, two), (3, three)):
+        at = lax.rem(place[0] + SIDE - offset, SIDE)
+        out[:, pl.ds(pl.multiple_of(at * WIDTH, WIDTH), WIDTH)] = block[...]
+
+
+def finish(core, own, other, grad_one, grad_two, loss):
+    half = SIDE * WIDTH
+    features = grad_one.shape[0]
+    classes = grad_two.shape[0]
+    for offset, part in ((0, own), (1, other)):
+        at = lax.rem(core[0] + offset, 2)
+        columns = pl.ds(pl.multiple_of(at * half, half), half)
+        grad_one[:, columns] = part[:features, :].astype(jnp.float32)
+        grad_two[:, columns] = part[features:, :].astype(jnp.float32)[:classes]
+
+        @pl.when(at == 0)
+        def _():
+            tail = part[ROWS - 16 :, :WIDTH].astype(jnp.float32)
+            row = lax.broadcasted_iota(jnp.int32, tail.shape, 0)
+            lane = lax.broadcasted_iota(jnp.int32, tail.shape, 1)
+            mine = (row == LOSS_ROW - (ROWS - 16)) & (lane < 3)
+            loss[...] = jnp.sum(
+                jnp.sum(jnp.where(mine, tail, 0.0), axis=1, keepdims=True), axis=0, keepdims=True
+            )
+
+
+def call(kernel, outs, scalars=0, arrays=0, limit=40 << 20, cost=None):
+    vmem = pl.BlockSpec(memory_space=pltpu.VMEM)
+    smem = pl.BlockSpec(memory_space=pltpu.SMEM)
+    return pl.pallas_call(
+        kernel,
+        out_shape=outs,
+        in_specs=[smem] * scalars + [vmem] * arrays,
+        out_specs=jax.tree.map(lambda _: vmem, outs),
+        compiler_params=pltpu.CompilerParams(vmem_limit_bytes=limit),
+        cost_estimate=cost,
+    )
+
+
+def sum_over_devices(sent, own, features, classes):
+    store, batch = lax.axis_index("store"), lax.axis_index("batch")
+    core = lax.rem(store, 2)
+    place = jnp.where(core == 0, store // (2 * SIDE), batch).astype(jnp.int32).reshape(1)
+    core = core.astype(jnp.int32).reshape(1)
+    bf = jnp.bfloat16
+    block = jax.ShapeDtypeStruct((ROWS, WIDTH), bf)
+    arrived = lax.ppermute(sent, AXES, swap_pairs())
+    keep, *parts = call(first_add, [block] * 4, 1, 2)(place, own, arrived)
+    got = [lax.ppermute(part, AXES, shift_pairs(FIRST, k + 1)) for k, part in enumerate(parts)]
+    total = call(four_add, block, 0, 4)(keep, *got)
+    for axes in (SECOND, THIRD):
+        got = [lax.ppermute(total, AXES, shift_pairs(axes, k)) for k in (1, 2, 3)]
+        total = call(four_add, block, 0, 4)(total, *got)
+    got = [lax.ppermute(total, AXES, shift_pairs(FIRST, k)) for k in (1, 2, 3)]
+    strip = call(place_blocks, jax.ShapeDtypeStruct((ROWS, SIDE * WIDTH), bf), 1, 4)(
+        place, total, *got
+    )
+    other = lax.ppermute(strip, AXES, swap_pairs())
+    hidden = 2 * SIDE * WIDTH
+    return call(
+        finish,
+        [
+            jax.ShapeDtypeStruct((features, hidden), jnp.float32),
+            jax.ShapeDtypeStruct((classes, hidden), jnp.float32),
+            jax.ShapeDtypeStruct((1, 1), jnp.float32),
+        ],
+        1,
+        2,
+    )(core, strip, other)
 
 
 def densify(adj_tiles, tile_row, tile_col, live_count, nodes):
@@ -70,7 +213,9 @@
     )
     batch_loss = jnp.mean(logsum[:, 0] - jnp.sum(truth * logits, axis=1))
     upstream = ((jnp.exp(logits - logsum) - truth) / logits.shape[0]).astype(jnp.bfloat16)
-    grad_two = jnp.dot(smooth.T, upstream, preferred_element_type=jnp.float32)
+    grad_two = lax.dot_general(
+        upstream, smooth, (((0,), (0,)), ((), ())), preferred_element_type=jnp.float32
+    )
     back_smooth = jnp.dot(upstream, layer_two.T, preferred_element_type=jnp.float32).astype(
         jnp.bfloat16
     )
@@ -79,8 +224,20 @@
         jnp.bfloat16
     )
     grad_one = jnp.dot(mixed.T, back_before, preferred_element_type=jnp.float32)
-    grad_one, grad_two, batch_loss = lax.psum((grad_one, grad_two, batch_loss), ("store", "batch"))
-    return (grad_one, grad_two, batch_loss)
+    width, classes = grad_one.shape[0], grad_two.shape[0]
+    high = batch_loss.astype(jnp.bfloat16).astype(jnp.float32)
+    middle = (batch_loss - high).astype(jnp.bfloat16).astype(jnp.float32)
+    low = batch_loss - high - middle
+    loss_row = jnp.pad(jnp.stack([high, middle, low]).reshape(1, 3), ((0, 0), (0, grad_one.shape[1] - 3)))
+    stacked = jnp.concatenate(
+        [grad_one, grad_two, loss_row, jnp.zeros((ROWS - LOSS_ROW - 1, grad_one.shape[1]), jnp.float32)]
+    ).astype(jnp.bfloat16)
+    core = lax.rem(lax.axis_index("store"), 2)
+    half = SIDE * WIDTH
+    own = lax.dynamic_slice_in_dim(stacked, core * half, half, 1)
+    sent = lax.dynamic_slice_in_dim(stacked, (1 - core) * half, half, 1)
+    grad_one, grad_two, loss = sum_over_devices(sent, own, width, classes)
+    return (grad_one, grad_two.T, loss.reshape(()))
 
 
 def solution(mesh):

time: 292 us -> 179 us (0.61)
  blocking collectives: 84.8 us -> 21.2 us
  waiting for transfers between devices: 109 us -> 55.7 us
  starting transfers between devices: 5.01 us -> 21.6 us
  between operations: 15.6 us -> 2.26 us
  Pallas kernels: 0 us -> 3.87 us
  local copies, waits for them, and re-layouts: 38.5 us -> 34.8 us
  other arithmetic: 12.7 us -> 15.8 us
    psum x1 -> x0, waiting for transfers between devices: 85.5 us -> none  [on_device(): lax.psum((grad_one, grad_two, batch_loss), ('store', 'batch'))]
    psum x1 -> x0, blocking collectives: 63.7 us -> none  [on_device(): lax.psum((grad_one, grad_two, batch_loss), ('store', 'batch'))]
    ppermute x0 -> x14, waiting for transfers between devices: none -> 31.7 us  [the longest x6 13.8 us: sum_over_devices(): got = [lax.ppermute(total, AXES, shift_pairs(axes, k)) for k in (1, 2, 3)]]
    ppermute x0 -> x14, starting transfers between devices: none -> 16.6 us  [the longest x6 5.46 us: sum_over_devices(): got = [lax.ppermute(total, AXES, shift_pairs(axes, k)) for k in (1, 2, 3)]]
    unnamed x22 -> x18, local copies, waits for them, and re-layouts: 6.14 us -> 1.18 us
    pallas_call x0 -> x6, Pallas kernels: none -> 3.87 us  [the longest x1 2.22 us: sum_over_devices(): call(finish, [jax.ShapeDtypeStruct((features, hidden), jnp.float32), jax....]
    concatenate x0 -> x1, other arithmetic: none -> 3.15 us  [on_device(): jnp.concatenate([grad_one, grad_two, loss_row, jnp.zeros((ROWS - LOSS_ROW...]
  transfers between devices with their start and end apart: 2 -> 15, of which waited for: 2 -> 12; matrix products, arithmetic and copies ran while one was open for 6% -> 10% of each run, Pallas kernels for 0% -> 0%
where the time goes in v1:
time: 179 us; the launch traced here: 178 us
  waiting for transfers between devices  55.7 us (31%)
  local copies, waits for them, and re-layouts  34.8 us (19%)
  matrix products  22.8 us (13%)
  starting transfers between devices  21.6 us (12%)
  blocking collectives  21.2 us (12%)
  other arithmetic  15.8 us (9%)
  Pallas kernels  3.87 us (2%)
  between operations  2.26 us (1%)
    all_to_all x1, waiting for transfers between devices, on_device(): lax.all_to_all(found, ('store', 'batch'), split_axis=0, concat_axis=0, ti...  24 us
    all_to_all x1, blocking collectives, on_device(): lax.all_to_all(requests, ('store', 'batch'), split_axis=0, concat_axis=0,...  21.2 us
    ppermute x6, waiting for transfers between devices, sum_over_devices(): got = [lax.ppermute(total, AXES, shift_pairs(axes, k)) for k in (1, 2, 3)]  13.8 us
    gather x1, local copies, waits for them, and re-layouts, on_device(): features[lax.all_to_all(requests, ('store', 'batch'), split_axis=0, conca...  13.7 us
    dot_general x1, matrix products, backward_spread(): lax.dot_general(dense, values, (((0,), (0,)), ((), ())), preferred_elemen...  9.59 us
    scatter-add x1, other arithmetic, densify(): jnp.zeros((blocks, blocks, tile, tile), jnp.bfloat16).at[tile_row, tile_col]  9.57 us
    gather x1, local copies, waits for them, and re-layouts, on_device(): inputs = arrived.reshape(devices * capacity, features.shape[1])[position]  6.95 us
    ppermute x3, waiting for transfers between devices, sum_over_devices(): lax.ppermute(part, AXES, shift_pairs(FIRST, k + 1))  6.79 us
  transfers between devices with their start and end apart: 15, of which 12 were waited for; matrix products, arithmetic and copies ran while one was open for 10% of the time, Pallas kernels for 0%

profile of v1, /device:TPU:1, one launch (start us, length us, event | category | flops | bytes accessed | tf_op | source)
XLA Modules:
  0.0 178.1 jit_solution(15905881664707552447)
XLA Ops:
  0.6 0.0 copy-start
  0.7 0.9 copy.17
  1.6 0.2 fusion.36
  1.9 0.1 copy.18
  2.0 0.4 fusion.35
  2.4 4.5 %scatter_custom_fusion.1 = s32[2048]{0:T(1024)S(1)} fusion(s32[1024]{0:T(1024)S(1)} %get-tuple-element.22, s32[1024]{0:T(1024)} %param.12, s32[]{:T(128)} %constant.26.clone.1), kind=kCustom, calls=%fused_computation.58 | custom fusion | bytes 8704 | tf_op jit(solution)/shard_map/scatter | solution.py:195
  6.8 0.1 all_to_all.11
  6.9 21.2 %all_to_all.17 = s32[128,1,16]{2,1,0:T(1,128)S(1)} all-to-all(s32[128,1,16]{2,1,0:T(1,128)S(1)} %bitcast.70), channel_id=1, replica_groups=mesh['store'=32,'batch'=4] {'store','batch'}, dimensions={0} | all-to-all | bytes 16384 | tf_op jit(solution)/shard_map/all_to_all | solution.py:199
  28.1 0.1 reshape.98
  28.2 13.7 %gather_fusion = bf16[2048,768]{1,0:T(8,128)(2,1)} fusion(bf16[4096,768]{1,0:T(8,128)(2,1)} %param.10, s32[2048]{0:T(1024)S(1)} %broadcast_clamp_fusion), kind=kCustom, calls=%fused_computation | custom fusion | bytes 6299648 | tf_op jit(solution)/shard_map/gather | solution.py:198
  41.9 5.0 %all-to-all-start.1 = ((bf16[128,16,768]{2,1,0:T(8,128)(2,1)}), bf16[128,16,768]{2,1,0:T(8,128)(2,1)}, u32[]{:S(2)}, u32[]{:S(2)}) async-start(bf16[128,16,768]{2,1,0:T(8,128)(2,1)} %bitcast.66), calls=%async_computation.1 | async-start | bytes 6291456 | tf_op jit(solution)/shard_map/all_to_all | solution.py:201
  47.6 1.6 broadcast_select_fusion
  49.2 1.9 %broadcast_in_dim.38 = bf16[8,8,128,128]{3,2,1,0:T(8,128)(2,1)} broadcast(bf16[]{:T(256)} %constant.32.clone.1), dimensions={} | broadcast | bytes 2097154 | tf_op jit(solution)/shard_map/broadcast_in_dim | solution.py:157
  51.0 9.6 %scatter_fusion = bf16[8,8,128,128]{3,2,1,0:T(8,128)(2,1)} fusion(bf16[8,8,128,128]{3,2,1,0:T(8,128)(2,1)} %broadcast_in_dim.38, s32[48]{0:T(128)S(1)} %fusion.44, bf16[48,128,128]{2,1,0:T(8,128)(2,1)S(1)} %broadcast_select_fusion), kind=kCustom, calls=%fused_computation.2 | custom fusion | flops 786432 | bytes 4718976 | tf_op jit(solution)/shard_map/scatter-add | solution.py:157
  60.6 4.3 %copy.16 = bf16[8,128,8,128]{3,2,1,0:T(8,128)(2,1)} copy(bf16[8,128,8,128]{3,1,2,0:T(8,128)(2,1)} %bitcast.65) | data formatting | bytes 4194304 | tf_op jit(solution)/shard_map/transpose | solution.py:158
  64.9 0.1 pad.9.clone
  65.0 24.0 %all-to-all-done.1 = bf16[128,16,768]{2,1,0:T(8,128)(2,1)} async-done(((bf16[128,16,768]{2,1,0:T(8,128)(2,1)}), bf16[128,16,768]{2,1,0:T(8,128)(2,1)}, u32[]{:S(2)}, u32[]{:S(2)}) %all-to-all-start.1) | async-done | bytes 3145760 | tf_op jit(solution)/shard_map/all_to_all | solution.py:201
  89.0 6.9 %gather_fusion.1 = bf16[1024,768]{1,0:T(8,128)(2,1)S(1)} fusion(bf16[2048,768]{1,0:T(8,128)(2,1)} %bitcast.14, s32[1024]{0:T(1024)S(1)} %get-tuple-element.21), kind=kCustom, calls=%fused_computation.1 | custom fusion | bytes 3149824 | tf_op jit(solution)/shard_map/gather | solution.py:202
  95.9 3.4 %fusion.29 = bf16[1024,768]{1,0:T(8,128)(2,1)S(1)} fusion(bf16[1024,768]{1,0:T(8,128)(2,1)S(1)} %gather_fusion.1, bf16[128,8,8,128]{3,2,1,0:T(8,128)(2,1)} %bitcast.67), kind=kOutput, calls=%fused_computation.33 | convolution fusion | flops 1611399168 | bytes 5242880 | tf_op jit(solution)/shard_map/dot_general | solution.py:162
  99.3 1.1 copy-done.8
  100.4 1.8 %fusion.50 = f32[1024,1024]{1,0:T(8,128)S(1)} fusion(bf16[1024,768]{1,0:T(8,128)(2,1)S(1)} %fusion.29, bf16[768,1024]{1,0:T(8,128)(2,1)S(1)} %copy-done), kind=kOutput, calls=%fused_computation.79 | convolution fusion | flops 1610612736 | bytes 7340032 | tf_op jit(solution)/shard_map/dot_general | solution.py:205
  102.3 0.0 copy-start.2
  102.3 2.5 %fusion.26 = bf16[1024,1024]{1,0:T(8,128)(2,1)S(1)} fusion(f32[1024,1024]{1,0:T(8,128)S(1)} %fusion.50, bf16[128,8,8,128]{3,2,1,0:T(8,128)(2,1)S(1)} %bitcast.69), kind=kOutput, calls=%fused_computation.32 | convolution fusion | flops 2157969408 | bytes 8388608 | tf_op jit(solution)/shard_map/dot_general | solution.py:162
  104.8 0.0 copy-start.4
  104.8 0.9 fusion.49
  105.7 0.2 select_reduce_fusion
  105.9 0.6 subtract_reduce_fusion
  106.5 0.6 convolution_convert_fusion.1
  107.0 9.6 %fusion.6 = bf16[1024,1024]{1,0:T(8,128)(2,1)} fusion(f32[1024,1024]{1,0:T(8,128)} %copy-done.7, bf16[1024,153]{0,1:T(8,128)(2,1)S(1)} %copy-done.2, bf16[128,8,8,128]{3,2,1,0:T(8,128)(2,1)} %bitcast.68, f32[1024,153]{0,1:T(8,128)S(1)} %get-tuple-element.26, s32[1024]{0:T(1024)S(1)} %copy-done.4, f32[1024]{0:T(1024)S(1)} %get-tuple-element.20), kind=kOutput, calls=%fused_computation.14 | convolution fusion | flops 2491308032 | bytes 9336832 | tf_op jit(solution)/shard_map/dot_general | solution.py:166
  117.3 4.1 %convolution_convert_fusion = bf16[768,1024]{1,0:T(8,128)(2,1)S(1)} fusion(bf16[1024,768]{1,0:T(8,128)(2,1)} %copy-done.8, bf16[1024,1024]{1,0:T(8,128)(2,1)} %fusion.6), kind=kOutput, calls=%fused_computation.34 | convolution fusion | flops 1611399168 | bytes 5242880 | tf_op jit(solution)/shard_map/dot_general | solution.py:226
  121.4 0.1 maximum_bitcast_fusion
  121.5 3.1 %fusion.25 = bf16[928,1024]{1,0:T(8,128)(2,1)S(1)} fusion(bf16[1,3]{1,0:T(2,128)(2,1)S(1)} %maximum_bitcast_fusion, bf16[153,1024]{1,0:T(8,128)(2,1)S(1)} %convolution_convert_fusion.1, bf16[768,1024]{1,0:T(8,128)(2,1)S(1)} %convolution_convert_fusion, bf16[928]{0:T(1024)(128)(2,1)S(1)} %pad.9.clone), kind=kLoop, calls=%fused_computation.31 | loop fusion | flops 11403264 | bytes 3788614 | tf_op jit(solution)/shard_map/concatenate | solution.py:232
  124.7 1.2 constant_dynamic-slice_fusion
  125.8 0.2 collective-permute-start
  126.1 2.5 %collective-permute-done.arrived = bf16[928,512]{1,0:T(8,128)(2,1)S(1)} collective-permute-done((bf16[928,512]{1,0:T(8,128)(2,1)}, bf16[928,512]{1,0:T(8,128)(2,1)S(1)}, u32[]{:S(2)}, u32[]{:S(2)}) %collective-permute-start) | collective-permute-done | bytes 950304 | tf_op jit(solution)/shard_map/ppermute | solution.py:127
  128.6 0.5 shard_map.121
  129.1 0.4 collective-permute-start.1
  129.5 2.0 %collective-permute-start.2 = (bf16[928,128]{1,0:T(8,128)(2,1)S(1)}, bf16[928,128]{1,0:T(8,128)(2,1)S(1)}, u32[]{:S(2)}, u32[]{:S(2)}) collective-permute-start(bf16[928,128]{1,0:T(8,128)(2,1)S(1)} %get-tuple-element.12), channel_id=1, source_target_pairs={{0,64},{4,6},{8,72},{12,14},{16,80},{20,22},{24,88},{28,30},{1,65}... | collective-permute-start | bytes 712712 | tf_op jit(solution)/shard_map/ppermute | solution.py:129
  131.5 0.5 collective-permute-start.3
  132.0 6.2 %collective-permute-done.1.one = bf16[928,128]{1,0:T(8,128)(2,1)S(1)} collective-permute-done((bf16[928,128]{1,0:T(8,128)(2,1)S(1)}, bf16[928,128]{1,0:T(8,128)(2,1)S(1)}, u32[]{:S(2)}, u32[]{:S(2)}) %collective-permute-start.1) | collective-permute-done | bytes 237600 | tf_op jit(solution)/shard_map/ppermute | solution.py:129
  138.2 0.6 collective-permute-done.3.three
  138.8 0.3 shard_map.122.own
  139.1 0.0 collective-permute-start.4
  139.1 1.3 collective-permute-start.5
  140.4 1.4 collective-permute-start.6
  141.8 6.3 %collective-permute-done.4.one = bf16[928,128]{1,0:T(8,128)(2,1)S(1)} collective-permute-done((bf16[928,128]{1,0:T(8,128)(2,1)S(1)}, bf16[928,128]{1,0:T(8,128)(2,1)S(1)}, u32[]{:S(2)}, u32[]{:S(2)}) %collective-permute-start.4) | collective-permute-done | bytes 237600 | tf_op jit(solution)/shard_map/ppermute | solution.py:132
  148.1 0.6 collective-permute-done.6.three
  148.7 0.3 shard_map.123.own
  149.0 0.3 collective-permute-start.7
  149.3 1.8 %collective-permute-start.8 = (bf16[928,128]{1,0:T(8,128)(2,1)S(1)}, bf16[928,128]{1,0:T(8,128)(2,1)S(1)}, u32[]{:S(2)}, u32[]{:S(2)}) collective-permute-start(bf16[928,128]{1,0:T(8,128)(2,1)S(1)} %shard_map.123.own), channel_id=1, source_target_pairs={{0,16},{4,68},{8,24},{12,76},{16,0},{20,84},{24,8},{28,92},{1,17},... | collective-permute-start | bytes 712712 | tf_op jit(solution)/shard_map/ppermute | solution.py:132
  151.1 0.7 collective-permute-start.9
  151.8 6.2 %collective-permute-done.7.one = bf16[928,128]{1,0:T(8,128)(2,1)S(1)} collective-permute-done((bf16[928,128]{1,0:T(8,128)(2,1)S(1)}, bf16[928,128]{1,0:T(8,128)(2,1)S(1)}, u32[]{:S(2)}, u32[]{:S(2)}) %collective-permute-start.7) | collective-permute-done | bytes 237600 | tf_op jit(solution)/shard_map/ppermute | solution.py:132
  158.0 0.6 collective-permute-done.9.three
  158.7 0.3 shard_map.124.own
  159.0 0.1 collective-permute-start.10
  159.1 3.0 %collective-permute-start.11 = (bf16[928,128]{1,0:T(8,128)(2,1)S(1)}, bf16[928,128]{1,0:T(8,128)(2,1)S(1)}, u32[]{:S(2)}, u32[]{:S(2)}) collective-permute-start(bf16[928,128]{1,0:T(8,128)(2,1)S(1)} %shard_map.124.own), channel_id=1, source_target_pairs={{0,64},{4,6},{8,72},{12,14},{16,80},{20,22},{24,88},{28,30},{1,65}... | collective-permute-start | bytes 712712 | tf_op jit(solution)/shard_map/ppermute | solution.py:134
  162.1 0.0 collective-permute-start.12
  162.1 3.1 %collective-permute-done.10.one = bf16[928,128]{1,0:T(8,128)(2,1)S(1)} collective-permute-done((bf16[928,128]{1,0:T(8,128)(2,1)S(1)}, bf16[928,128]{1,0:T(8,128)(2,1)S(1)}, u32[]{:S(2)}, u32[]{:S(2)}) %collective-permute-start.10) | collective-permute-done | bytes 237600 | tf_op jit(solution)/shard_map/ppermute | solution.py:134
  165.1 3.0 %collective-permute-done.11.two = bf16[928,128]{1,0:T(8,128)(2,1)S(1)} collective-permute-done((bf16[928,128]{1,0:T(8,128)(2,1)S(1)}, bf16[928,128]{1,0:T(8,128)(2,1)S(1)}, u32[]{:S(2)}, u32[]{:S(2)}) %collective-permute-start.11) | collective-permute-done | bytes 237600 | tf_op jit(solution)/shard_map/ppermute | solution.py:134
  168.1 0.5 collective-permute-done.12.three
  168.6 0.3 shard_map.125.own
  168.9 4.9 %collective-permute-start.13 = (bf16[928,512]{1,0:T(8,128)(2,1)S(1)}, bf16[928,512]{1,0:T(8,128)(2,1)S(1)}, u32[]{:S(2)}, u32[]{:S(2)}) collective-permute-start(bf16[928,512]{1,0:T(8,128)(2,1)S(1)} %shard_map.125.own), channel_id=1, source_target_pairs={{0,4},{4,0},{8,12},{12,8},{16,20},{20,16},{24,28},{28,24},{1,5},{5... | collective-permute-start | bytes 2850824 | tf_op jit(solution)/shard_map/ppermute | solution.py:138
  173.7 2.1 %collective-permute-done.13.other = bf16[928,512]{1,0:T(8,128)(2,1)S(1)} collective-permute-done((bf16[928,512]{1,0:T(8,128)(2,1)S(1)}, bf16[928,512]{1,0:T(8,128)(2,1)S(1)}, u32[]{:S(2)}, u32[]{:S(2)}) %collective-permute-start.13) | collective-permute-done | bytes 950304 | tf_op jit(solution)/shard_map/ppermute | solution.py:138
  175.9 2.2 %shard_map.126 = (f32[768,1024]{1,0:T(8,128)}, f32[153,1024]{1,0:T(8,128)}, f32[1,1]{1,0:T(1,128)}) custom-call(s32[1]{0:T(128)} %bitcast.core, bf16[928,512]{1,0:T(8,128)(2,1)S(1)} %shard_map.125.own, bf16[928,512]{1,0:T(8,128)(2,1)S(1)} %collective-permute-done.13.other), custom_call_target="tpu_custom_call" | custom-call | tf_op jit(solution)/shard_map/pallas_call | solution.py:140
  (27 shorter events, 0.2 us)
Async XLA Ops:
  0.6 99.8 %copy-start = (bf16[768,1024]{1,0:T(8,128)(2,1)S(1)}, bf16[768,1024]{1,0:T(8,128)(2,1)}, u32[]{:S(2)}) copy-start(bf16[768,1024]{1,0:T(8,128)(2,1)} %param.18) | copy-start | bytes 4718596
  0.6 1.3 copy-start.3
  41.9 5.7 %copy-start.5 = (s32[48]{0:T(128)S(1)}, s32[48]{0:T(128)}, u32[]{:S(2)}) copy-start(s32[48]{0:T(128)} %param.15) | copy-start | bytes 580
  41.9 5.7 %copy-start.6 = (s32[48]{0:T(128)S(1)}, s32[48]{0:T(128)}, u32[]{:S(2)}) copy-start(s32[48]{0:T(128)} %param.14) | copy-start | bytes 580
  41.9 47.1 %all-to-all-start.1 = ((bf16[128,16,768]{2,1,0:T(8,128)(2,1)}), bf16[128,16,768]{2,1,0:T(8,128)(2,1)}, u32[]{:S(2)}, u32[]{:S(2)}) async-start(bf16[128,16,768]{2,1,0:T(8,128)(2,1)} %bitcast.66), calls=%async_computation.1 | async-start | bytes 6291456 | tf_op jit(solution)/shard_map/all_to_all | solution.py:201
  99.3 1.1 copy-start.8
  100.4 1.8 %copy-start.1 = (bf16[8,128,8,128]{3,2,1,0:T(8,128)(2,1)S(1)}, bf16[8,128,8,128]{3,2,1,0:T(8,128)(2,1)}, u32[]{:S(2)}) copy-start(bf16[8,128,8,128]{3,2,1,0:T(8,128)(2,1)} %copy.16) | copy-start | bytes 6291460
  102.3 2.5 %copy-start.7 = (f32[1024,1024]{1,0:T(8,128)}, f32[1024,1024]{1,0:T(8,128)S(1)}, u32[]{:S(2)}) copy-start(f32[1024,1024]{1,0:T(8,128)S(1)} %fusion.50) | copy-start | bytes 12582916
  102.3 2.5 %copy-start.2 = (bf16[1024,153]{0,1:T(8,128)(2,1)S(1)}, bf16[1024,153]{0,1:T(8,128)(2,1)}, u32[]{:S(2)}) copy-start(bf16[1024,153]{0,1:T(8,128)(2,1)} %param.19) | copy-start | bytes 940036
  104.8 0.9 copy-start.4
  125.8 2.7 %collective-permute-start = (bf16[928,512]{1,0:T(8,128)(2,1)}, bf16[928,512]{1,0:T(8,128)(2,1)S(1)}, u32[]{:S(2)}, u32[]{:S(2)}) collective-permute-start(bf16[928,512]{1,0:T(8,128)(2,1)} %get-tuple-element.23), channel_id=1, source_target_pairs={{0,4},{4,0},{8,12},{12,8},{16,20},{20,16},{24,28},{28,24},{1,5},{5... | collective-permute-start | bytes 2850824 | tf_op jit(solution)/shard_map/ppermute | solution.py:127
  129.1 9.1 %collective-permute-start.1 = (bf16[928,128]{1,0:T(8,128)(2,1)S(1)}, bf16[928,128]{1,0:T(8,128)(2,1)S(1)}, u32[]{:S(2)}, u32[]{:S(2)}) collective-permute-start(bf16[928,128]{1,0:T(8,128)(2,1)S(1)} %get-tuple-element.11), channel_id=1, source_target_pairs={{0,32},{4,5},{8,40},{12,13},{16,48},{20,21},{24,56},{28,29},{1,33}... | collective-permute-start | bytes 712712 | tf_op jit(solution)/shard_map/ppermute | solution.py:129
  129.5 8.6 %collective-permute-start.2 = (bf16[928,128]{1,0:T(8,128)(2,1)S(1)}, bf16[928,128]{1,0:T(8,128)(2,1)S(1)}, u32[]{:S(2)}, u32[]{:S(2)}) collective-permute-start(bf16[928,128]{1,0:T(8,128)(2,1)S(1)} %get-tuple-element.12), channel_id=1, source_target_pairs={{0,64},{4,6},{8,72},{12,14},{16,80},{20,22},{24,88},{28,30},{1,65}... | collective-permute-start | bytes 712712 | tf_op jit(solution)/shard_map/ppermute | solution.py:129
  131.5 7.3 %collective-permute-start.3 = (bf16[928,128]{1,0:T(8,128)(2,1)S(1)}, bf16[928,128]{1,0:T(8,128)(2,1)S(1)}, u32[]{:S(2)}, u32[]{:S(2)}) collective-permute-start(bf16[928,128]{1,0:T(8,128)(2,1)S(1)} %get-tuple-element.13), channel_id=1, source_target_pairs={{0,96},{4,7},{8,104},{12,15},{16,112},{20,23},{24,120},{28,31},{1,... | collective-permute-start | bytes 712712 | tf_op jit(solution)/shard_map/ppermute | solution.py:129
  139.1 9.0 %collective-permute-start.4 = (bf16[928,128]{1,0:T(8,128)(2,1)S(1)}, bf16[928,128]{1,0:T(8,128)(2,1)S(1)}, u32[]{:S(2)}, u32[]{:S(2)}) collective-permute-start(bf16[928,128]{1,0:T(8,128)(2,1)S(1)} %shard_map.122.own), channel_id=1, source_target_pairs={{0,1},{4,12},{8,9},{12,20},{16,17},{20,28},{24,25},{28,4},{1,2},{5... | collective-permute-start | bytes 712712 | tf_op jit(solution)/shard_map/ppermute | solution.py:132
  139.1 9.0 %collective-permute-start.5 = (bf16[928,128]{1,0:T(8,128)(2,1)S(1)}, bf16[928,128]{1,0:T(8,128)(2,1)S(1)}, u32[]{:S(2)}, u32[]{:S(2)}) collective-permute-start(bf16[928,128]{1,0:T(8,128)(2,1)S(1)} %shard_map.122.own), channel_id=1, source_target_pairs={{0,2},{4,20},{8,10},{12,28},{16,18},{20,4},{24,26},{28,12},{1,3},{... | collective-permute-start | bytes 712712 | tf_op jit(solution)/shard_map/ppermute | solution.py:132
  140.4 8.3 %collective-permute-start.6 = (bf16[928,128]{1,0:T(8,128)(2,1)S(1)}, bf16[928,128]{1,0:T(8,128)(2,1)S(1)}, u32[]{:S(2)}, u32[]{:S(2)}) collective-permute-start(bf16[928,128]{1,0:T(8,128)(2,1)S(1)} %shard_map.122.own), channel_id=1, source_target_pairs={{0,3},{4,28},{8,11},{12,4},{16,19},{20,12},{24,27},{28,20},{1,0},{... | collective-permute-start | bytes 712712 | tf_op jit(solution)/shard_map/ppermute | solution.py:132
  149.0 9.0 %collective-permute-start.7 = (bf16[928,128]{1,0:T(8,128)(2,1)S(1)}, bf16[928,128]{1,0:T(8,128)(2,1)S(1)}, u32[]{:S(2)}, u32[]{:S(2)}) collective-permute-start(bf16[928,128]{1,0:T(8,128)(2,1)S(1)} %shard_map.123.own), channel_id=1, source_target_pairs={{0,8},{4,36},{8,16},{12,44},{16,24},{20,52},{24,0},{28,60},{1,9},{... | collective-permute-start | bytes 712712 | tf_op jit(solution)/shard_map/ppermute | solution.py:132
  149.3 8.7 %collective-permute-start.8 = (bf16[928,128]{1,0:T(8,128)(2,1)S(1)}, bf16[928,128]{1,0:T(8,128)(2,1)S(1)}, u32[]{:S(2)}, u32[]{:S(2)}) collective-permute-start(bf16[928,128]{1,0:T(8,128)(2,1)S(1)} %shard_map.123.own), channel_id=1, source_target_pairs={{0,16},{4,68},{8,24},{12,76},{16,0},{20,84},{24,8},{28,92},{1,17},... | collective-permute-start | bytes 712712 | tf_op jit(solution)/shard_map/ppermute | solution.py:132
  151.1 7.5 %collective-permute-start.9 = (bf16[928,128]{1,0:T(8,128)(2,1)S(1)}, bf16[928,128]{1,0:T(8,128)(2,1)S(1)}, u32[]{:S(2)}, u32[]{:S(2)}) collective-permute-start(bf16[928,128]{1,0:T(8,128)(2,1)S(1)} %shard_map.123.own), channel_id=1, source_target_pairs={{0,24},{4,100},{8,0},{12,108},{16,8},{20,116},{24,16},{28,124},{1,... | collective-permute-start | bytes 712712 | tf_op jit(solution)/shard_map/ppermute | solution.py:132
  159.0 6.2 %collective-permute-start.10 = (bf16[928,128]{1,0:T(8,128)(2,1)S(1)}, bf16[928,128]{1,0:T(8,128)(2,1)S(1)}, u32[]{:S(2)}, u32[]{:S(2)}) collective-permute-start(bf16[928,128]{1,0:T(8,128)(2,1)S(1)} %shard_map.124.own), channel_id=1, source_target_pairs={{0,32},{4,5},{8,40},{12,13},{16,48},{20,21},{24,56},{28,29},{1,33}... | collective-permute-start | bytes 712712 | tf_op jit(solution)/shard_map/ppermute | solution.py:134
  159.1 9.0 %collective-permute-start.11 = (bf16[928,128]{1,0:T(8,128)(2,1)S(1)}, bf16[928,128]{1,0:T(8,128)(2,1)S(1)}, u32[]{:S(2)}, u32[]{:S(2)}) collective-permute-start(bf16[928,128]{1,0:T(8,128)(2,1)S(1)} %shard_map.124.own), channel_id=1, source_target_pairs={{0,64},{4,6},{8,72},{12,14},{16,80},{20,22},{24,88},{28,30},{1,65}... | collective-permute-start | bytes 712712 | tf_op jit(solution)/shard_map/ppermute | solution.py:134
  162.1 6.5 %collective-permute-start.12 = (bf16[928,128]{1,0:T(8,128)(2,1)S(1)}, bf16[928,128]{1,0:T(8,128)(2,1)S(1)}, u32[]{:S(2)}, u32[]{:S(2)}) collective-permute-start(bf16[928,128]{1,0:T(8,128)(2,1)S(1)} %shard_map.124.own), channel_id=1, source_target_pairs={{0,96},{4,7},{8,104},{12,15},{16,112},{20,23},{24,120},{28,31},{1,... | collective-permute-start | bytes 712712 | tf_op jit(solution)/shard_map/ppermute | solution.py:134
  168.9 7.0 %collective-permute-start.13 = (bf16[928,512]{1,0:T(8,128)(2,1)S(1)}, bf16[928,512]{1,0:T(8,128)(2,1)S(1)}, u32[]{:S(2)}, u32[]{:S(2)}) collective-permute-start(bf16[928,512]{1,0:T(8,128)(2,1)S(1)} %shard_map.125.own), channel_id=1, source_target_pairs={{0,4},{4,0},{8,12},{12,8},{16,20},{20,16},{24,28},{28,24},{1,5},{5... | collective-permute-start | bytes 2850824 | tf_op jit(solution)/shard_map/ppermute | solution.py:138

commit v2 on v1

--- a/solution.py
+++ b/solution.py
@@ -149,23 +149,152 @@
     )(core, strip, other)
 
 
-def densify(adj_tiles, tile_row, tile_col, live_count, nodes):
-    tile = adj_tiles.shape[1]
-    blocks = nodes // tile
-    live = jnp.arange(tile_row.shape[0], dtype=jnp.int32) < live_count
-    masked = jnp.where(live[:, None, None], adj_tiles, jnp.zeros_like(adj_tiles))
-    grid = jnp.zeros((blocks, blocks, tile, tile), jnp.bfloat16).at[tile_row, tile_col].add(masked)
-    return grid.transpose(0, 2, 1, 3).reshape(nodes, nodes)
-
-
-def forward_spread(dense, values):
-    return jnp.dot(dense, values, preferred_element_type=jnp.float32)
-
-
-def backward_spread(dense, values):
-    return lax.dot_general(
-        dense, values, (((0,), (0,)), ((), ())), preferred_element_type=jnp.float32
-    )
+def number_requests(parts, rows, requests, position):
+    devices, capacity = requests.shape
+    nodes = parts.shape[1]
+    piece = 128
+    owner = lax.broadcasted_iota(jnp.int32, (devices, nodes), 0)
+    mine = jnp.where(owner == parts[...], 1.0, 0.0)
+    line = lax.broadcasted_iota(jnp.int32, (piece, piece), 0)
+    lane = lax.broadcasted_iota(jnp.int32, (piece, piece), 1)
+    earlier = jnp.where(line < lane, 1.0, 0.0).astype(jnp.bfloat16)
+    seen = jnp.zeros((devices, 1), jnp.float32)
+    slots = []
+    for start in range(0, nodes, piece):
+        here = mine[:, start : start + piece]
+        rank = jnp.dot(here.astype(jnp.bfloat16), earlier, preferred_element_type=jnp.float32)
+        slots.append(jnp.sum(here * (rank + seen), axis=0, keepdims=True))
+        seen = seen + jnp.sum(here, axis=1, keepdims=True)
+    slot = jnp.concatenate(slots, axis=1).astype(jnp.int32)
+    position[...] = parts[...] * capacity + slot
+    placed = lax.broadcasted_iota(jnp.int32, (capacity, nodes), 0) == slot
+    total = jnp.zeros((devices, capacity), jnp.float32)
+    for scale, digit in ((64.0, lax.shift_right_logical(rows[...], 6)), (1.0, rows[...] & 63)):
+        values = jnp.where(placed, digit.astype(jnp.float32), 0.0).astype(jnp.bfloat16)
+        total += scale * lax.dot_general(
+            mine.astype(jnp.bfloat16),
+            values,
+            (((1,), (1,)), ((), ())),
+            preferred_element_type=jnp.float32,
+        )
+    requests[...] = total.astype(jnp.int32)
+
+
+def build_spread(row, column, count, tiles, position, dense, turned, moved):
+    nodes = dense.shape[0]
+    tile = tiles.shape[1]
+    dense[...] = jnp.zeros_like(dense)
+    turned[...] = jnp.zeros_like(turned)
+
+    @pl.loop(0, count[0])
+    def _(t):
+        at_row = pl.ds(pl.multiple_of(row[t] * tile, tile), tile)
+        at_column = pl.ds(pl.multiple_of(column[t] * tile, tile), tile)
+        values = tiles[t]
+        dense[at_row, at_column] = values
+        turned[at_column, at_row] = values.T
+
+    width = 256
+
+    @pl.loop(0, moved.shape[1] // width)
+    def _(step):
+        start = pl.multiple_of(step * width, width)
+        slot = lax.broadcasted_iota(jnp.int32, (width, nodes), 0) + start
+        chosen = jnp.where(slot == position[...], 1.0, 0.0).astype(jnp.bfloat16)
+        moved[:, pl.ds(start, width)] = lax.dot_general(
+            dense[...], chosen, (((1,), (1,)), ((), ())), preferred_element_type=jnp.float32
+        ).astype(jnp.bfloat16)
+
+
+def train(
+    core,
+    arrived,
+    moved,
+    dense,
+    turned,
+    layer_one,
+    layer_two,
+    labels,
+    sent,
+    own,
+    mixed_turned,
+    slope,
+    hidden,
+    smooth,
+    upstream,
+    upstream_turned,
+    *,
+    classes,
+):
+    nodes = dense.shape[0]
+    features = mixed_turned.shape[0]
+    step = 256
+    for start in range(0, nodes, step):
+        rows = slice(start, start + step)
+        mixed = jnp.dot(moved[rows, :], arrived[...], preferred_element_type=jnp.float32).astype(
+            jnp.bfloat16
+        )
+        mixed_turned[:, rows] = mixed.T
+        before = jnp.dot(mixed, layer_one[...], preferred_element_type=jnp.float32)
+        square = before * before
+        rate = 0.7978845608028654
+        bend = jnp.tanh(rate * before * (1.0 + 0.044715 * square))
+        rise = 0.5 * (1.0 + bend)
+        hidden[rows, :] = (before * rise).astype(jnp.bfloat16)
+        slope[rows, :] = rise + 0.5 * before * (1.0 - bend * bend) * (
+            rate + (3.0 * 0.044715 * rate) * square
+        )
+    loss = jnp.zeros((1, 1), jnp.float32)
+    for start in range(0, nodes, step):
+        rows = slice(start, start + step)
+        spread = jnp.dot(dense[rows, :], hidden[...], preferred_element_type=jnp.float32).astype(
+            jnp.bfloat16
+        )
+        smooth[rows, :] = spread
+        logits = lax.dot_general(
+            spread, layer_two[...], (((1,), (1,)), ((), ())), preferred_element_type=jnp.float32
+        )
+        lane = lax.broadcasted_iota(jnp.int32, logits.shape, 1)
+        logits = jnp.where(lane < classes, logits, -jnp.inf)
+        largest = jnp.max(logits, axis=1, keepdims=True)
+        logsum = jnp.log(jnp.sum(jnp.exp(logits - largest), axis=1, keepdims=True)) + largest
+        truth = lane == labels[rows, :]
+        picked = jnp.sum(jnp.where(truth, logits, 0.0), axis=1, keepdims=True)
+        loss += jnp.sum(logsum - picked, axis=0, keepdims=True)
+        gap = (jnp.exp(logits - logsum) - jnp.where(truth, 1.0, 0.0)) * (1.0 / nodes)
+        upstream[rows, :] = gap.astype(jnp.bfloat16)
+        upstream_turned[:, rows] = gap.astype(jnp.bfloat16).T
+    loss = loss * (1.0 / nodes)
+    high = loss.astype(jnp.bfloat16).astype(jnp.float32)
+    middle = (loss - high).astype(jnp.bfloat16).astype(jnp.float32)
+    low = loss - high - middle
+    half = SIDE * WIDTH
+    for offset, out in ((1, sent), (0, own)):
+        part = lax.rem(core[0] + offset, 2)
+        for start in range(0, half, step):
+            columns = pl.ds(pl.multiple_of(part * half + start, step), step)
+            place = slice(start, start + step)
+            second = jnp.dot(
+                upstream_turned[: ROWS - features, :],
+                smooth[:, columns],
+                preferred_element_type=jnp.float32,
+            )
+            if start == 0:
+                row = lax.broadcasted_iota(jnp.int32, second.shape, 0)
+                lane = lax.broadcasted_iota(jnp.int32, second.shape, 1)
+                here = (row == LOSS_ROW - features) & (part == 0)
+                second += jnp.where(here & (lane == 0), high, 0.0)
+                second += jnp.where(here & (lane == 1), middle, 0.0)
+                second += jnp.where(here & (lane == 2), low, 0.0)
+            out[features:, place] = second.astype(out.dtype)
+            back = jnp.dot(
+                upstream[...], layer_two[:, columns], preferred_element_type=jnp.float32
+            ).astype(jnp.bfloat16)
+            back = jnp.dot(turned[...], back, preferred_element_type=jnp.float32)
+            back = (slope[:, columns] * back).astype(jnp.bfloat16)
+            out[:features, place] = jnp.dot(
+                mixed_turned[...], back, preferred_element_type=jnp.float32
+            ).astype(out.dtype)
 
 
 def on_device(
@@ -180,62 +309,71 @@
     layer_one,
     layer_two,
 ):
-    devices = lax.axis_size(("store", "batch"))
+    devices = lax.axis_size(AXES)
     nodes = source_part.shape[0]
+    width, hidden = layer_one.shape
+    classes = layer_two.shape[1]
     capacity = max(2, 2 * nodes // devices)
-    owners = (source_part[:, None] == jnp.arange(devices, dtype=jnp.int32)[None, :]).astype(
-        jnp.int32
-    )
-    ranking = jnp.cumsum(owners, axis=0) - 1
-    source_slot = jnp.sum(owners * ranking, axis=1)
-    position = source_part * capacity + source_slot
-    requests = (
-        jnp.zeros((devices * capacity,), jnp.int32)
-        .at[position]
-        .set(source_row)
-        .reshape(devices, capacity)
-    )
-    found = features[
-        lax.all_to_all(requests, ("store", "batch"), split_axis=0, concat_axis=0, tiled=True)
-    ]
-    arrived = lax.all_to_all(found, ("store", "batch"), split_axis=0, concat_axis=0, tiled=True)
-    inputs = arrived.reshape(devices * capacity, features.shape[1])[position]
-    dense = densify(adj_tiles, tile_row, tile_col, tile_count[0], nodes)
-    mixed = forward_spread(dense, inputs).astype(jnp.bfloat16)
-    before = jnp.dot(mixed, layer_one, preferred_element_type=jnp.float32)
-    hidden = jax.nn.gelu(before, approximate=True).astype(jnp.bfloat16)
-    smooth = forward_spread(dense, hidden).astype(jnp.bfloat16)
-    logits = jnp.dot(smooth, layer_two, preferred_element_type=jnp.float32)
-    largest = jnp.max(logits, axis=1, keepdims=True)
-    logsum = jnp.log(jnp.sum(jnp.exp(logits - largest), axis=1, keepdims=True)) + largest
-    truth = (labels[:, None] == jnp.arange(logits.shape[1], dtype=jnp.int32)[None, :]).astype(
-        jnp.float32
-    )
-    batch_loss = jnp.mean(logsum[:, 0] - jnp.sum(truth * logits, axis=1))
-    upstream = ((jnp.exp(logits - logsum) - truth) / logits.shape[0]).astype(jnp.bfloat16)
-    grad_two = lax.dot_general(
-        upstream, smooth, (((0,), (0,)), ((), ())), preferred_element_type=jnp.float32
-    )
-    back_smooth = jnp.dot(upstream, layer_two.T, preferred_element_type=jnp.float32).astype(
-        jnp.bfloat16
-    )
-    back_hidden = backward_spread(dense, back_smooth)
-    back_before = jax.vjp(partial(jax.nn.gelu, approximate=True), before)[1](back_hidden)[0].astype(
-        jnp.bfloat16
-    )
-    grad_one = jnp.dot(mixed.T, back_before, preferred_element_type=jnp.float32)
-    width, classes = grad_one.shape[0], grad_two.shape[0]
-    high = batch_loss.astype(jnp.bfloat16).astype(jnp.float32)
-    middle = (batch_loss - high).astype(jnp.bfloat16).astype(jnp.float32)
-    low = batch_loss - high - middle
-    loss_row = jnp.pad(jnp.stack([high, middle, low]).reshape(1, 3), ((0, 0), (0, grad_one.shape[1] - 3)))
-    stacked = jnp.concatenate(
-        [grad_one, grad_two, loss_row, jnp.zeros((ROWS - LOSS_ROW - 1, grad_one.shape[1]), jnp.float32)]
-    ).astype(jnp.bfloat16)
-    core = lax.rem(lax.axis_index("store"), 2)
+    slots = devices * capacity
+    bf = jnp.bfloat16
+    requests, position = call(
+        number_requests,
+        [
+            jax.ShapeDtypeStruct((devices, capacity), jnp.int32),
+            jax.ShapeDtypeStruct((1, nodes), jnp.int32),
+        ],
+        0,
+        2,
+    )(source_part.reshape(1, nodes), source_row.reshape(1, nodes))
+    found = features[lax.all_to_all(requests, AXES, split_axis=0, concat_axis=0, tiled=True)]
+    arrived = lax.all_to_all(found, AXES, split_axis=0, concat_axis=0, tiled=True)
+    dense, turned, moved = call(
+        build_spread,
+        [
+            jax.ShapeDtypeStruct((nodes, nodes), bf),
+            jax.ShapeDtypeStruct((nodes, nodes), bf),
+            jax.ShapeDtypeStruct((nodes, slots), bf),
+        ],
+        3,
+        2,
+        cost=pl.CostEstimate(
+            flops=2 * nodes * nodes * slots, bytes_accessed=12 << 20, transcendentals=0
+        ),
+    )(tile_row, tile_col, tile_count, adj_tiles, position)
+    padded = jnp.pad(layer_two.T, ((0, 256 - classes), (0, 0)))
+    core = lax.rem(lax.axis_index("store"), 2).astype(jnp.int32).reshape(1)
     half = SIDE * WIDTH
-    own = lax.dynamic_slice_in_dim(stacked, core * half, half, 1)
-    sent = lax.dynamic_slice_in_dim(stacked, (1 - core) * half, half, 1)
+    vmem = pl.BlockSpec(memory_space=pltpu.VMEM)
+    sent, own = pl.pallas_call(
+        partial(train, classes=classes),
+        out_shape=[
+            jax.ShapeDtypeStruct((ROWS, half), bf),
+            jax.ShapeDtypeStruct((ROWS, half), jnp.float32),
+        ],
+        in_specs=[pl.BlockSpec(memory_space=pltpu.SMEM)] + [vmem] * 7,
+        out_specs=[vmem] * 2,
+        scratch_shapes=[
+            pltpu.VMEM((width, nodes), bf),
+            pltpu.VMEM((nodes, hidden), jnp.float32),
+            pltpu.VMEM((nodes, hidden), bf),
+            pltpu.VMEM((nodes, hidden), bf),
+            pltpu.VMEM((nodes, 256), bf),
+            pltpu.VMEM((256, nodes), bf),
+        ],
+        compiler_params=pltpu.CompilerParams(vmem_limit_bytes=56 << 20),
+        cost_estimate=pl.CostEstimate(
+            flops=12 * nodes * nodes * hidden, bytes_accessed=16 << 20, transcendentals=nodes * hidden
+        ),
+    )(
+        core,
+        arrived.reshape(slots, width),
+        moved,
+        dense,
+        turned,
+        layer_one,
+        padded,
+        labels.reshape(nodes, 1),
+    )
     grad_one, grad_two, loss = sum_over_devices(sent, own, width, classes)
     return (grad_one, grad_two.T, loss.reshape(()))
 

time: 179 us -> 166 us (0.927)
  Pallas kernels: 3.87 us -> 38.9 us
  matrix products: 22.8 us -> 0 us
  other arithmetic: 15.8 us -> 0.02 us
  local copies, waits for them, and re-layouts: 34.8 us -> 23.2 us
  waiting for transfers between devices: 55.7 us -> 60.7 us
  starting transfers between devices: 21.6 us -> 19.8 us
    pallas_call x0 -> x3, Pallas kernels: none -> 35.1 us  [the longest x1 24.6 us: on_device(): pl.pallas_call(partial(train, classes=classes), out_shape=[jax.ShapeDtype...]
    dot_general x7 -> x0, matrix products: 22.8 us -> none  [the longest x1 9.59 us: backward_spread(): lax.dot_general(dense, values, (((0,), (0,)), ((), ())), preferred_elemen...]
    scatter-add x1 -> x0, other arithmetic: 9.57 us -> none  [densify(): jnp.zeros((blocks, blocks, tile, tile), jnp.bfloat16).at[tile_row, tile_col]]
    gather x2 -> x1, local copies, waits for them, and re-layouts: 20.6 us -> 13.7 us  [on_device(): features[lax.all_to_all(requests, AXES, split_axis=0, concat_axis=0, tile...]
    unnamed x18 -> x22, local copies, waits for them, and re-layouts: 1.18 us -> 7.57 us
    scatter x1 -> x0, local copies, waits for them, and re-layouts: 4.48 us -> none  [on_device(): requests = jnp.zeros((devices * capacity,), jnp.int32).at[position].set(s...]
    transpose x1 -> x0, local copies, waits for them, and re-layouts: 4.27 us -> none  [densify(): return grid.transpose(0, 2, 1, 3).reshape(nodes, nodes)]
    concatenate x2 -> x0, other arithmetic: 3.16 us -> none  [the longest x1 3.15 us: on_device(): jnp.concatenate([grad_one, grad_two, loss_row, jnp.zeros((ROWS - LOSS_ROW...]
  transfers between devices with their start and end apart: 15 -> 15, of which waited for: 12 -> 14; matrix products, arithmetic and copies ran while one was open for 10% -> 1% of each run, Pallas kernels for 0% -> 6%
where the time goes in v2:
time: 166 us; the launch traced here: 165 us
  waiting for transfers between devices  60.7 us (37%)
  Pallas kernels  38.9 us (23%)
  local copies, waits for them, and re-layouts  23.2 us (14%)
  blocking collectives  21.2 us (13%)
  starting transfers between devices  19.8 us (12%)
    all_to_all x1, waiting for transfers between devices, on_device(): lax.all_to_all(found, AXES, split_axis=0, concat_axis=0, tiled=True)  24.8 us
    pallas_call x1, Pallas kernels, on_device(): pl.pallas_call(partial(train, classes=classes), out_shape=[jax.ShapeDtype...  24.6 us
    all_to_all x1, blocking collectives, on_device(): lax.all_to_all(requests, AXES, split_axis=0, concat_axis=0, tiled=True)  21.2 us
    ppermute x6, waiting for transfers between devices, sum_over_devices(): got = [lax.ppermute(total, AXES, shift_pairs(axes, k)) for k in (1, 2, 3)]  15.8 us
    gather x1, local copies, waits for them, and re-layouts, on_device(): features[lax.all_to_all(requests, AXES, split_axis=0, concat_axis=0, tile...  13.7 us
    pallas_call x1, Pallas kernels, on_device(): call(build_spread, [jax.ShapeDtypeStruct((nodes, nodes), bf), jax.ShapeDt...  9.98 us
    ppermute x3, waiting for transfers between devices, sum_over_devices(): got = [lax.ppermute(total, AXES, shift_pairs(FIRST, k)) for k in (1, 2, 3)]  8.61 us
    unnamed x22, local copies, waits for them, and re-layouts  7.57 us
  transfers between devices with their start and end apart: 15, of which 14 were waited for; matrix products, arithmetic and copies ran while one was open for 1% of the time, Pallas kernels for 6%

profile of v2, /device:TPU:1, one launch (start us, length us, event | category | flops | bytes accessed | tf_op | source)
XLA Modules:
  0.0 165.2 jit_solution(15452580220443049505)
XLA Ops:
  0.6 0.0 copy-start.1
  0.6 0.7 copy-done.1
  1.3 0.0 copy-start.2
  1.3 0.7 copy-done.2
  2.0 0.5 shard_map.121
  2.5 21.2 %all_to_all.17 = s32[128,1,16]{2,1,0:T(1,128)S(1)} all-to-all(s32[128,1,16]{2,1,0:T(1,128)S(1)} %bitcast.16), channel_id=1, replica_groups=mesh['store'=32,'batch'=4] {'store','batch'}, dimensions={0} | all-to-all | bytes 16384 | tf_op jit(solution)/shard_map/all_to_all | solution.py:328
  23.7 0.1 reshape.67
  23.8 13.7 %gather_fusion = bf16[2048,768]{1,0:T(8,128)(2,1)} fusion(bf16[4096,768]{1,0:T(8,128)(2,1)} %param.10, s32[2048]{0:T(1024)S(1)} %broadcast_clamp_fusion), kind=kCustom, calls=%fused_computation | custom fusion | bytes 6299648 | tf_op jit(solution)/shard_map/gather | solution.py:328
  37.5 0.0 copy-start.10
  37.5 0.0 copy-start.9
  37.5 0.0 copy-start.3
  37.5 0.0 copy-start.4
  37.5 0.0 copy-start.5
  37.5 5.0 %all-to-all-start.1 = ((bf16[128,16,768]{2,1,0:T(8,128)(2,1)}), bf16[128,16,768]{2,1,0:T(8,128)(2,1)}, u32[]{:S(2)}, u32[]{:S(2)}) async-start(bf16[128,16,768]{2,1,0:T(8,128)(2,1)} %bitcast.19), calls=%async_computation.1 | async-start | bytes 6291456 | tf_op jit(solution)/shard_map/all_to_all | solution.py:329
  43.2 0.0 copy-done.10
  43.2 1.1 copy.15.labels
  44.3 0.0 copy-done.9
  44.3 0.8 pad.4.layer_two
  45.1 0.0 copy-done.3
  45.1 0.0 copy-done.4
  45.1 0.0 copy-done.5
  45.1 10.0 %shard_map.122 = (bf16[1024,1024]{1,0:T(8,128)(2,1)S(1)}, bf16[1024,1024]{1,0:T(8,128)(2,1)S(1)}, bf16[1024,2048]{1,0:T(8,128)(2,1)S(1)}) custom-call(s32[48]{0:T(128)S(1)} %copy-done.4, s32[48]{0:T(128)S(1)} %copy-done.5, s32[1]{0:T(128)S(6)} %copy.16.count, bf16[48,128,128]{2,1,0:T(8,128)(2,1)S(1)} %copy-done.3, s32[1,1024]{1,0:T(1,128)S(1)} %get-tuple-element.18.position), custom_call_target="tpu_custom_call" | custom-call | flops 4294967296 | bytes 12582912 | tf_op jit(solution)/shard_map/pallas_call | solution.py:330
  55.1 0.0 copy-start.6
  55.1 2.0 %copy-done.6 = bf16[1024,2048]{1,0:T(8,128)(2,1)} copy-done((bf16[1024,2048]{1,0:T(8,128)(2,1)}, bf16[1024,2048]{1,0:T(8,128)(2,1)S(1)}, u32[]{:S(2)}) %copy-start.6) | copy-done | bytes 4194328
  57.1 0.0 copy-start.7
  57.1 1.4 copy-done.7
  58.5 1.3 copy-done.8
  59.8 24.8 %all-to-all-done.1 = bf16[128,16,768]{2,1,0:T(8,128)(2,1)} async-done(((bf16[128,16,768]{2,1,0:T(8,128)(2,1)}), bf16[128,16,768]{2,1,0:T(8,128)(2,1)}, u32[]{:S(2)}, u32[]{:S(2)}) %all-to-all-start.1) | async-done | bytes 3145760 | tf_op jit(solution)/shard_map/all_to_all | solution.py:329
  84.6 24.6 %shard_map.123 = (bf16[928,512]{1,0:T(8,128)(2,1)}, f32[928,512]{1,0:T(8,128)}) custom-call(s32[1]{0:T(128)} %bitcast.core, bf16[2048,768]{1,0:T(8,128)(2,1)} %bitcast.8.arrived, bf16[1024,2048]{1,0:T(8,128)(2,1)} %copy-done.6, bf16[1024,1024]{1,0:T(8,128)(2,1)} %copy-done.7, bf16[1024,1024]{1,0:T(8,128)(2,1)} %copy-done.8, bf16[768,1024]{1,0:T(8,128)(2,1)} %layer_one.1, ...), custom_call_target="tpu_custom_call" | custom-call | flops 12884901888 | bytes 16777216 | tf_op jit(solution)/shard_map/pallas_call | solution.py:347
  109.2 0.2 collective-permute-start
  109.4 2.5 %collective-permute-done.arrived = bf16[928,512]{1,0:T(8,128)(2,1)S(1)} collective-permute-done((bf16[928,512]{1,0:T(8,128)(2,1)}, bf16[928,512]{1,0:T(8,128)(2,1)S(1)}, u32[]{:S(2)}, u32[]{:S(2)}) %collective-permute-start) | collective-permute-done | bytes 950304 | tf_op jit(solution)/shard_map/ppermute | solution.py:127
  111.9 1.5 copy-done
  113.4 0.5 shard_map.124
  113.9 0.4 collective-permute-start.1
  114.3 2.0 %collective-permute-start.2 = (bf16[928,128]{1,0:T(8,128)(2,1)S(1)}, bf16[928,128]{1,0:T(8,128)(2,1)S(1)}, u32[]{:S(2)}, u32[]{:S(2)}) collective-permute-start(bf16[928,128]{1,0:T(8,128)(2,1)S(1)} %get-tuple-element.26), channel_id=1, source_target_pairs={{0,64},{4,6},{8,72},{12,14},{16,80},{20,22},{24,88},{28,30},{1,65}... | collective-permute-start | bytes 712712 | tf_op jit(solution)/shard_map/ppermute | solution.py:129
  116.3 0.5 collective-permute-start.3
  116.8 6.2 %collective-permute-done.1.one = bf16[928,128]{1,0:T(8,128)(2,1)S(1)} collective-permute-done((bf16[928,128]{1,0:T(8,128)(2,1)S(1)}, bf16[928,128]{1,0:T(8,128)(2,1)S(1)}, u32[]{:S(2)}, u32[]{:S(2)}) %collective-permute-start.1) | collective-permute-done | bytes 237600 | tf_op jit(solution)/shard_map/ppermute | solution.py:129
  123.0 0.0 collective-permute-done.2.two
  123.0 0.6 collective-permute-done.3.three
  123.6 0.3 shard_map.125.own
  123.9 0.1 collective-permute-start.6
  124.0 1.6 collective-permute-start.5
  125.6 0.0 collective-permute-start.4
  125.6 3.6 %collective-permute-done.6.three = bf16[928,128]{1,0:T(8,128)(2,1)S(1)} collective-permute-done((bf16[928,128]{1,0:T(8,128)(2,1)S(1)}, bf16[928,128]{1,0:T(8,128)(2,1)S(1)}, u32[]{:S(2)}, u32[]{:S(2)}) %collective-permute-start.6) | collective-permute-done | bytes 237600 | tf_op jit(solution)/shard_map/ppermute | solution.py:132
  129.1 1.4 collective-permute-done.5.two
  130.6 2.7 %collective-permute-done.4.one = bf16[928,128]{1,0:T(8,128)(2,1)S(1)} collective-permute-done((bf16[928,128]{1,0:T(8,128)(2,1)S(1)}, bf16[928,128]{1,0:T(8,128)(2,1)S(1)}, u32[]{:S(2)}, u32[]{:S(2)}) %collective-permute-start.4) | collective-permute-done | bytes 237600 | tf_op jit(solution)/shard_map/ppermute | solution.py:132
  133.3 0.3 shard_map.126.own
  133.6 0.9 collective-permute-start.9
  134.5 1.2 collective-permute-start.8
  135.7 0.0 collective-permute-start.7
  135.7 2.9 %collective-permute-done.9.three = bf16[928,128]{1,0:T(8,128)(2,1)S(1)} collective-permute-done((bf16[928,128]{1,0:T(8,128)(2,1)S(1)}, bf16[928,128]{1,0:T(8,128)(2,1)S(1)}, u32[]{:S(2)}, u32[]{:S(2)}) %collective-permute-start.9) | collective-permute-done | bytes 237600 | tf_op jit(solution)/shard_map/ppermute | solution.py:132
  138.6 2.5 %collective-permute-done.8.two = bf16[928,128]{1,0:T(8,128)(2,1)S(1)} collective-permute-done((bf16[928,128]{1,0:T(8,128)(2,1)S(1)}, bf16[928,128]{1,0:T(8,128)(2,1)S(1)}, u32[]{:S(2)}, u32[]{:S(2)}) %collective-permute-start.8) | collective-permute-done | bytes 237600 | tf_op jit(solution)/shard_map/ppermute | solution.py:132
  141.1 2.7 %collective-permute-done.7.one = bf16[928,128]{1,0:T(8,128)(2,1)S(1)} collective-permute-done((bf16[928,128]{1,0:T(8,128)(2,1)S(1)}, bf16[928,128]{1,0:T(8,128)(2,1)S(1)}, u32[]{:S(2)}, u32[]{:S(2)}) %collective-permute-start.7) | collective-permute-done | bytes 237600 | tf_op jit(solution)/shard_map/ppermute | solution.py:132
  143.8 0.3 shard_map.127.own
  144.1 2.4 %collective-permute-start.12 = (bf16[928,128]{1,0:T(8,128)(2,1)S(1)}, bf16[928,128]{1,0:T(8,128)(2,1)S(1)}, u32[]{:S(2)}, u32[]{:S(2)}) collective-permute-start(bf16[928,128]{1,0:T(8,128)(2,1)S(1)} %shard_map.127.own), channel_id=1, source_target_pairs={{0,96},{4,7},{8,104},{12,15},{16,112},{20,23},{24,120},{28,31},{1,... | collective-permute-start | bytes 712712 | tf_op jit(solution)/shard_map/ppermute | solution.py:134
  146.4 0.3 collective-permute-start.11
  146.7 0.4 collective-permute-start.10
  147.1 4.9 %collective-permute-done.12.three = bf16[928,128]{1,0:T(8,128)(2,1)S(1)} collective-permute-done((bf16[928,128]{1,0:T(8,128)(2,1)S(1)}, bf16[928,128]{1,0:T(8,128)(2,1)S(1)}, u32[]{:S(2)}, u32[]{:S(2)}) %collective-permute-start.12) | collective-permute-done | bytes 237600 | tf_op jit(solution)/shard_map/ppermute | solution.py:134
  152.0 1.0 collective-permute-done.11.two
  153.0 2.7 %collective-permute-done.10.one = bf16[928,128]{1,0:T(8,128)(2,1)S(1)} collective-permute-done((bf16[928,128]{1,0:T(8,128)(2,1)S(1)}, bf16[928,128]{1,0:T(8,128)(2,1)S(1)}, u32[]{:S(2)}, u32[]{:S(2)}) %collective-permute-start.10) | collective-permute-done | bytes 237600 | tf_op jit(solution)/shard_map/ppermute | solution.py:134
  155.7 0.3 shard_map.128.own
  156.0 4.9 %collective-permute-start.13 = (bf16[928,512]{1,0:T(8,128)(2,1)S(1)}, bf16[928,512]{1,0:T(8,128)(2,1)S(1)}, u32[]{:S(2)}, u32[]{:S(2)}) collective-permute-start(bf16[928,512]{1,0:T(8,128)(2,1)S(1)} %shard_map.128.own), channel_id=1, source_target_pairs={{0,4},{4,0},{8,12},{12,8},{16,20},{20,16},{24,28},{28,24},{1,5},{5... | collective-permute-start | bytes 2850824 | tf_op jit(solution)/shard_map/ppermute | solution.py:138
  160.9 2.1 %collective-permute-done.13.other = bf16[928,512]{1,0:T(8,128)(2,1)S(1)} collective-permute-done((bf16[928,512]{1,0:T(8,128)(2,1)S(1)}, bf16[928,512]{1,0:T(8,128)(2,1)S(1)}, u32[]{:S(2)}, u32[]{:S(2)}) %collective-permute-start.13) | collective-permute-done | bytes 950304 | tf_op jit(solution)/shard_map/ppermute | solution.py:138
  163.0 2.2 %shard_map.129 = (f32[768,1024]{1,0:T(8,128)}, f32[153,1024]{1,0:T(8,128)}, f32[1,1]{1,0:T(1,128)}) custom-call(s32[1]{0:T(128)} %bitcast.core, bf16[928,512]{1,0:T(8,128)(2,1)S(1)} %shard_map.128.own, bf16[928,512]{1,0:T(8,128)(2,1)S(1)} %collective-permute-done.13.other), custom_call_target="tpu_custom_call" | custom-call | tf_op jit(solution)/shard_map/pallas_call | solution.py:140
  (4 shorter events, 0.0 us)
Async XLA Ops:
  0.6 0.7 copy-start.1
  1.3 0.7 copy-start.2
  37.5 5.7 %copy-start.10 = (s32[1024]{0:T(1024)S(1)}, s32[1024]{0:T(1024)}, u32[]{:S(2)}) copy-start(s32[1024]{0:T(1024)} %param.17) | copy-start | bytes 12292
  37.5 6.8 %copy-start.9 = (bf16[1024,153]{0,1:T(8,128)(2,1)S(1)}, bf16[1024,153]{0,1:T(8,128)(2,1)}, u32[]{:S(2)}) copy-start(bf16[1024,153]{0,1:T(8,128)(2,1)} %param.19) | copy-start | bytes 940036
  37.5 7.6 %copy-start.3 = (bf16[48,128,128]{2,1,0:T(8,128)(2,1)S(1)}, bf16[48,128,128]{2,1,0:T(8,128)(2,1)}, u32[]{:S(2)}) copy-start(bf16[48,128,128]{2,1,0:T(8,128)(2,1)} %tiles.1) | copy-start | bytes 4718596
  37.5 7.6 %copy-start.4 = (s32[48]{0:T(128)S(1)}, s32[48]{0:T(128)}, u32[]{:S(2)}) copy-start(s32[48]{0:T(128)} %row.1) | copy-start | bytes 580
  37.5 7.6 %copy-start.5 = (s32[48]{0:T(128)S(1)}, s32[48]{0:T(128)}, u32[]{:S(2)}) copy-start(s32[48]{0:T(128)} %column.1) | copy-start | bytes 580
  37.5 47.1 %all-to-all-start.1 = ((bf16[128,16,768]{2,1,0:T(8,128)(2,1)}), bf16[128,16,768]{2,1,0:T(8,128)(2,1)}, u32[]{:S(2)}, u32[]{:S(2)}) async-start(bf16[128,16,768]{2,1,0:T(8,128)(2,1)} %bitcast.19), calls=%async_computation.1 | async-start | bytes 6291456 | tf_op jit(solution)/shard_map/all_to_all | solution.py:329
  55.1 2.0 %copy-start.6 = (bf16[1024,2048]{1,0:T(8,128)(2,1)}, bf16[1024,2048]{1,0:T(8,128)(2,1)S(1)}, u32[]{:S(2)}) copy-start(bf16[1024,2048]{1,0:T(8,128)(2,1)S(1)} %get-tuple-element.19.moved) | copy-start | bytes 12582916
  57.1 1.4 copy-start.7
  58.5 1.3 copy-start.8
  109.2 2.7 %collective-permute-start = (bf16[928,512]{1,0:T(8,128)(2,1)}, bf16[928,512]{1,0:T(8,128)(2,1)S(1)}, u32[]{:S(2)}, u32[]{:S(2)}) collective-permute-start(bf16[928,512]{1,0:T(8,128)(2,1)} %get-tuple-element.23), channel_id=1, source_target_pairs={{0,4},{4,0},{8,12},{12,8},{16,20},{20,16},{24,28},{28,24},{1,5},{5... | collective-permute-start | bytes 2850824 | tf_op jit(solution)/shard_map/ppermute | solution.py:127
  111.9 1.5 copy-start
  113.9 9.1 %collective-permute-start.1 = (bf16[928,128]{1,0:T(8,128)(2,1)S(1)}, bf16[928,128]{1,0:T(8,128)(2,1)S(1)}, u32[]{:S(2)}, u32[]{:S(2)}) collective-permute-start(bf16[928,128]{1,0:T(8,128)(2,1)S(1)} %get-tuple-element.25), channel_id=1, source_target_pairs={{0,32},{4,5},{8,40},{12,13},{16,48},{20,21},{24,56},{28,29},{1,33}... | collective-permute-start | bytes 712712 | tf_op jit(solution)/shard_map/ppermute | solution.py:129
  114.3 8.7 %collective-permute-start.2 = (bf16[928,128]{1,0:T(8,128)(2,1)S(1)}, bf16[928,128]{1,0:T(8,128)(2,1)S(1)}, u32[]{:S(2)}, u32[]{:S(2)}) collective-permute-start(bf16[928,128]{1,0:T(8,128)(2,1)S(1)} %get-tuple-element.26), channel_id=1, source_target_pairs={{0,64},{4,6},{8,72},{12,14},{16,80},{20,22},{24,88},{28,30},{1,65}... | collective-permute-start | bytes 712712 | tf_op jit(solution)/shard_map/ppermute | solution.py:129
  116.3 7.3 %collective-permute-start.3 = (bf16[928,128]{1,0:T(8,128)(2,1)S(1)}, bf16[928,128]{1,0:T(8,128)(2,1)S(1)}, u32[]{:S(2)}, u32[]{:S(2)}) collective-permute-start(bf16[928,128]{1,0:T(8,128)(2,1)S(1)} %get-tuple-element.27), channel_id=1, source_target_pairs={{0,96},{4,7},{8,104},{12,15},{16,112},{20,23},{24,120},{28,31},{1,... | collective-permute-start | bytes 712712 | tf_op jit(solution)/shard_map/ppermute | solution.py:129
  123.9 5.3 %collective-permute-start.6 = (bf16[928,128]{1,0:T(8,128)(2,1)S(1)}, bf16[928,128]{1,0:T(8,128)(2,1)S(1)}, u32[]{:S(2)}, u32[]{:S(2)}) collective-permute-start(bf16[928,128]{1,0:T(8,128)(2,1)S(1)} %shard_map.125.own), channel_id=1, source_target_pairs={{0,3},{4,28},{8,11},{12,4},{16,19},{20,12},{24,27},{28,20},{1,0},{... | collective-permute-start | bytes 712712 | tf_op jit(solution)/shard_map/ppermute | solution.py:132
  124.0 6.6 %collective-permute-start.5 = (bf16[928,128]{1,0:T(8,128)(2,1)S(1)}, bf16[928,128]{1,0:T(8,128)(2,1)S(1)}, u32[]{:S(2)}, u32[]{:S(2)}) collective-permute-start(bf16[928,128]{1,0:T(8,128)(2,1)S(1)} %shard_map.125.own), channel_id=1, source_target_pairs={{0,2},{4,20},{8,10},{12,28},{16,18},{20,4},{24,26},{28,12},{1,3},{... | collective-permute-start | bytes 712712 | tf_op jit(solution)/shard_map/ppermute | solution.py:132
  125.6 7.7 %collective-permute-start.4 = (bf16[928,128]{1,0:T(8,128)(2,1)S(1)}, bf16[928,128]{1,0:T(8,128)(2,1)S(1)}, u32[]{:S(2)}, u32[]{:S(2)}) collective-permute-start(bf16[928,128]{1,0:T(8,128)(2,1)S(1)} %shard_map.125.own), channel_id=1, source_target_pairs={{0,1},{4,12},{8,9},{12,20},{16,17},{20,28},{24,25},{28,4},{1,2},{5... | collective-permute-start | bytes 712712 | tf_op jit(solution)/shard_map/ppermute | solution.py:132
  133.6 5.0 %collective-permute-start.9 = (bf16[928,128]{1,0:T(8,128)(2,1)S(1)}, bf16[928,128]{1,0:T(8,128)(2,1)S(1)}, u32[]{:S(2)}, u32[]{:S(2)}) collective-permute-start(bf16[928,128]{1,0:T(8,128)(2,1)S(1)} %shard_map.126.own), channel_id=1, source_target_pairs={{0,24},{4,100},{8,0},{12,108},{16,8},{20,116},{24,16},{28,124},{1,... | collective-permute-start | bytes 712712 | tf_op jit(solution)/shard_map/ppermute | solution.py:132
  134.5 6.6 %collective-permute-start.8 = (bf16[928,128]{1,0:T(8,128)(2,1)S(1)}, bf16[928,128]{1,0:T(8,128)(2,1)S(1)}, u32[]{:S(2)}, u32[]{:S(2)}) collective-permute-start(bf16[928,128]{1,0:T(8,128)(2,1)S(1)} %shard_map.126.own), channel_id=1, source_target_pairs={{0,16},{4,68},{8,24},{12,76},{16,0},{20,84},{24,8},{28,92},{1,17},... | collective-permute-start | bytes 712712 | tf_op jit(solution)/shard_map/ppermute | solution.py:132
  135.7 8.1 %collective-permute-start.7 = (bf16[928,128]{1,0:T(8,128)(2,1)S(1)}, bf16[928,128]{1,0:T(8,128)(2,1)S(1)}, u32[]{:S(2)}, u32[]{:S(2)}) collective-permute-start(bf16[928,128]{1,0:T(8,128)(2,1)S(1)} %shard_map.126.own), channel_id=1, source_target_pairs={{0,8},{4,36},{8,16},{12,44},{16,24},{20,52},{24,0},{28,60},{1,9},{... | collective-permute-start | bytes 712712 | tf_op jit(solution)/shard_map/ppermute | solution.py:132
  144.1 8.0 %collective-permute-start.12 = (bf16[928,128]{1,0:T(8,128)(2,1)S(1)}, bf16[928,128]{1,0:T(8,128)(2,1)S(1)}, u32[]{:S(2)}, u32[]{:S(2)}) collective-permute-start(bf16[928,128]{1,0:T(8,128)(2,1)S(1)} %shard_map.127.own), channel_id=1, source_target_pairs={{0,96},{4,7},{8,104},{12,15},{16,112},{20,23},{24,120},{28,31},{1,... | collective-permute-start | bytes 712712 | tf_op jit(solution)/shard_map/ppermute | solution.py:134
  146.4 6.6 %collective-permute-start.11 = (bf16[928,128]{1,0:T(8,128)(2,1)S(1)}, bf16[928,128]{1,0:T(8,128)(2,1)S(1)}, u32[]{:S(2)}, u32[]{:S(2)}) collective-permute-start(bf16[928,128]{1,0:T(8,128)(2,1)S(1)} %shard_map.127.own), channel_id=1, source_target_pairs={{0,64},{4,6},{8,72},{12,14},{16,80},{20,22},{24,88},{28,30},{1,65}... | collective-permute-start | bytes 712712 | tf_op jit(solution)/shard_map/ppermute | solution.py:134
  146.7 9.0 %collective-permute-start.10 = (bf16[928,128]{1,0:T(8,128)(2,1)S(1)}, bf16[928,128]{1,0:T(8,128)(2,1)S(1)}, u32[]{:S(2)}, u32[]{:S(2)}) collective-permute-start(bf16[928,128]{1,0:T(8,128)(2,1)S(1)} %shard_map.127.own), channel_id=1, source_target_pairs={{0,32},{4,5},{8,40},{12,13},{16,48},{20,21},{24,56},{28,29},{1,33}... | collective-permute-start | bytes 712712 | tf_op jit(solution)/shard_map/ppermute | solution.py:134
  156.0 7.0 %collective-permute-start.13 = (bf16[928,512]{1,0:T(8,128)(2,1)S(1)}, bf16[928,512]{1,0:T(8,128)(2,1)S(1)}, u32[]{:S(2)}, u32[]{:S(2)}) collective-permute-start(bf16[928,512]{1,0:T(8,128)(2,1)S(1)} %shard_map.128.own), channel_id=1, source_target_pairs={{0,4},{4,0},{8,12},{12,8},{16,20},{20,16},{24,28},{28,24},{1,5},{5... | collective-permute-start | bytes 2850824 | tf_op jit(solution)/shard_map/ppermute | solution.py:138

commit v3 on v2

--- a/solution.py
+++ b/solution.py
@@ -83,28 +83,41 @@
         out[:, pl.ds(pl.multiple_of(at * WIDTH, WIDTH), WIDTH)] = block[...]
 
 
-def finish(core, own, other, grad_one, grad_two, loss):
-    half = SIDE * WIDTH
-    features = grad_one.shape[0]
-    classes = grad_two.shape[0]
-    for offset, part in ((0, own), (1, other)):
-        at = lax.rem(core[0] + offset, 2)
-        columns = pl.ds(pl.multiple_of(at * half, half), half)
-        grad_one[:, columns] = part[:features, :].astype(jnp.float32)
-        grad_two[:, columns] = part[features:, :].astype(jnp.float32)[:classes]
-
-        @pl.when(at == 0)
-        def _():
-            tail = part[ROWS - 16 :, :WIDTH].astype(jnp.float32)
-            row = lax.broadcasted_iota(jnp.int32, tail.shape, 0)
-            lane = lax.broadcasted_iota(jnp.int32, tail.shape, 1)
-            mine = (row == LOSS_ROW - (ROWS - 16)) & (lane < 3)
-            loss[...] = jnp.sum(
-                jnp.sum(jnp.where(mine, tail, 0.0), axis=1, keepdims=True), axis=0, keepdims=True
-            )
-
-
-def call(kernel, outs, scalars=0, arrays=0, limit=40 << 20, cost=None):
+def write_half(at, part, one_far, two_far, one, two, leaving):
+    half = part.shape[1]
+    features = one.shape[0]
+    classes = two.shape[0]
+    columns = pl.ds(pl.multiple_of(at * half, half), half)
+    one[...] = part[:features, :].astype(jnp.float32)
+    first = pltpu.make_async_copy(one, one_far.at[:, columns], leaving.at[0])
+    first.start()
+    two[...] = part[features:, :].astype(jnp.float32)[:classes]
+    second = pltpu.make_async_copy(two, two_far.at[:, columns], leaving.at[1])
+    second.start()
+    return first, second
+
+
+def read_loss(part):
+    tail = part[ROWS - 16 :, :WIDTH].astype(jnp.float32)
+    row = lax.broadcasted_iota(jnp.int32, tail.shape, 0)
+    lane = lax.broadcasted_iota(jnp.int32, tail.shape, 1)
+    mine = (row == LOSS_ROW - (ROWS - 16)) & (lane < 3)
+    return jnp.sum(jnp.sum(jnp.where(mine, tail, 0.0), axis=1, keepdims=True), axis=0, keepdims=True)
+
+
+def write_own(core, own, one_far, two_far, one, two, leaving):
+    for copy in write_half(core[0], own, one_far, two_far, one, two, leaving):
+        copy.wait()
+
+
+def write_other(core, own, other, one_in, two_in, one_far, two_far, loss, one, two, leaving):
+    copies = write_half(1 - core[0], other, one_far, two_far, one, two, leaving)
+    loss[...] = jnp.where(core[0] == 0, read_loss(own), read_loss(other))
+    for copy in copies:
+        copy.wait()
+
+
+def call(kernel, outs, scalars=0, arrays=0, limit=16 << 20, cost=None, scratch=()):
     vmem = pl.BlockSpec(memory_space=pltpu.VMEM)
     smem = pl.BlockSpec(memory_space=pltpu.SMEM)
     return pl.pallas_call(
@@ -112,6 +125,7 @@
         out_shape=outs,
         in_specs=[smem] * scalars + [vmem] * arrays,
         out_specs=jax.tree.map(lambda _: vmem, outs),
+        scratch_shapes=list(scratch),
         compiler_params=pltpu.CompilerParams(vmem_limit_bytes=limit),
         cost_estimate=cost,
     )
@@ -136,17 +150,37 @@
         place, total, *got
     )
     other = lax.ppermute(strip, AXES, swap_pairs())
-    hidden = 2 * SIDE * WIDTH
-    return call(
-        finish,
-        [
-            jax.ShapeDtypeStruct((features, hidden), jnp.float32),
-            jax.ShapeDtypeStruct((classes, hidden), jnp.float32),
-            jax.ShapeDtypeStruct((1, 1), jnp.float32),
-        ],
-        1,
-        2,
-    )(core, strip, other)
+    half = SIDE * WIDTH
+    grads = [
+        jax.ShapeDtypeStruct((features, 2 * half), jnp.float32),
+        jax.ShapeDtypeStruct((classes, 2 * half), jnp.float32),
+    ]
+    anywhere = pl.BlockSpec(memory_space=pl.ANY)
+    vmem = pl.BlockSpec(memory_space=pltpu.VMEM)
+    smem = pl.BlockSpec(memory_space=pltpu.SMEM)
+    scratch = [
+        pltpu.VMEM((features, half), jnp.float32),
+        pltpu.VMEM((classes, half), jnp.float32),
+        pltpu.SemaphoreType.DMA((2,)),
+    ]
+    params = pltpu.CompilerParams(vmem_limit_bytes=16 << 20)
+    grad_one, grad_two = pl.pallas_call(
+        write_own,
+        out_shape=grads,
+        in_specs=[smem, vmem],
+        out_specs=[anywhere] * 2,
+        scratch_shapes=scratch,
+        compiler_params=params,
+    )(core, strip)
+    return pl.pallas_call(
+        write_other,
+        out_shape=[*grads, jax.ShapeDtypeStruct((1, 1), jnp.float32)],
+        in_specs=[smem, vmem, vmem, anywhere, anywhere],
+        out_specs=[anywhere, anywhere, vmem],
+        scratch_shapes=scratch,
+        input_output_aliases={3: 0, 4: 1},
+        compiler_params=params,
+    )(core, strip, other, grad_one, grad_two)
 
 
 def number_requests(parts, rows, requests, position):
@@ -180,6 +214,44 @@
     requests[...] = total.astype(jnp.int32)
 
 
+def fetch_rows(wanted, table, far, narrow, wide, some, out, arrival, leaving):
+    stored, width = table.shape
+    step = stored // arrival.shape[0]
+
+    def load(block):
+        rows = pl.ds(block * step, step)
+        return pltpu.make_async_copy(table.at[rows, :], narrow.at[rows, :], arrival.at[block])
+
+    for block in range(arrival.shape[0]):
+        load(block).start()
+    for block in range(arrival.shape[0]):
+        load(block).wait()
+        for start in range(block * step, (block + 1) * step, 128):
+            rows = slice(start, start + 128)
+            wide[rows, :] = narrow[rows, :].astype(jnp.float32)
+
+    devices, capacity = wanted.shape
+    owners = some.shape[0] // capacity
+
+    def send(block):
+        rows = pl.ds(pl.multiple_of(block * some.shape[0], some.shape[0]), some.shape[0])
+        return pltpu.make_async_copy(out.at[rows, :], far.at[rows, :], leaving.at[block])
+
+    @pl.loop(0, devices // owners)
+    def _(block):
+        for owner in range(owners):
+            for slot in range(capacity):
+                row = wanted[block * owners + owner, slot]
+                some[pl.ds(owner * capacity + slot, 1), :] = wide[pl.ds(row, 1), :]
+        rows = pl.ds(pl.multiple_of(block * some.shape[0], some.shape[0]), some.shape[0])
+        out[rows, :] = some[...].astype(jnp.bfloat16)
+        send(block).start()
+
+    @pl.loop(0, devices // owners)
+    def _(block):
+        send(block).wait()
+
+
 def build_spread(row, column, count, tiles, position, dense, turned, moved):
     nodes = dense.shape[0]
     tile = tiles.shape[1]
@@ -208,6 +280,15 @@
 
 def train(
     core,
+    arrived_far,
+    moved_far,
+    dense_far,
+    turned_far,
+    one_far,
+    two_far,
+    labels_far,
+    sent_far,
+    own_far,
     arrived,
     moved,
     dense,
@@ -223,18 +304,50 @@
     smooth,
     upstream,
     upstream_turned,
+    arrival,
+    leaving,
     *,
     classes,
 ):
     nodes = dense.shape[0]
     features = mixed_turned.shape[0]
     step = 256
-    for start in range(0, nodes, step):
+    tiles = range(0, nodes, step)
+
+    def load(index, far, near):
+        return pltpu.make_async_copy(far, near, arrival.at[index])
+
+    get_arrived = load(0, arrived_far, arrived)
+    get_one = load(1, one_far, layer_one)
+    get_dense = load(2, dense_far, dense)
+    get_two = load(3, two_far, layer_two)
+    get_labels = load(4, labels_far, labels)
+    get_turned = load(5, turned_far, turned)
+    get_moved = [
+        load(6 + at, moved_far.at[pl.ds(start, step), :], moved.at[pl.ds(start, step), :])
+        for at, start in enumerate(tiles)
+    ]
+    get_arrived.start()
+    get_moved[0].start()
+    get_one.start()
+    get_arrived.wait()
+    get_moved[0].wait()
+    for copy in get_moved[1:]:
+        copy.start()
+    for at, start in enumerate(tiles):
         rows = slice(start, start + step)
+        if at > 0:
+            get_moved[at].wait()
         mixed = jnp.dot(moved[rows, :], arrived[...], preferred_element_type=jnp.float32).astype(
             jnp.bfloat16
         )
         mixed_turned[:, rows] = mixed.T
+        if at == 0:
+            get_one.wait()
+            get_dense.start()
+            get_two.start()
+            get_labels.start()
+            get_turned.start()
         before = jnp.dot(mixed, layer_one[...], preferred_element_type=jnp.float32)
         square = before * before
         rate = 0.7978845608028654
@@ -244,8 +357,11 @@
         slope[rows, :] = rise + 0.5 * before * (1.0 - bend * bend) * (
             rate + (3.0 * 0.044715 * rate) * square
         )
+    get_dense.wait()
+    get_two.wait()
+    get_labels.wait()
     loss = jnp.zeros((1, 1), jnp.float32)
-    for start in range(0, nodes, step):
+    for start in tiles:
         rows = slice(start, start + step)
         spread = jnp.dot(dense[rows, :], hidden[...], preferred_element_type=jnp.float32).astype(
             jnp.bfloat16
@@ -269,32 +385,35 @@
     middle = (loss - high).astype(jnp.bfloat16).astype(jnp.float32)
     low = loss - high - middle
     half = SIDE * WIDTH
-    for offset, out in ((1, sent), (0, own)):
+    get_turned.wait()
+    stores = []
+    for offset, out, far in ((1, sent, sent_far), (0, own, own_far)):
         part = lax.rem(core[0] + offset, 2)
-        for start in range(0, half, step):
-            columns = pl.ds(pl.multiple_of(part * half + start, step), step)
-            place = slice(start, start + step)
-            second = jnp.dot(
-                upstream_turned[: ROWS - features, :],
-                smooth[:, columns],
-                preferred_element_type=jnp.float32,
-            )
-            if start == 0:
-                row = lax.broadcasted_iota(jnp.int32, second.shape, 0)
-                lane = lax.broadcasted_iota(jnp.int32, second.shape, 1)
-                here = (row == LOSS_ROW - features) & (part == 0)
-                second += jnp.where(here & (lane == 0), high, 0.0)
-                second += jnp.where(here & (lane == 1), middle, 0.0)
-                second += jnp.where(here & (lane == 2), low, 0.0)
-            out[features:, place] = second.astype(out.dtype)
-            back = jnp.dot(
-                upstream[...], layer_two[:, columns], preferred_element_type=jnp.float32
-            ).astype(jnp.bfloat16)
-            back = jnp.dot(turned[...], back, preferred_element_type=jnp.float32)
-            back = (slope[:, columns] * back).astype(jnp.bfloat16)
-            out[:features, place] = jnp.dot(
-                mixed_turned[...], back, preferred_element_type=jnp.float32
-            ).astype(out.dtype)
+        columns = pl.ds(pl.multiple_of(part * half, half), half)
+        second = jnp.dot(
+            upstream_turned[: ROWS - features, :],
+            smooth[:, columns],
+            preferred_element_type=jnp.float32,
+        )
+        row = lax.broadcasted_iota(jnp.int32, second.shape, 0)
+        lane = lax.broadcasted_iota(jnp.int32, second.shape, 1)
+        here = (row == LOSS_ROW - features) & (part == 0)
+        second += jnp.where(here & (lane == 0), high, 0.0)
+        second += jnp.where(here & (lane == 1), middle, 0.0)
+        second += jnp.where(here & (lane == 2), low, 0.0)
+        out[features:, :] = second.astype(out.dtype)
+        back = jnp.dot(
+            upstream[...], layer_two[:, columns], preferred_element_type=jnp.float32
+        ).astype(jnp.bfloat16)
+        back = jnp.dot(turned[...], back, preferred_element_type=jnp.float32)
+        back = (slope[:, columns] * back).astype(jnp.bfloat16)
+        out[:features, :] = jnp.dot(
+            mixed_turned[...], back, preferred_element_type=jnp.float32
+        ).astype(out.dtype)
+        stores.append(pltpu.make_async_copy(out, far, leaving.at[len(stores)]))
+        stores[-1].start()
+    for copy in stores:
+        copy.wait()
 
 
 def on_device(
@@ -324,8 +443,27 @@
         ],
         0,
         2,
+        limit=56 << 20,
     )(source_part.reshape(1, nodes), source_row.reshape(1, nodes))
-    found = features[lax.all_to_all(requests, AXES, split_axis=0, concat_axis=0, tiled=True)]
+    wanted = lax.all_to_all(requests, AXES, split_axis=0, concat_axis=0, tiled=True)
+    anywhere = pl.BlockSpec(memory_space=pl.ANY)
+    vmem = pl.BlockSpec(memory_space=pltpu.VMEM)
+    smem = pl.BlockSpec(memory_space=pltpu.SMEM)
+    found = pl.pallas_call(
+        fetch_rows,
+        out_shape=jax.ShapeDtypeStruct((slots, width), bf),
+        in_specs=[smem, anywhere],
+        out_specs=anywhere,
+        scratch_shapes=[
+            pltpu.VMEM(features.shape, bf),
+            pltpu.VMEM(features.shape, jnp.float32),
+            pltpu.VMEM((64, width), jnp.float32),
+            pltpu.VMEM((slots, width), bf),
+            pltpu.SemaphoreType.DMA((8,)),
+            pltpu.SemaphoreType.DMA((slots // 64,)),
+        ],
+        compiler_params=pltpu.CompilerParams(vmem_limit_bytes=56 << 20),
+    )(wanted, features)
     arrived = lax.all_to_all(found, AXES, split_axis=0, concat_axis=0, tiled=True)
     dense, turned, moved = call(
         build_spread,
@@ -343,22 +481,32 @@
     padded = jnp.pad(layer_two.T, ((0, 256 - classes), (0, 0)))
     core = lax.rem(lax.axis_index("store"), 2).astype(jnp.int32).reshape(1)
     half = SIDE * WIDTH
-    vmem = pl.BlockSpec(memory_space=pltpu.VMEM)
     sent, own = pl.pallas_call(
         partial(train, classes=classes),
         out_shape=[
             jax.ShapeDtypeStruct((ROWS, half), bf),
-            jax.ShapeDtypeStruct((ROWS, half), jnp.float32),
+            jax.ShapeDtypeStruct((ROWS, half), bf),
         ],
-        in_specs=[pl.BlockSpec(memory_space=pltpu.SMEM)] + [vmem] * 7,
-        out_specs=[vmem] * 2,
+        in_specs=[smem] + [anywhere] * 7,
+        out_specs=[anywhere] * 2,
         scratch_shapes=[
+            pltpu.VMEM((slots, width), bf),
+            pltpu.VMEM((nodes, slots), bf),
+            pltpu.VMEM((nodes, nodes), bf),
+            pltpu.VMEM((nodes, nodes), bf),
+            pltpu.VMEM((width, hidden), bf),
+            pltpu.VMEM((256, hidden), bf),
+            pltpu.VMEM((nodes, 1), jnp.int32),
+            pltpu.VMEM((ROWS, half), bf),
+            pltpu.VMEM((ROWS, half), bf),
             pltpu.VMEM((width, nodes), bf),
             pltpu.VMEM((nodes, hidden), jnp.float32),
             pltpu.VMEM((nodes, hidden), bf),
             pltpu.VMEM((nodes, hidden), bf),
             pltpu.VMEM((nodes, 256), bf),
             pltpu.VMEM((256, nodes), bf),
+            pltpu.SemaphoreType.DMA((10,)),
+            pltpu.SemaphoreType.DMA((2,)),
         ],
         compiler_params=pltpu.CompilerParams(vmem_limit_bytes=56 << 20),
         cost_estimate=pl.CostEstimate(

time: 166 us -> 158 us (0.952)
  local copies, waits for them, and re-layouts: 23.2 us -> 7.82 us
  Pallas kernels: 38.9 us -> 47.6 us
  waiting for transfers between devices: 60.7 us -> 59 us
    gather x1 -> x0, local copies, waits for them, and re-layouts: 13.7 us -> none  [on_device(): features[lax.all_to_all(requests, AXES, split_axis=0, concat_axis=0, tile...]
    pallas_call x1 -> x3, Pallas kernels: 2.22 us -> 13.9 us  [the longest x1 10.6 us: on_device(): pl.pallas_call(fetch_rows, out_shape=jax.ShapeDtypeStruct((slots, width),...]
    pallas_call x1, Pallas kernels: 24.6 us -> 20.1 us  [on_device(): pl.pallas_call(partial(train, classes=classes), out_shape=[jax.ShapeDtype...]
    unnamed x22 -> x20, local copies, waits for them, and re-layouts: 7.57 us -> 5.89 us
  transfers between devices with their start and end apart: 15 -> 15, of which waited for: 14 -> 14; matrix products, arithmetic and copies ran while one was open for 1% -> 1% of each run, Pallas kernels for 6% -> 7%
where the time goes in v3:
time: 158 us
  waiting for transfers between devices  59 us (37%)
  Pallas kernels  47.6 us (30%)
  blocking collectives  21.9 us (14%)
  starting transfers between devices  19.7 us (12%)
  local copies, waits for them, and re-layouts  7.82 us (5%)
  between operations  1.6 us (1%)
    all_to_all x1, waiting for transfers between devices, on_device(): lax.all_to_all(found, AXES, split_axis=0, concat_axis=0, tiled=True)  24.5 us
    all_to_all x1, blocking collectives, on_device(): lax.all_to_all(requests, AXES, split_axis=0, concat_axis=0, tiled=True)  21.9 us
    pallas_call x1, Pallas kernels, on_device(): pl.pallas_call(partial(train, classes=classes), out_shape=[jax.ShapeDtype...  20.1 us
    ppermute x6, waiting for transfers between devices, sum_over_devices(): got = [lax.ppermute(total, AXES, shift_pairs(axes, k)) for k in (1, 2, 3)]  15.8 us
    pallas_call x1, Pallas kernels, on_device(): pl.pallas_call(fetch_rows, out_shape=jax.ShapeDtypeStruct((slots, width),...  10.6 us
    pallas_call x1, Pallas kernels, on_device(): call(build_spread, [jax.ShapeDtypeStruct((nodes, nodes), bf), jax.ShapeDt...  10.1 us
    ppermute x3, waiting for transfers between devices, sum_over_devices(): got = [lax.ppermute(total, AXES, shift_pairs(FIRST, k)) for k in (1, 2, 3)]  8.61 us
    ppermute x3, waiting for transfers between devices, sum_over_devices(): lax.ppermute(part, AXES, shift_pairs(FIRST, k + 1))  6.8 us
  transfers between devices with their start and end apart: 15, of which 14 were waited for; matrix products, arithmetic and copies ran while one was open for 1% of the time, Pallas kernels for 7%

profile of v3, /device:TPU:1, one launch (start us, length us, event | category | flops | bytes accessed | tf_op | source)
XLA Modules:
  0.0 157.6 jit_solution(14814916939656208157)
XLA Ops:
  0.6 1.8 %shard_map.121 = (s32[128,16]{1,0:T(8,128)}, s32[1,1024]{1,0:T(1,128)}) custom-call(s32[1,1024]{1,0:T(1,128)} %bitcast.20, s32[1,1024]{1,0:T(1,128)} %bitcast.21), custom_call_target="tpu_custom_call" | custom-call | tf_op jit(solution)/shard_map/pallas_call | solution.py:438
  2.5 21.9 %all_to_all.22 = s32[128,1,16]{2,1,0:T(1,128)} all-to-all(s32[128,1,16]{2,1,0:T(1,128)} %bitcast.18), channel_id=1, replica_groups=mesh['store'=32,'batch'=4] {'store','batch'}, dimensions={0} | all-to-all | bytes 16384 | tf_op jit(solution)/shard_map/all_to_all | solution.py:448
  24.3 10.6 %shard_map.122 = bf16[2048,768]{1,0:T(8,128)(2,1)} custom-call(s32[128,16]{1,0:T(8,128)} %bitcast.17, bf16[4096,768]{1,0:T(8,128)(2,1)} %table.1), custom_call_target="tpu_custom_call" | custom-call | tf_op jit(solution)/shard_map/pallas_call | solution.py:452
  35.0 0.0 copy-start.9
  35.0 0.0 copy-start.8
  35.0 0.0 copy-start.1
  35.0 0.0 copy-start.2
  35.0 0.0 copy-start.3
  35.0 0.0 copy-start.4
  35.1 4.8 %all-to-all-start.1 = ((bf16[128,16,768]{2,1,0:T(8,128)(2,1)}), bf16[128,16,768]{2,1,0:T(8,128)(2,1)}, u32[]{:S(2)}, u32[]{:S(2)}) async-start(bf16[128,16,768]{2,1,0:T(8,128)(2,1)} %bitcast.14), calls=%async_computation.1 | async-start | bytes 6291456 | tf_op jit(solution)/shard_map/all_to_all | solution.py:467
  40.5 0.0 copy-done.9
  40.6 1.1 copy.17.labels_far
  41.6 0.0 copy-done.8
  41.7 0.8 pad.4.two_far
  42.5 0.0 copy-done.1
  42.5 0.0 copy-done.2
  42.5 0.0 copy-done.3
  42.5 0.0 copy-done.4
  42.5 10.1 %shard_map.123 = (bf16[1024,1024]{1,0:T(8,128)(2,1)S(1)}, bf16[1024,1024]{1,0:T(8,128)(2,1)S(1)}, bf16[1024,2048]{1,0:T(8,128)(2,1)S(1)}) custom-call(s32[48]{0:T(128)S(1)} %copy-done.3, s32[48]{0:T(128)S(1)} %copy-done.4, s32[1]{0:T(128)S(6)} %copy.20.count, bf16[48,128,128]{2,1,0:T(8,128)(2,1)S(1)} %copy-done.1, s32[1,1024]{1,0:T(1,128)S(1)} %copy-done.2), custom_call_target="tpu_custom_call" | custom-call | flops 4294967296 | bytes 12582912 | tf_op jit(solution)/shard_map/pallas_call | solution.py:468
  52.7 0.0 copy-start.5
  52.7 2.0 %copy-done.5 = bf16[1024,2048]{1,0:T(8,128)(2,1)} copy-done((bf16[1024,2048]{1,0:T(8,128)(2,1)}, bf16[1024,2048]{1,0:T(8,128)(2,1)S(1)}, u32[]{:S(2)}) %copy-start.5) | copy-done | bytes 4194328
  54.6 0.0 copy-start.6
  54.6 1.4 copy-done.6
  56.0 0.0 copy-start.7
  56.0 1.3 copy-done.7
  57.3 24.5 %all-to-all-done.1 = bf16[128,16,768]{2,1,0:T(8,128)(2,1)} async-done(((bf16[128,16,768]{2,1,0:T(8,128)(2,1)}), bf16[128,16,768]{2,1,0:T(8,128)(2,1)}, u32[]{:S(2)}, u32[]{:S(2)}) %all-to-all-start.1) | async-done | bytes 3145760 | tf_op jit(solution)/shard_map/all_to_all | solution.py:467
  81.8 20.1 %shard_map.124 = (bf16[928,512]{1,0:T(8,128)(2,1)}, bf16[928,512]{1,0:T(8,128)(2,1)}) custom-call(s32[1]{0:T(128)} %bitcast.core, bf16[2048,768]{1,0:T(8,128)(2,1)} %bitcast.8.arrived_far, bf16[1024,2048]{1,0:T(8,128)(2,1)} %copy-done.5, bf16[1024,1024]{1,0:T(8,128)(2,1)} %copy-done.6, bf16[1024,1024]{1,0:T(8,128)(2,1)} %copy-done.7, ...), custom_call_target="tpu_custom_call" | custom-call | flops 12884901888 | bytes 16777216 | tf_op jit(solution)/shard_map/pallas_call | solution.py:484
  101.9 0.3 collective-permute-start
  102.2 2.5 %collective-permute-done.arrived = bf16[928,512]{1,0:T(8,128)(2,1)S(1)} collective-permute-done((bf16[928,512]{1,0:T(8,128)(2,1)}, bf16[928,512]{1,0:T(8,128)(2,1)S(1)}, u32[]{:S(2)}, u32[]{:S(2)}) %collective-permute-start) | collective-permute-done | bytes 950304 | tf_op jit(solution)/shard_map/ppermute | solution.py:141
  104.7 0.0 copy-start
  104.7 1.2 copy-done
  105.9 0.5 shard_map.125
  106.4 0.4 collective-permute-start.1
  106.9 2.0 %collective-permute-start.2 = (bf16[928,128]{1,0:T(8,128)(2,1)S(1)}, bf16[928,128]{1,0:T(8,128)(2,1)S(1)}, u32[]{:S(2)}, u32[]{:S(2)}) collective-permute-start(bf16[928,128]{1,0:T(8,128)(2,1)S(1)} %get-tuple-element.28), channel_id=1, source_target_pairs={{0,64},{4,6},{8,72},{12,14},{16,80},{20,22},{24,88},{28,30},{1,65}... | collective-permute-start | bytes 712712 | tf_op jit(solution)/shard_map/ppermute | solution.py:143
  108.8 0.5 collective-permute-start.3
  109.3 6.2 %collective-permute-done.1.one = bf16[928,128]{1,0:T(8,128)(2,1)S(1)} collective-permute-done((bf16[928,128]{1,0:T(8,128)(2,1)S(1)}, bf16[928,128]{1,0:T(8,128)(2,1)S(1)}, u32[]{:S(2)}, u32[]{:S(2)}) %collective-permute-start.1) | collective-permute-done | bytes 237600 | tf_op jit(solution)/shard_map/ppermute | solution.py:143
  115.5 0.0 collective-permute-done.2.two
  115.5 0.6 collective-permute-done.3.three
  116.2 0.3 shard_map.126.own
  116.4 0.1 collective-permute-start.6
  116.5 1.6 collective-permute-start.5
  118.1 0.0 collective-permute-start.4
  118.1 3.6 %collective-permute-done.6.three = bf16[928,128]{1,0:T(8,128)(2,1)S(1)} collective-permute-done((bf16[928,128]{1,0:T(8,128)(2,1)S(1)}, bf16[928,128]{1,0:T(8,128)(2,1)S(1)}, u32[]{:S(2)}, u32[]{:S(2)}) %collective-permute-start.6) | collective-permute-done | bytes 237600 | tf_op jit(solution)/shard_map/ppermute | solution.py:146
  121.7 1.4 collective-permute-done.5.two
  123.1 2.7 %collective-permute-done.4.one = bf16[928,128]{1,0:T(8,128)(2,1)S(1)} collective-permute-done((bf16[928,128]{1,0:T(8,128)(2,1)S(1)}, bf16[928,128]{1,0:T(8,128)(2,1)S(1)}, u32[]{:S(2)}, u32[]{:S(2)}) %collective-permute-start.4) | collective-permute-done | bytes 237600 | tf_op jit(solution)/shard_map/ppermute | solution.py:146
  125.8 0.3 shard_map.127.own
  126.1 0.9 collective-permute-start.9
  127.0 1.2 collective-permute-start.8
  128.2 0.0 collective-permute-start.7
  128.2 2.9 %collective-permute-done.9.three = bf16[928,128]{1,0:T(8,128)(2,1)S(1)} collective-permute-done((bf16[928,128]{1,0:T(8,128)(2,1)S(1)}, bf16[928,128]{1,0:T(8,128)(2,1)S(1)}, u32[]{:S(2)}, u32[]{:S(2)}) %collective-permute-start.9) | collective-permute-done | bytes 237600 | tf_op jit(solution)/shard_map/ppermute | solution.py:146
  131.1 2.5 %collective-permute-done.8.two = bf16[928,128]{1,0:T(8,128)(2,1)S(1)} collective-permute-done((bf16[928,128]{1,0:T(8,128)(2,1)S(1)}, bf16[928,128]{1,0:T(8,128)(2,1)S(1)}, u32[]{:S(2)}, u32[]{:S(2)}) %collective-permute-start.8) | collective-permute-done | bytes 237600 | tf_op jit(solution)/shard_map/ppermute | solution.py:146
  133.6 2.7 %collective-permute-done.7.one = bf16[928,128]{1,0:T(8,128)(2,1)S(1)} collective-permute-done((bf16[928,128]{1,0:T(8,128)(2,1)S(1)}, bf16[928,128]{1,0:T(8,128)(2,1)S(1)}, u32[]{:S(2)}, u32[]{:S(2)}) %collective-permute-start.7) | collective-permute-done | bytes 237600 | tf_op jit(solution)/shard_map/ppermute | solution.py:146
  136.3 0.3 shard_map.128.own
  136.6 2.4 %collective-permute-start.12 = (bf16[928,128]{1,0:T(8,128)(2,1)S(1)}, bf16[928,128]{1,0:T(8,128)(2,1)S(1)}, u32[]{:S(2)}, u32[]{:S(2)}) collective-permute-start(bf16[928,128]{1,0:T(8,128)(2,1)S(1)} %shard_map.128.own), channel_id=1, source_target_pairs={{0,96},{4,7},{8,104},{12,15},{16,112},{20,23},{24,120},{28,31},{1,... | collective-permute-start | bytes 712712 | tf_op jit(solution)/shard_map/ppermute | solution.py:148
  139.0 0.3 collective-permute-start.11
  139.3 0.4 collective-permute-start.10
  139.7 4.9 %collective-permute-done.12.three = bf16[928,128]{1,0:T(8,128)(2,1)S(1)} collective-permute-done((bf16[928,128]{1,0:T(8,128)(2,1)S(1)}, bf16[928,128]{1,0:T(8,128)(2,1)S(1)}, u32[]{:S(2)}, u32[]{:S(2)}) %collective-permute-start.12) | collective-permute-done | bytes 237600 | tf_op jit(solution)/shard_map/ppermute | solution.py:148
  144.6 1.0 collective-permute-done.11.two
  145.6 2.7 %collective-permute-done.10.one = bf16[928,128]{1,0:T(8,128)(2,1)S(1)} collective-permute-done((bf16[928,128]{1,0:T(8,128)(2,1)S(1)}, bf16[928,128]{1,0:T(8,128)(2,1)S(1)}, u32[]{:S(2)}, u32[]{:S(2)}) %collective-permute-start.10) | collective-permute-done | bytes 237600 | tf_op jit(solution)/shard_map/ppermute | solution.py:148
  148.3 0.3 shard_map.129.own
  148.5 4.9 %collective-permute-start.13 = (bf16[928,512]{1,0:T(8,128)(2,1)S(1)}, bf16[928,512]{1,0:T(8,128)(2,1)S(1)}, u32[]{:S(2)}, u32[]{:S(2)}) collective-permute-start(bf16[928,512]{1,0:T(8,128)(2,1)S(1)} %shard_map.129.own), channel_id=1, source_target_pairs={{0,4},{4,0},{8,12},{12,8},{16,20},{20,16},{24,28},{28,24},{1,5},{5... | collective-permute-start | bytes 2850824 | tf_op jit(solution)/shard_map/ppermute | solution.py:152
  153.4 1.4 shard_map.130
  154.8 0.8 collective-permute-done.13.other
  155.6 1.9 %shard_map.131 = (f32[768,1024]{1,0:T(8,128)}, f32[153,1024]{1,0:T(8,128)}, f32[1,1]{1,0:T(1,128)}) custom-call(s32[1]{0:T(128)} %bitcast.core, bf16[928,512]{1,0:T(8,128)(2,1)S(1)} %shard_map.129.own, bf16[928,512]{1,0:T(8,128)(2,1)S(1)} %collective-permute-done.13.other, ...), custom_call_target="tpu_custom_call", output_to_operand_aliasing={{0}: (3, {}), {1}: (4, {})} | custom-call | tf_op jit(solution)/shard_map/pallas_call | solution.py:175
Async XLA Ops:
  35.0 5.6 %copy-start.9 = (s32[1024]{0:T(1024)S(1)}, s32[1024]{0:T(1024)}, u32[]{:S(2)}) copy-start(s32[1024]{0:T(1024)} %param.17) | copy-start | bytes 12292
  35.0 6.6 %copy-start.8 = (bf16[1024,153]{0,1:T(8,128)(2,1)S(1)}, bf16[1024,153]{0,1:T(8,128)(2,1)}, u32[]{:S(2)}) copy-start(bf16[1024,153]{0,1:T(8,128)(2,1)} %param.19) | copy-start | bytes 940036
  35.0 7.5 %copy-start.1 = (bf16[48,128,128]{2,1,0:T(8,128)(2,1)S(1)}, bf16[48,128,128]{2,1,0:T(8,128)(2,1)}, u32[]{:S(2)}) copy-start(bf16[48,128,128]{2,1,0:T(8,128)(2,1)} %tiles.1) | copy-start | bytes 4718596
  35.0 7.5 %copy-start.2 = (s32[1,1024]{1,0:T(1,128)S(1)}, s32[1,1024]{1,0:T(1,128)}, u32[]{:S(2)}) copy-start(s32[1,1024]{1,0:T(1,128)} %get-tuple-element.20.position) | copy-start | bytes 12292
  35.0 7.5 %copy-start.3 = (s32[48]{0:T(128)S(1)}, s32[48]{0:T(128)}, u32[]{:S(2)}) copy-start(s32[48]{0:T(128)} %row.1) | copy-start | bytes 580
  35.0 7.5 %copy-start.4 = (s32[48]{0:T(128)S(1)}, s32[48]{0:T(128)}, u32[]{:S(2)}) copy-start(s32[48]{0:T(128)} %column.1) | copy-start | bytes 580
  35.1 46.7 %all-to-all-start.1 = ((bf16[128,16,768]{2,1,0:T(8,128)(2,1)}), bf16[128,16,768]{2,1,0:T(8,128)(2,1)}, u32[]{:S(2)}, u32[]{:S(2)}) async-start(bf16[128,16,768]{2,1,0:T(8,128)(2,1)} %bitcast.14), calls=%async_computation.1 | async-start | bytes 6291456 | tf_op jit(solution)/shard_map/all_to_all | solution.py:467
  52.7 2.0 %copy-start.5 = (bf16[1024,2048]{1,0:T(8,128)(2,1)}, bf16[1024,2048]{1,0:T(8,128)(2,1)S(1)}, u32[]{:S(2)}) copy-start(bf16[1024,2048]{1,0:T(8,128)(2,1)S(1)} %get-tuple-element.21.moved_far) | copy-start | bytes 12582916
  54.6 1.4 copy-start.6
  56.0 1.3 copy-start.7
  101.9 2.8 %collective-permute-start = (bf16[928,512]{1,0:T(8,128)(2,1)}, bf16[928,512]{1,0:T(8,128)(2,1)S(1)}, u32[]{:S(2)}, u32[]{:S(2)}) collective-permute-start(bf16[928,512]{1,0:T(8,128)(2,1)} %get-tuple-element.25), channel_id=1, source_target_pairs={{0,4},{4,0},{8,12},{12,8},{16,20},{20,16},{24,28},{28,24},{1,5},{5... | collective-permute-start | bytes 2850824 | tf_op jit(solution)/shard_map/ppermute | solution.py:141
  104.7 1.2 copy-start
  106.4 9.1 %collective-permute-start.1 = (bf16[928,128]{1,0:T(8,128)(2,1)S(1)}, bf16[928,128]{1,0:T(8,128)(2,1)S(1)}, u32[]{:S(2)}, u32[]{:S(2)}) collective-permute-start(bf16[928,128]{1,0:T(8,128)(2,1)S(1)} %get-tuple-element.27), channel_id=1, source_target_pairs={{0,32},{4,5},{8,40},{12,13},{16,48},{20,21},{24,56},{28,29},{1,33}... | collective-permute-start | bytes 712712 | tf_op jit(solution)/shard_map/ppermute | solution.py:143
  106.9 8.7 %collective-permute-start.2 = (bf16[928,128]{1,0:T(8,128)(2,1)S(1)}, bf16[928,128]{1,0:T(8,128)(2,1)S(1)}, u32[]{:S(2)}, u32[]{:S(2)}) collective-permute-start(bf16[928,128]{1,0:T(8,128)(2,1)S(1)} %get-tuple-element.28), channel_id=1, source_target_pairs={{0,64},{4,6},{8,72},{12,14},{16,80},{20,22},{24,88},{28,30},{1,65}... | collective-permute-start | bytes 712712 | tf_op jit(solution)/shard_map/ppermute | solution.py:143
  108.8 7.3 %collective-permute-start.3 = (bf16[928,128]{1,0:T(8,128)(2,1)S(1)}, bf16[928,128]{1,0:T(8,128)(2,1)S(1)}, u32[]{:S(2)}, u32[]{:S(2)}) collective-permute-start(bf16[928,128]{1,0:T(8,128)(2,1)S(1)} %get-tuple-element.29), channel_id=1, source_target_pairs={{0,96},{4,7},{8,104},{12,15},{16,112},{20,23},{24,120},{28,31},{1,... | collective-permute-start | bytes 712712 | tf_op jit(solution)/shard_map/ppermute | solution.py:143
  116.4 5.3 %collective-permute-start.6 = (bf16[928,128]{1,0:T(8,128)(2,1)S(1)}, bf16[928,128]{1,0:T(8,128)(2,1)S(1)}, u32[]{:S(2)}, u32[]{:S(2)}) collective-permute-start(bf16[928,128]{1,0:T(8,128)(2,1)S(1)} %shard_map.126.own), channel_id=1, source_target_pairs={{0,3},{4,28},{8,11},{12,4},{16,19},{20,12},{24,27},{28,20},{1,0},{... | collective-permute-start | bytes 712712 | tf_op jit(solution)/shard_map/ppermute | solution.py:146
  116.5 6.6 %collective-permute-start.5 = (bf16[928,128]{1,0:T(8,128)(2,1)S(1)}, bf16[928,128]{1,0:T(8,128)(2,1)S(1)}, u32[]{:S(2)}, u32[]{:S(2)}) collective-permute-start(bf16[928,128]{1,0:T(8,128)(2,1)S(1)} %shard_map.126.own), channel_id=1, source_target_pairs={{0,2},{4,20},{8,10},{12,28},{16,18},{20,4},{24,26},{28,12},{1,3},{... | collective-permute-start | bytes 712712 | tf_op jit(solution)/shard_map/ppermute | solution.py:146
  118.1 7.7 %collective-permute-start.4 = (bf16[928,128]{1,0:T(8,128)(2,1)S(1)}, bf16[928,128]{1,0:T(8,128)(2,1)S(1)}, u32[]{:S(2)}, u32[]{:S(2)}) collective-permute-start(bf16[928,128]{1,0:T(8,128)(2,1)S(1)} %shard_map.126.own), channel_id=1, source_target_pairs={{0,1},{4,12},{8,9},{12,20},{16,17},{20,28},{24,25},{28,4},{1,2},{5... | collective-permute-start | bytes 712712 | tf_op jit(solution)/shard_map/ppermute | solution.py:146
  126.1 5.0 %collective-permute-start.9 = (bf16[928,128]{1,0:T(8,128)(2,1)S(1)}, bf16[928,128]{1,0:T(8,128)(2,1)S(1)}, u32[]{:S(2)}, u32[]{:S(2)}) collective-permute-start(bf16[928,128]{1,0:T(8,128)(2,1)S(1)} %shard_map.127.own), channel_id=1, source_target_pairs={{0,24},{4,100},{8,0},{12,108},{16,8},{20,116},{24,16},{28,124},{1,... | collective-permute-start | bytes 712712 | tf_op jit(solution)/shard_map/ppermute | solution.py:146
  127.0 6.6 %collective-permute-start.8 = (bf16[928,128]{1,0:T(8,128)(2,1)S(1)}, bf16[928,128]{1,0:T(8,128)(2,1)S(1)}, u32[]{:S(2)}, u32[]{:S(2)}) collective-permute-start(bf16[928,128]{1,0:T(8,128)(2,1)S(1)} %shard_map.127.own), channel_id=1, source_target_pairs={{0,16},{4,68},{8,24},{12,76},{16,0},{20,84},{24,8},{28,92},{1,17},... | collective-permute-start | bytes 712712 | tf_op jit(solution)/shard_map/ppermute | solution.py:146
  128.2 8.1 %collective-permute-start.7 = (bf16[928,128]{1,0:T(8,128)(2,1)S(1)}, bf16[928,128]{1,0:T(8,128)(2,1)S(1)}, u32[]{:S(2)}, u32[]{:S(2)}) collective-permute-start(bf16[928,128]{1,0:T(8,128)(2,1)S(1)} %shard_map.127.own), channel_id=1, source_target_pairs={{0,8},{4,36},{8,16},{12,44},{16,24},{20,52},{24,0},{28,60},{1,9},{... | collective-permute-start | bytes 712712 | tf_op jit(solution)/shard_map/ppermute | solution.py:146
  136.6 8.0 %collective-permute-start.12 = (bf16[928,128]{1,0:T(8,128)(2,1)S(1)}, bf16[928,128]{1,0:T(8,128)(2,1)S(1)}, u32[]{:S(2)}, u32[]{:S(2)}) collective-permute-start(bf16[928,128]{1,0:T(8,128)(2,1)S(1)} %shard_map.128.own), channel_id=1, source_target_pairs={{0,96},{4,7},{8,104},{12,15},{16,112},{20,23},{24,120},{28,31},{1,... | collective-permute-start | bytes 712712 | tf_op jit(solution)/shard_map/ppermute | solution.py:148
  139.0 6.6 %collective-permute-start.11 = (bf16[928,128]{1,0:T(8,128)(2,1)S(1)}, bf16[928,128]{1,0:T(8,128)(2,1)S(1)}, u32[]{:S(2)}, u32[]{:S(2)}) collective-permute-start(bf16[928,128]{1,0:T(8,128)(2,1)S(1)} %shard_map.128.own), channel_id=1, source_target_pairs={{0,64},{4,6},{8,72},{12,14},{16,80},{20,22},{24,88},{28,30},{1,65}... | collective-permute-start | bytes 712712 | tf_op jit(solution)/shard_map/ppermute | solution.py:148
  139.3 9.0 %collective-permute-start.10 = (bf16[928,128]{1,0:T(8,128)(2,1)S(1)}, bf16[928,128]{1,0:T(8,128)(2,1)S(1)}, u32[]{:S(2)}, u32[]{:S(2)}) collective-permute-start(bf16[928,128]{1,0:T(8,128)(2,1)S(1)} %shard_map.128.own), channel_id=1, source_target_pairs={{0,32},{4,5},{8,40},{12,13},{16,48},{20,21},{24,56},{28,29},{1,33}... | collective-permute-start | bytes 712712 | tf_op jit(solution)/shard_map/ppermute | solution.py:148
  148.5 7.0 %collective-permute-start.13 = (bf16[928,512]{1,0:T(8,128)(2,1)S(1)}, bf16[928,512]{1,0:T(8,128)(2,1)S(1)}, u32[]{:S(2)}, u32[]{:S(2)}) collective-permute-start(bf16[928,512]{1,0:T(8,128)(2,1)S(1)} %shard_map.129.own), channel_id=1, source_target_pairs={{0,4},{4,0},{8,12},{12,8},{16,20},{20,16},{24,28},{28,24},{1,5},{5... | collective-permute-start | bytes 2850824 | tf_op jit(solution)/shard_map/ppermute | solution.py:152

commit v4 on v3

--- a/solution.py
+++ b/solution.py
@@ -88,13 +88,21 @@
     features = one.shape[0]
     classes = two.shape[0]
     columns = pl.ds(pl.multiple_of(at * half, half), half)
-    one[...] = part[:features, :].astype(jnp.float32)
-    first = pltpu.make_async_copy(one, one_far.at[:, columns], leaving.at[0])
-    first.start()
     two[...] = part[features:, :].astype(jnp.float32)[:classes]
-    second = pltpu.make_async_copy(two, two_far.at[:, columns], leaving.at[1])
-    second.start()
-    return first, second
+    copies = [pltpu.make_async_copy(two, two_far.at[:, columns], leaving.at[0])]
+    copies[0].start()
+    step = features // 4
+    for index in range(4):
+        rows = slice(index * step, (index + 1) * step)
+        one[rows, :] = part[rows, :].astype(jnp.float32)
+        lines = pl.ds(index * step, step)
+        copies.append(
+            pltpu.make_async_copy(
+                one.at[lines, :], one_far.at[lines, columns], leaving.at[index + 1]
+            )
+        )
+        copies[-1].start()
+    return copies
 
 
 def read_loss(part):
@@ -161,7 +169,7 @@
     scratch = [
         pltpu.VMEM((features, half), jnp.float32),
         pltpu.VMEM((classes, half), jnp.float32),
-        pltpu.SemaphoreType.DMA((2,)),
+        pltpu.SemaphoreType.DMA((5,)),
     ]
     params = pltpu.CompilerParams(vmem_limit_bytes=16 << 20)
     grad_one, grad_two = pl.pallas_call(
@@ -214,7 +222,7 @@
     requests[...] = total.astype(jnp.int32)
 
 
-def fetch_rows(wanted, table, far, narrow, wide, some, out, arrival, leaving):
+def fetch_rows(wanted_far, table, far, wanted, narrow, wide, some, out, listed, arrival, leaving):
     stored, width = table.shape
     step = stored // arrival.shape[0]
 
@@ -222,6 +230,8 @@
         rows = pl.ds(block * step, step)
         return pltpu.make_async_copy(table.at[rows, :], narrow.at[rows, :], arrival.at[block])
 
+    listing = pltpu.make_async_copy(wanted_far, wanted, listed)
+    listing.start()
     for block in range(arrival.shape[0]):
         load(block).start()
     for block in range(arrival.shape[0]):
@@ -230,6 +240,7 @@
             rows = slice(start, start + 128)
             wide[rows, :] = narrow[rows, :].astype(jnp.float32)
 
+    listing.wait()
     devices, capacity = wanted.shape
     owners = some.shape[0] // capacity
 
@@ -317,30 +328,41 @@
     def load(index, far, near):
         return pltpu.make_async_copy(far, near, arrival.at[index])
 
-    get_arrived = load(0, arrived_far, arrived)
-    get_one = load(1, one_far, layer_one)
-    get_dense = load(2, dense_far, dense)
-    get_two = load(3, two_far, layer_two)
-    get_labels = load(4, labels_far, labels)
-    get_turned = load(5, turned_far, turned)
+    part = arrived.shape[0] // SIDE
+    get_arrived = [
+        load(at, arrived_far.at[pl.ds(at * part, part), :], arrived.at[pl.ds(at * part, part), :])
+        for at in range(SIDE)
+    ]
+    get_one = load(4, one_far, layer_one)
+    get_dense = load(5, dense_far, dense)
+    get_two = load(6, two_far, layer_two)
+    get_labels = load(7, labels_far, labels)
+    get_turned = load(8, turned_far, turned)
     get_moved = [
-        load(6 + at, moved_far.at[pl.ds(start, step), :], moved.at[pl.ds(start, step), :])
+        load(9 + at, moved_far.at[pl.ds(start, step), :], moved.at[pl.ds(start, step), :])
         for at, start in enumerate(tiles)
     ]
-    get_arrived.start()
     get_moved[0].start()
+    for copy in get_arrived:
+        copy.start()
     get_one.start()
-    get_arrived.wait()
     get_moved[0].wait()
-    for copy in get_moved[1:]:
-        copy.start()
     for at, start in enumerate(tiles):
         rows = slice(start, start + step)
         if at > 0:
             get_moved[at].wait()
-        mixed = jnp.dot(moved[rows, :], arrived[...], preferred_element_type=jnp.float32).astype(
-            jnp.bfloat16
-        )
+            mixed = jnp.dot(moved[rows, :], arrived[...], preferred_element_type=jnp.float32)
+        else:
+            mixed = 0.0
+            for index, copy in enumerate(get_arrived):
+                copy.wait()
+                slots = slice(index * part, (index + 1) * part)
+                mixed += jnp.dot(
+                    moved[rows, slots], arrived[slots, :], preferred_element_type=jnp.float32
+                )
+            for copy in get_moved[1:]:
+                copy.start()
+        mixed = mixed.astype(jnp.bfloat16)
         mixed_turned[:, rows] = mixed.T
         if at == 0:
             get_one.wait()
@@ -452,13 +474,15 @@
     found = pl.pallas_call(
         fetch_rows,
         out_shape=jax.ShapeDtypeStruct((slots, width), bf),
-        in_specs=[smem, anywhere],
+        in_specs=[anywhere, anywhere],
         out_specs=anywhere,
         scratch_shapes=[
+            pltpu.SMEM(wanted.shape, jnp.int32),
             pltpu.VMEM(features.shape, bf),
             pltpu.VMEM(features.shape, jnp.float32),
             pltpu.VMEM((64, width), jnp.float32),
             pltpu.VMEM((slots, width), bf),
+            pltpu.SemaphoreType.DMA,
             pltpu.SemaphoreType.DMA((8,)),
             pltpu.SemaphoreType.DMA((slots // 64,)),
         ],
@@ -505,7 +529,7 @@
             pltpu.VMEM((nodes, hidden), bf),
             pltpu.VMEM((nodes, 256), bf),
             pltpu.VMEM((256, nodes), bf),
-            pltpu.SemaphoreType.DMA((10,)),
+            pltpu.SemaphoreType.DMA((13,)),
             pltpu.SemaphoreType.DMA((2,)),
         ],
         compiler_params=pltpu.CompilerParams(vmem_limit_bytes=56 << 20),

time: 158 us -> 156 us (0.987)
  Pallas kernels: 47.6 us -> 44.2 us
    pallas_call x1, Pallas kernels: 10.6 us -> 8.92 us  [on_device(): pl.pallas_call(fetch_rows, out_shape=jax.ShapeDtypeStruct((slots, width),...]
where the time goes in v4:
time: 156 us; the launch traced here: 155 us
  waiting for transfers between devices  60.2 us (39%)
  Pallas kernels  44.2 us (28%)
  blocking collectives  21.9 us (14%)
  starting transfers between devices  19.7 us (13%)
  local copies, waits for them, and re-layouts  7.82 us (5%)
  between operations  1.6 us (1%)
    all_to_all x1, waiting for transfers between devices, on_device(): lax.all_to_all(found, AXES, split_axis=0, concat_axis=0, tiled=True)  25.6 us
    all_to_all x1, blocking collectives, on_device(): lax.all_to_all(requests, AXES, split_axis=0, concat_axis=0, tiled=True)  21.9 us
    pallas_call x1, Pallas kernels, on_device(): pl.pallas_call(partial(train, classes=classes), out_shape=[jax.ShapeDtype...  19.7 us
    ppermute x6, waiting for transfers between devices, sum_over_devices(): got = [lax.ppermute(total, AXES, shift_pairs(axes, k)) for k in (1, 2, 3)]  15.8 us
    pallas_call x1, Pallas kernels, on_device(): call(build_spread, [jax.ShapeDtypeStruct((nodes, nodes), bf), jax.ShapeDt...  8.97 us
    pallas_call x1, Pallas kernels, on_device(): pl.pallas_call(fetch_rows, out_shape=jax.ShapeDtypeStruct((slots, width),...  8.92 us
    ppermute x3, waiting for transfers between devices, sum_over_devices(): got = [lax.ppermute(total, AXES, shift_pairs(FIRST, k)) for k in (1, 2, 3)]  8.61 us
    ppermute x3, waiting for transfers between devices, sum_over_devices(): lax.ppermute(part, AXES, shift_pairs(FIRST, k + 1))  6.8 us
  transfers between devices with their start and end apart: 15, of which 14 were waited for; matrix products, arithmetic and copies ran while one was open for 1% of the time, Pallas kernels for 7%

profile of v4, /device:TPU:1, one launch (start us, length us, event | category | flops | bytes accessed | tf_op | source)
XLA Modules:
  0.0 155.5 jit_solution(12982200451774849586)
XLA Ops:
  0.6 1.8 %shard_map.121 = (s32[128,16]{1,0:T(8,128)}, s32[1,1024]{1,0:T(1,128)}) custom-call(s32[1,1024]{1,0:T(1,128)} %bitcast.20, s32[1,1024]{1,0:T(1,128)} %bitcast.21), custom_call_target="tpu_custom_call" | custom-call | tf_op jit(solution)/shard_map/pallas_call | solution.py:460
  2.5 21.9 %all_to_all.22 = s32[128,1,16]{2,1,0:T(1,128)} all-to-all(s32[128,1,16]{2,1,0:T(1,128)} %bitcast.18), channel_id=1, replica_groups=mesh['store'=32,'batch'=4] {'store','batch'}, dimensions={0} | all-to-all | bytes 16384 | tf_op jit(solution)/shard_map/all_to_all | solution.py:470
  24.3 8.9 %shard_map.122 = bf16[2048,768]{1,0:T(8,128)(2,1)} custom-call(s32[128,16]{1,0:T(8,128)} %bitcast.17, bf16[4096,768]{1,0:T(8,128)(2,1)} %table.1), custom_call_target="tpu_custom_call" | custom-call | tf_op jit(solution)/shard_map/pallas_call | solution.py:474
  33.3 0.0 copy-start.9
  33.3 0.0 copy-start.8
  33.3 0.0 copy-start.1
  33.3 0.0 copy-start.2
  33.3 0.0 copy-start.3
  33.3 0.0 copy-start.4
  33.4 4.8 %all-to-all-start.1 = ((bf16[128,16,768]{2,1,0:T(8,128)(2,1)}), bf16[128,16,768]{2,1,0:T(8,128)(2,1)}, u32[]{:S(2)}, u32[]{:S(2)}) async-start(bf16[128,16,768]{2,1,0:T(8,128)(2,1)} %bitcast.14), calls=%async_computation.1 | async-start | bytes 6291456 | tf_op jit(solution)/shard_map/all_to_all | solution.py:491
  38.8 0.0 copy-done.9
  38.8 1.1 copy.17.labels_far
  39.9 0.0 copy-done.8
  39.9 0.8 pad.4.two_far
  40.8 0.0 copy-done.1
  40.8 0.0 copy-done.2
  40.8 0.0 copy-done.3
  40.8 0.0 copy-done.4
  40.8 9.0 %shard_map.123 = (bf16[1024,1024]{1,0:T(8,128)(2,1)S(1)}, bf16[1024,1024]{1,0:T(8,128)(2,1)S(1)}, bf16[1024,2048]{1,0:T(8,128)(2,1)S(1)}) custom-call(s32[48]{0:T(128)S(1)} %copy-done.3, s32[48]{0:T(128)S(1)} %copy-done.4, s32[1]{0:T(128)S(6)} %copy.20.count, bf16[48,128,128]{2,1,0:T(8,128)(2,1)S(1)} %copy-done.1, s32[1,1024]{1,0:T(1,128)S(1)} %copy-done.2), custom_call_target="tpu_custom_call" | custom-call | flops 4294967296 | bytes 12582912 | tf_op jit(solution)/shard_map/pallas_call | solution.py:492
  49.8 0.0 copy-start.5
  49.8 2.0 %copy-done.5 = bf16[1024,2048]{1,0:T(8,128)(2,1)} copy-done((bf16[1024,2048]{1,0:T(8,128)(2,1)}, bf16[1024,2048]{1,0:T(8,128)(2,1)S(1)}, u32[]{:S(2)}) %copy-start.5) | copy-done | bytes 4194328
  51.7 0.0 copy-start.6
  51.7 1.4 copy-done.6
  53.1 0.0 copy-start.7
  53.1 1.3 copy-done.7
  54.4 25.6 %all-to-all-done.1 = bf16[128,16,768]{2,1,0:T(8,128)(2,1)} async-done(((bf16[128,16,768]{2,1,0:T(8,128)(2,1)}), bf16[128,16,768]{2,1,0:T(8,128)(2,1)}, u32[]{:S(2)}, u32[]{:S(2)}) %all-to-all-start.1) | async-done | bytes 3145760 | tf_op jit(solution)/shard_map/all_to_all | solution.py:491
  80.1 19.7 %shard_map.124 = (bf16[928,512]{1,0:T(8,128)(2,1)}, bf16[928,512]{1,0:T(8,128)(2,1)}) custom-call(s32[1]{0:T(128)} %bitcast.core, bf16[2048,768]{1,0:T(8,128)(2,1)} %bitcast.8.arrived_far, bf16[1024,2048]{1,0:T(8,128)(2,1)} %copy-done.5, bf16[1024,1024]{1,0:T(8,128)(2,1)} %copy-done.6, bf16[1024,1024]{1,0:T(8,128)(2,1)} %copy-done.7, ...), custom_call_target="tpu_custom_call" | custom-call | flops 12884901888 | bytes 16777216 | tf_op jit(solution)/shard_map/pallas_call | solution.py:508
  99.8 0.3 collective-permute-start
  100.1 2.5 %collective-permute-done.arrived = bf16[928,512]{1,0:T(8,128)(2,1)S(1)} collective-permute-done((bf16[928,512]{1,0:T(8,128)(2,1)}, bf16[928,512]{1,0:T(8,128)(2,1)S(1)}, u32[]{:S(2)}, u32[]{:S(2)}) %collective-permute-start) | collective-permute-done | bytes 950304 | tf_op jit(solution)/shard_map/ppermute | solution.py:149
  102.6 0.0 copy-start
  102.6 1.2 copy-done
  103.8 0.5 shard_map.125
  104.4 0.4 collective-permute-start.1
  104.8 2.0 %collective-permute-start.2 = (bf16[928,128]{1,0:T(8,128)(2,1)S(1)}, bf16[928,128]{1,0:T(8,128)(2,1)S(1)}, u32[]{:S(2)}, u32[]{:S(2)}) collective-permute-start(bf16[928,128]{1,0:T(8,128)(2,1)S(1)} %get-tuple-element.28), channel_id=1, source_target_pairs={{0,64},{4,6},{8,72},{12,14},{16,80},{20,22},{24,88},{28,30},{1,65}... | collective-permute-start | bytes 712712 | tf_op jit(solution)/shard_map/ppermute | solution.py:151
  106.8 0.5 collective-permute-start.3
  107.3 6.2 %collective-permute-done.1.one = bf16[928,128]{1,0:T(8,128)(2,1)S(1)} collective-permute-done((bf16[928,128]{1,0:T(8,128)(2,1)S(1)}, bf16[928,128]{1,0:T(8,128)(2,1)S(1)}, u32[]{:S(2)}, u32[]{:S(2)}) %collective-permute-start.1) | collective-permute-done | bytes 237600 | tf_op jit(solution)/shard_map/ppermute | solution.py:151
  113.5 0.0 collective-permute-done.2.two
  113.5 0.6 collective-permute-done.3.three
  114.1 0.3 shard_map.126.own
  114.4 0.1 collective-permute-start.6
  114.5 1.6 %collective-permute-start.5 = (bf16[928,128]{1,0:T(8,128)(2,1)S(1)}, bf16[928,128]{1,0:T(8,128)(2,1)S(1)}, u32[]{:S(2)}, u32[]{:S(2)}) collective-permute-start(bf16[928,128]{1,0:T(8,128)(2,1)S(1)} %shard_map.126.own), channel_id=1, source_target_pairs={{0,2},{4,20},{8,10},{12,28},{16,18},{20,4},{24,26},{28,12},{1,3},{... | collective-permute-start | bytes 712712 | tf_op jit(solution)/shard_map/ppermute | solution.py:154
  116.0 0.0 collective-permute-start.4
  116.0 3.6 %collective-permute-done.6.three = bf16[928,128]{1,0:T(8,128)(2,1)S(1)} collective-permute-done((bf16[928,128]{1,0:T(8,128)(2,1)S(1)}, bf16[928,128]{1,0:T(8,128)(2,1)S(1)}, u32[]{:S(2)}, u32[]{:S(2)}) %collective-permute-start.6) | collective-permute-done | bytes 237600 | tf_op jit(solution)/shard_map/ppermute | solution.py:154
  119.6 1.4 collective-permute-done.5.two
  121.0 2.7 %collective-permute-done.4.one = bf16[928,128]{1,0:T(8,128)(2,1)S(1)} collective-permute-done((bf16[928,128]{1,0:T(8,128)(2,1)S(1)}, bf16[928,128]{1,0:T(8,128)(2,1)S(1)}, u32[]{:S(2)}, u32[]{:S(2)}) %collective-permute-start.4) | collective-permute-done | bytes 237600 | tf_op jit(solution)/shard_map/ppermute | solution.py:154
  123.8 0.3 shard_map.127.own
  124.1 0.9 collective-permute-start.9
  125.0 1.2 collective-permute-start.8
  126.2 0.0 collective-permute-start.7
  126.2 2.9 %collective-permute-done.9.three = bf16[928,128]{1,0:T(8,128)(2,1)S(1)} collective-permute-done((bf16[928,128]{1,0:T(8,128)(2,1)S(1)}, bf16[928,128]{1,0:T(8,128)(2,1)S(1)}, u32[]{:S(2)}, u32[]{:S(2)}) %collective-permute-start.9) | collective-permute-done | bytes 237600 | tf_op jit(solution)/shard_map/ppermute | solution.py:154
  129.0 2.5 %collective-permute-done.8.two = bf16[928,128]{1,0:T(8,128)(2,1)S(1)} collective-permute-done((bf16[928,128]{1,0:T(8,128)(2,1)S(1)}, bf16[928,128]{1,0:T(8,128)(2,1)S(1)}, u32[]{:S(2)}, u32[]{:S(2)}) %collective-permute-start.8) | collective-permute-done | bytes 237600 | tf_op jit(solution)/shard_map/ppermute | solution.py:154
  131.5 2.7 %collective-permute-done.7.one = bf16[928,128]{1,0:T(8,128)(2,1)S(1)} collective-permute-done((bf16[928,128]{1,0:T(8,128)(2,1)S(1)}, bf16[928,128]{1,0:T(8,128)(2,1)S(1)}, u32[]{:S(2)}, u32[]{:S(2)}) %collective-permute-start.7) | collective-permute-done | bytes 237600 | tf_op jit(solution)/shard_map/ppermute | solution.py:154
  134.3 0.3 shard_map.128.own
  134.5 2.4 %collective-permute-start.12 = (bf16[928,128]{1,0:T(8,128)(2,1)S(1)}, bf16[928,128]{1,0:T(8,128)(2,1)S(1)}, u32[]{:S(2)}, u32[]{:S(2)}) collective-permute-start(bf16[928,128]{1,0:T(8,128)(2,1)S(1)} %shard_map.128.own), channel_id=1, source_target_pairs={{0,96},{4,7},{8,104},{12,15},{16,112},{20,23},{24,120},{28,31},{1,... | collective-permute-start | bytes 712712 | tf_op jit(solution)/shard_map/ppermute | solution.py:156
  136.9 0.3 collective-permute-start.11
  137.2 0.4 collective-permute-start.10
  137.6 4.9 %collective-permute-done.12.three = bf16[928,128]{1,0:T(8,128)(2,1)S(1)} collective-permute-done((bf16[928,128]{1,0:T(8,128)(2,1)S(1)}, bf16[928,128]{1,0:T(8,128)(2,1)S(1)}, u32[]{:S(2)}, u32[]{:S(2)}) %collective-permute-start.12) | collective-permute-done | bytes 237600 | tf_op jit(solution)/shard_map/ppermute | solution.py:156
  142.5 1.0 collective-permute-done.11.two
  143.5 2.7 %collective-permute-done.10.one = bf16[928,128]{1,0:T(8,128)(2,1)S(1)} collective-permute-done((bf16[928,128]{1,0:T(8,128)(2,1)S(1)}, bf16[928,128]{1,0:T(8,128)(2,1)S(1)}, u32[]{:S(2)}, u32[]{:S(2)}) %collective-permute-start.10) | collective-permute-done | bytes 237600 | tf_op jit(solution)/shard_map/ppermute | solution.py:156
  146.2 0.3 shard_map.129.own
  146.4 4.9 %collective-permute-start.13 = (bf16[928,512]{1,0:T(8,128)(2,1)S(1)}, bf16[928,512]{1,0:T(8,128)(2,1)S(1)}, u32[]{:S(2)}, u32[]{:S(2)}) collective-permute-start(bf16[928,512]{1,0:T(8,128)(2,1)S(1)} %shard_map.129.own), channel_id=1, source_target_pairs={{0,4},{4,0},{8,12},{12,8},{16,20},{20,16},{24,28},{28,24},{1,5},{5... | collective-permute-start | bytes 2850824 | tf_op jit(solution)/shard_map/ppermute | solution.py:160
  151.3 1.3 shard_map.130
  152.6 0.8 collective-permute-done.13.other
  153.5 1.8 %shard_map.131 = (f32[768,1024]{1,0:T(8,128)}, f32[153,1024]{1,0:T(8,128)}, f32[1,1]{1,0:T(1,128)}) custom-call(s32[1]{0:T(128)} %bitcast.core, bf16[928,512]{1,0:T(8,128)(2,1)S(1)} %shard_map.129.own, bf16[928,512]{1,0:T(8,128)(2,1)S(1)} %collective-permute-done.13.other, ...), custom_call_target="tpu_custom_call", output_to_operand_aliasing={{0}: (3, {}), {1}: (4, {})} | custom-call | tf_op jit(solution)/shard_map/pallas_call | solution.py:183
Async XLA Ops:
  33.3 5.6 %copy-start.9 = (s32[1024]{0:T(1024)S(1)}, s32[1024]{0:T(1024)}, u32[]{:S(2)}) copy-start(s32[1024]{0:T(1024)} %param.17) | copy-start | bytes 12292
  33.3 6.6 %copy-start.8 = (bf16[1024,153]{0,1:T(8,128)(2,1)S(1)}, bf16[1024,153]{0,1:T(8,128)(2,1)}, u32[]{:S(2)}) copy-start(bf16[1024,153]{0,1:T(8,128)(2,1)} %param.19) | copy-start | bytes 940036
  33.3 7.5 %copy-start.1 = (bf16[48,128,128]{2,1,0:T(8,128)(2,1)S(1)}, bf16[48,128,128]{2,1,0:T(8,128)(2,1)}, u32[]{:S(2)}) copy-start(bf16[48,128,128]{2,1,0:T(8,128)(2,1)} %tiles.1) | copy-start | bytes 4718596
  33.3 7.5 %copy-start.2 = (s32[1,1024]{1,0:T(1,128)S(1)}, s32[1,1024]{1,0:T(1,128)}, u32[]{:S(2)}) copy-start(s32[1,1024]{1,0:T(1,128)} %get-tuple-element.20.position) | copy-start | bytes 12292
  33.3 7.5 %copy-start.3 = (s32[48]{0:T(128)S(1)}, s32[48]{0:T(128)}, u32[]{:S(2)}) copy-start(s32[48]{0:T(128)} %row.1) | copy-start | bytes 580
  33.3 7.5 %copy-start.4 = (s32[48]{0:T(128)S(1)}, s32[48]{0:T(128)}, u32[]{:S(2)}) copy-start(s32[48]{0:T(128)} %column.1) | copy-start | bytes 580
  33.4 46.7 %all-to-all-start.1 = ((bf16[128,16,768]{2,1,0:T(8,128)(2,1)}), bf16[128,16,768]{2,1,0:T(8,128)(2,1)}, u32[]{:S(2)}, u32[]{:S(2)}) async-start(bf16[128,16,768]{2,1,0:T(8,128)(2,1)} %bitcast.14), calls=%async_computation.1 | async-start | bytes 6291456 | tf_op jit(solution)/shard_map/all_to_all | solution.py:491
  49.8 2.0 %copy-start.5 = (bf16[1024,2048]{1,0:T(8,128)(2,1)}, bf16[1024,2048]{1,0:T(8,128)(2,1)S(1)}, u32[]{:S(2)}) copy-start(bf16[1024,2048]{1,0:T(8,128)(2,1)S(1)} %get-tuple-element.21.moved_far) | copy-start | bytes 12582916
  51.7 1.4 copy-start.6
  53.1 1.3 copy-start.7
  99.8 2.8 %collective-permute-start = (bf16[928,512]{1,0:T(8,128)(2,1)}, bf16[928,512]{1,0:T(8,128)(2,1)S(1)}, u32[]{:S(2)}, u32[]{:S(2)}) collective-permute-start(bf16[928,512]{1,0:T(8,128)(2,1)} %get-tuple-element.25), channel_id=1, source_target_pairs={{0,4},{4,0},{8,12},{12,8},{16,20},{20,16},{24,28},{28,24},{1,5},{5... | collective-permute-start | bytes 2850824 | tf_op jit(solution)/shard_map/ppermute | solution.py:149
  102.6 1.2 copy-start
  104.4 9.1 %collective-permute-start.1 = (bf16[928,128]{1,0:T(8,128)(2,1)S(1)}, bf16[928,128]{1,0:T(8,128)(2,1)S(1)}, u32[]{:S(2)}, u32[]{:S(2)}) collective-permute-start(bf16[928,128]{1,0:T(8,128)(2,1)S(1)} %get-tuple-element.27), channel_id=1, source_target_pairs={{0,32},{4,5},{8,40},{12,13},{16,48},{20,21},{24,56},{28,29},{1,33}... | collective-permute-start | bytes 712712 | tf_op jit(solution)/shard_map/ppermute | solution.py:151
  104.8 8.7 %collective-permute-start.2 = (bf16[928,128]{1,0:T(8,128)(2,1)S(1)}, bf16[928,128]{1,0:T(8,128)(2,1)S(1)}, u32[]{:S(2)}, u32[]{:S(2)}) collective-permute-start(bf16[928,128]{1,0:T(8,128)(2,1)S(1)} %get-tuple-element.28), channel_id=1, source_target_pairs={{0,64},{4,6},{8,72},{12,14},{16,80},{20,22},{24,88},{28,30},{1,65}... | collective-permute-start | bytes 712712 | tf_op jit(solution)/shard_map/ppermute | solution.py:151
  106.8 7.3 %collective-permute-start.3 = (bf16[928,128]{1,0:T(8,128)(2,1)S(1)}, bf16[928,128]{1,0:T(8,128)(2,1)S(1)}, u32[]{:S(2)}, u32[]{:S(2)}) collective-permute-start(bf16[928,128]{1,0:T(8,128)(2,1)S(1)} %get-tuple-element.29), channel_id=1, source_target_pairs={{0,96},{4,7},{8,104},{12,15},{16,112},{20,23},{24,120},{28,31},{1,... | collective-permute-start | bytes 712712 | tf_op jit(solution)/shard_map/ppermute | solution.py:151
  114.4 5.3 %collective-permute-start.6 = (bf16[928,128]{1,0:T(8,128)(2,1)S(1)}, bf16[928,128]{1,0:T(8,128)(2,1)S(1)}, u32[]{:S(2)}, u32[]{:S(2)}) collective-permute-start(bf16[928,128]{1,0:T(8,128)(2,1)S(1)} %shard_map.126.own), channel_id=1, source_target_pairs={{0,3},{4,28},{8,11},{12,4},{16,19},{20,12},{24,27},{28,20},{1,0},{... | collective-permute-start | bytes 712712 | tf_op jit(solution)/shard_map/ppermute | solution.py:154
  114.5 6.6 %collective-permute-start.5 = (bf16[928,128]{1,0:T(8,128)(2,1)S(1)}, bf16[928,128]{1,0:T(8,128)(2,1)S(1)}, u32[]{:S(2)}, u32[]{:S(2)}) collective-permute-start(bf16[928,128]{1,0:T(8,128)(2,1)S(1)} %shard_map.126.own), channel_id=1, source_target_pairs={{0,2},{4,20},{8,10},{12,28},{16,18},{20,4},{24,26},{28,12},{1,3},{... | collective-permute-start | bytes 712712 | tf_op jit(solution)/shard_map/ppermute | solution.py:154
  116.0 7.7 %collective-permute-start.4 = (bf16[928,128]{1,0:T(8,128)(2,1)S(1)}, bf16[928,128]{1,0:T(8,128)(2,1)S(1)}, u32[]{:S(2)}, u32[]{:S(2)}) collective-permute-start(bf16[928,128]{1,0:T(8,128)(2,1)S(1)} %shard_map.126.own), channel_id=1, source_target_pairs={{0,1},{4,12},{8,9},{12,20},{16,17},{20,28},{24,25},{28,4},{1,2},{5... | collective-permute-start | bytes 712712 | tf_op jit(solution)/shard_map/ppermute | solution.py:154
  124.1 5.0 %collective-permute-start.9 = (bf16[928,128]{1,0:T(8,128)(2,1)S(1)}, bf16[928,128]{1,0:T(8,128)(2,1)S(1)}, u32[]{:S(2)}, u32[]{:S(2)}) collective-permute-start(bf16[928,128]{1,0:T(8,128)(2,1)S(1)} %shard_map.127.own), channel_id=1, source_target_pairs={{0,24},{4,100},{8,0},{12,108},{16,8},{20,116},{24,16},{28,124},{1,... | collective-permute-start | bytes 712712 | tf_op jit(solution)/shard_map/ppermute | solution.py:154
  125.0 6.6 %collective-permute-start.8 = (bf16[928,128]{1,0:T(8,128)(2,1)S(1)}, bf16[928,128]{1,0:T(8,128)(2,1)S(1)}, u32[]{:S(2)}, u32[]{:S(2)}) collective-permute-start(bf16[928,128]{1,0:T(8,128)(2,1)S(1)} %shard_map.127.own), channel_id=1, source_target_pairs={{0,16},{4,68},{8,24},{12,76},{16,0},{20,84},{24,8},{28,92},{1,17},... | collective-permute-start | bytes 712712 | tf_op jit(solution)/shard_map/ppermute | solution.py:154
  126.2 8.1 %collective-permute-start.7 = (bf16[928,128]{1,0:T(8,128)(2,1)S(1)}, bf16[928,128]{1,0:T(8,128)(2,1)S(1)}, u32[]{:S(2)}, u32[]{:S(2)}) collective-permute-start(bf16[928,128]{1,0:T(8,128)(2,1)S(1)} %shard_map.127.own), channel_id=1, source_target_pairs={{0,8},{4,36},{8,16},{12,44},{16,24},{20,52},{24,0},{28,60},{1,9},{... | collective-permute-start | bytes 712712 | tf_op jit(solution)/shard_map/ppermute | solution.py:154
  134.5 8.0 %collective-permute-start.12 = (bf16[928,128]{1,0:T(8,128)(2,1)S(1)}, bf16[928,128]{1,0:T(8,128)(2,1)S(1)}, u32[]{:S(2)}, u32[]{:S(2)}) collective-permute-start(bf16[928,128]{1,0:T(8,128)(2,1)S(1)} %shard_map.128.own), channel_id=1, source_target_pairs={{0,96},{4,7},{8,104},{12,15},{16,112},{20,23},{24,120},{28,31},{1,... | collective-permute-start | bytes 712712 | tf_op jit(solution)/shard_map/ppermute | solution.py:156
  136.9 6.6 %collective-permute-start.11 = (bf16[928,128]{1,0:T(8,128)(2,1)S(1)}, bf16[928,128]{1,0:T(8,128)(2,1)S(1)}, u32[]{:S(2)}, u32[]{:S(2)}) collective-permute-start(bf16[928,128]{1,0:T(8,128)(2,1)S(1)} %shard_map.128.own), channel_id=1, source_target_pairs={{0,64},{4,6},{8,72},{12,14},{16,80},{20,22},{24,88},{28,30},{1,65}... | collective-permute-start | bytes 712712 | tf_op jit(solution)/shard_map/ppermute | solution.py:156
  137.2 9.0 %collective-permute-start.10 = (bf16[928,128]{1,0:T(8,128)(2,1)S(1)}, bf16[928,128]{1,0:T(8,128)(2,1)S(1)}, u32[]{:S(2)}, u32[]{:S(2)}) collective-permute-start(bf16[928,128]{1,0:T(8,128)(2,1)S(1)} %shard_map.128.own), channel_id=1, source_target_pairs={{0,32},{4,5},{8,40},{12,13},{16,48},{20,21},{24,56},{28,29},{1,33}... | collective-permute-start | bytes 712712 | tf_op jit(solution)/shard_map/ppermute | solution.py:156
  146.4 7.0 %collective-permute-start.13 = (bf16[928,512]{1,0:T(8,128)(2,1)S(1)}, bf16[928,512]{1,0:T(8,128)(2,1)S(1)}, u32[]{:S(2)}, u32[]{:S(2)}) collective-permute-start(bf16[928,512]{1,0:T(8,128)(2,1)S(1)} %shard_map.129.own), channel_id=1, source_target_pairs={{0,4},{4,0},{8,12},{12,8},{16,20},{20,16},{24,28},{28,24},{1,5},{5... | collective-permute-start | bytes 2850824 | tf_op jit(solution)/shard_map/ppermute | solution.py:160

commit v5 on v4

--- a/solution.py
+++ b/solution.py
@@ -62,11 +62,24 @@
     out[ROWS - 16 :, columns] = last.astype(jnp.bfloat16)
 
 
-def first_add(place, own, arrived, keep, one, two, three):
-    for offset, out in ((1, one), (2, two), (3, three), (0, keep)):
+def pick_blocks(place, far, near, arrival):
+    copies = []
+    for index, offset in enumerate((1, 2, 3, 0)):
         block = lax.rem(place[0] + offset, SIDE)
         columns = pl.ds(pl.multiple_of(block * WIDTH, WIDTH), WIDTH)
-        total = own[:, columns].astype(jnp.float32) + arrived[:, columns].astype(jnp.float32)
+        copies.append(
+            pltpu.make_async_copy(far.at[:, columns], near.at[index], arrival.at[index])
+        )
+        copies[-1].start()
+    for copy in copies:
+        copy.wait()
+
+
+def first_add(place, own, arrived, keep, one, two, three):
+    for index, (offset, out) in enumerate(((1, one), (2, two), (3, three), (0, keep))):
+        block = lax.rem(place[0] + offset, SIDE)
+        columns = pl.ds(pl.multiple_of(block * WIDTH, WIDTH), WIDTH)
+        total = own[index].astype(jnp.float32) + arrived[:, columns].astype(jnp.float32)
         store_total(out, slice(None), total)
 
 
@@ -147,7 +160,15 @@
     bf = jnp.bfloat16
     block = jax.ShapeDtypeStruct((ROWS, WIDTH), bf)
     arrived = lax.ppermute(sent, AXES, swap_pairs())
-    keep, *parts = call(first_add, [block] * 4, 1, 2)(place, own, arrived)
+    picked = pl.pallas_call(
+        pick_blocks,
+        out_shape=jax.ShapeDtypeStruct((SIDE, ROWS, WIDTH), bf),
+        in_specs=[pl.BlockSpec(memory_space=pltpu.SMEM), pl.BlockSpec(memory_space=pl.ANY)],
+        out_specs=pl.BlockSpec(memory_space=pltpu.VMEM),
+        scratch_shapes=[pltpu.SemaphoreType.DMA((SIDE,))],
+        compiler_params=pltpu.CompilerParams(vmem_limit_bytes=16 << 20),
+    )(place, own)
+    keep, *parts = call(first_add, [block] * 4, 1, 2)(place, picked, arrived)
     got = [lax.ppermute(part, AXES, shift_pairs(FIRST, k + 1)) for k, part in enumerate(parts)]
     total = call(four_add, block, 0, 4)(keep, *got)
     for axes in (SECOND, THIRD):

time: 156 us -> 154 us (0.987)
  no operation moved by 1% of the time
where the time goes in v5:
time: 154 us
  waiting for transfers between devices  58.7 us (38%)
  Pallas kernels  44.5 us (29%)
  blocking collectives  21.9 us (14%)
  starting transfers between devices  19.7 us (13%)
  local copies, waits for them, and re-layouts  7.82 us (5%)
  between operations  1.61 us (1%)
    all_to_all x1, waiting for transfers between devices, on_device(): lax.all_to_all(found, AXES, split_axis=0, concat_axis=0, tiled=True)  25.5 us
    all_to_all x1, blocking collectives, on_device(): lax.all_to_all(requests, AXES, split_axis=0, concat_axis=0, tiled=True)  21.9 us
    pallas_call x1, Pallas kernels, on_device(): pl.pallas_call(partial(train, classes=classes), out_shape=[jax.ShapeDtype...  19.7 us
    ppermute x6, waiting for transfers between devices, sum_over_devices(): got = [lax.ppermute(total, AXES, shift_pairs(axes, k)) for k in (1, 2, 3)]  15.8 us
    pallas_call x1, Pallas kernels, on_device(): call(build_spread, [jax.ShapeDtypeStruct((nodes, nodes), bf), jax.ShapeDt...  9.11 us
    pallas_call x1, Pallas kernels, on_device(): pl.pallas_call(fetch_rows, out_shape=jax.ShapeDtypeStruct((slots, width),...  8.92 us
    ppermute x3, waiting for transfers between devices, sum_over_devices(): got = [lax.ppermute(total, AXES, shift_pairs(FIRST, k)) for k in (1, 2, 3)]  8.61 us
    ppermute x3, waiting for transfers between devices, sum_over_devices(): lax.ppermute(part, AXES, shift_pairs(FIRST, k + 1))  6.8 us
  transfers between devices with their start and end apart: 15, of which 14 were waited for; matrix products, arithmetic and copies ran while one was open for 1% of the time, Pallas kernels for 7%

profile of v5, /device:TPU:1, one launch (start us, length us, event | category | flops | bytes accessed | tf_op | source)
XLA Modules:
  0.0 154.2 jit_solution(14499803852165501448)
XLA Ops:
  0.6 1.8 %shard_map.121 = (s32[128,16]{1,0:T(8,128)}, s32[1,1024]{1,0:T(1,128)}) custom-call(s32[1,1024]{1,0:T(1,128)} %bitcast.20, s32[1,1024]{1,0:T(1,128)} %bitcast.21), custom_call_target="tpu_custom_call" | custom-call | tf_op jit(solution)/shard_map/pallas_call | solution.py:481
  2.5 21.9 %all_to_all.22 = s32[128,1,16]{2,1,0:T(1,128)} all-to-all(s32[128,1,16]{2,1,0:T(1,128)} %bitcast.18), channel_id=1, replica_groups=mesh['store'=32,'batch'=4] {'store','batch'}, dimensions={0} | all-to-all | bytes 16384 | tf_op jit(solution)/shard_map/all_to_all | solution.py:491
  24.3 8.9 %shard_map.122 = bf16[2048,768]{1,0:T(8,128)(2,1)} custom-call(s32[128,16]{1,0:T(8,128)} %bitcast.17, bf16[4096,768]{1,0:T(8,128)(2,1)} %table.1), custom_call_target="tpu_custom_call" | custom-call | tf_op jit(solution)/shard_map/pallas_call | solution.py:495
  33.3 0.0 copy-start.9
  33.3 0.0 copy-start.8
  33.3 0.0 copy-start.1
  33.3 0.0 copy-start.2
  33.3 0.0 copy-start.3
  33.3 0.0 copy-start.4
  33.4 4.8 %all-to-all-start.1 = ((bf16[128,16,768]{2,1,0:T(8,128)(2,1)}), bf16[128,16,768]{2,1,0:T(8,128)(2,1)}, u32[]{:S(2)}, u32[]{:S(2)}) async-start(bf16[128,16,768]{2,1,0:T(8,128)(2,1)} %bitcast.14), calls=%async_computation.1 | async-start | bytes 6291456 | tf_op jit(solution)/shard_map/all_to_all | solution.py:512
  38.8 0.0 copy-done.9
  38.8 1.1 copy.17.labels_far
  39.9 0.0 copy-done.8
  39.9 0.8 pad.4.two_far
  40.8 0.0 copy-done.1
  40.8 0.0 copy-done.2
  40.8 0.0 copy-done.3
  40.8 0.0 copy-done.4
  40.8 9.1 %shard_map.123 = (bf16[1024,1024]{1,0:T(8,128)(2,1)S(1)}, bf16[1024,1024]{1,0:T(8,128)(2,1)S(1)}, bf16[1024,2048]{1,0:T(8,128)(2,1)S(1)}) custom-call(s32[48]{0:T(128)S(1)} %copy-done.3, s32[48]{0:T(128)S(1)} %copy-done.4, s32[1]{0:T(128)S(6)} %copy.20.count, bf16[48,128,128]{2,1,0:T(8,128)(2,1)S(1)} %copy-done.1, s32[1,1024]{1,0:T(1,128)S(1)} %copy-done.2), custom_call_target="tpu_custom_call" | custom-call | flops 4294967296 | bytes 12582912 | tf_op jit(solution)/shard_map/pallas_call | solution.py:513
  49.9 0.0 copy-start.5
  49.9 2.0 %copy-done.5 = bf16[1024,2048]{1,0:T(8,128)(2,1)} copy-done((bf16[1024,2048]{1,0:T(8,128)(2,1)}, bf16[1024,2048]{1,0:T(8,128)(2,1)S(1)}, u32[]{:S(2)}) %copy-start.5) | copy-done | bytes 4194328
  51.9 0.0 copy-start.6
  51.9 1.4 copy-done.6
  53.3 0.0 copy-start.7
  53.3 1.3 copy-done.7
  54.6 25.5 %all-to-all-done.1 = bf16[128,16,768]{2,1,0:T(8,128)(2,1)} async-done(((bf16[128,16,768]{2,1,0:T(8,128)(2,1)}), bf16[128,16,768]{2,1,0:T(8,128)(2,1)}, u32[]{:S(2)}, u32[]{:S(2)}) %all-to-all-start.1) | async-done | bytes 3145760 | tf_op jit(solution)/shard_map/all_to_all | solution.py:512
  80.1 19.7 %shard_map.124 = (bf16[928,512]{1,0:T(8,128)(2,1)}, bf16[928,512]{1,0:T(8,128)(2,1)}) custom-call(s32[1]{0:T(128)} %bitcast.core, bf16[2048,768]{1,0:T(8,128)(2,1)} %bitcast.8.arrived_far, bf16[1024,2048]{1,0:T(8,128)(2,1)} %copy-done.5, bf16[1024,1024]{1,0:T(8,128)(2,1)} %copy-done.6, bf16[1024,1024]{1,0:T(8,128)(2,1)} %copy-done.7, ...), custom_call_target="tpu_custom_call" | custom-call | flops 12884901888 | bytes 16777216 | tf_op jit(solution)/shard_map/pallas_call | solution.py:529
  99.8 0.3 collective-permute-start
  100.1 1.2 copy-done
  101.3 0.2 shard_map.125.own
  101.6 1.1 collective-permute-done.arrived
  102.6 0.5 shard_map.126
  103.1 0.4 collective-permute-start.1
  103.5 2.0 %collective-permute-start.2 = (bf16[928,128]{1,0:T(8,128)(2,1)S(1)}, bf16[928,128]{1,0:T(8,128)(2,1)S(1)}, u32[]{:S(2)}, u32[]{:S(2)}) collective-permute-start(bf16[928,128]{1,0:T(8,128)(2,1)S(1)} %get-tuple-element.28), channel_id=1, source_target_pairs={{0,64},{4,6},{8,72},{12,14},{16,80},{20,22},{24,88},{28,30},{1,65}... | collective-permute-start | bytes 712712 | tf_op jit(solution)/shard_map/ppermute | solution.py:172
  105.5 0.5 collective-permute-start.3
  106.0 6.2 %collective-permute-done.1.one = bf16[928,128]{1,0:T(8,128)(2,1)S(1)} collective-permute-done((bf16[928,128]{1,0:T(8,128)(2,1)S(1)}, bf16[928,128]{1,0:T(8,128)(2,1)S(1)}, u32[]{:S(2)}, u32[]{:S(2)}) %collective-permute-start.1) | collective-permute-done | bytes 237600 | tf_op jit(solution)/shard_map/ppermute | solution.py:172
  112.2 0.0 collective-permute-done.2.two
  112.2 0.6 collective-permute-done.3.three
  112.8 0.3 shard_map.127.own
  113.1 0.1 collective-permute-start.6
  113.2 1.6 %collective-permute-start.5 = (bf16[928,128]{1,0:T(8,128)(2,1)S(1)}, bf16[928,128]{1,0:T(8,128)(2,1)S(1)}, u32[]{:S(2)}, u32[]{:S(2)}) collective-permute-start(bf16[928,128]{1,0:T(8,128)(2,1)S(1)} %shard_map.127.own), channel_id=1, source_target_pairs={{0,2},{4,20},{8,10},{12,28},{16,18},{20,4},{24,26},{28,12},{1,3},{... | collective-permute-start | bytes 712712 | tf_op jit(solution)/shard_map/ppermute | solution.py:175
  114.8 0.0 collective-permute-start.4
  114.8 3.6 %collective-permute-done.6.three = bf16[928,128]{1,0:T(8,128)(2,1)S(1)} collective-permute-done((bf16[928,128]{1,0:T(8,128)(2,1)S(1)}, bf16[928,128]{1,0:T(8,128)(2,1)S(1)}, u32[]{:S(2)}, u32[]{:S(2)}) %collective-permute-start.6) | collective-permute-done | bytes 237600 | tf_op jit(solution)/shard_map/ppermute | solution.py:175
  118.4 1.4 collective-permute-done.5.two
  119.8 2.7 %collective-permute-done.4.one = bf16[928,128]{1,0:T(8,128)(2,1)S(1)} collective-permute-done((bf16[928,128]{1,0:T(8,128)(2,1)S(1)}, bf16[928,128]{1,0:T(8,128)(2,1)S(1)}, u32[]{:S(2)}, u32[]{:S(2)}) %collective-permute-start.4) | collective-permute-done | bytes 237600 | tf_op jit(solution)/shard_map/ppermute | solution.py:175
  122.5 0.3 shard_map.128.own
  122.8 0.9 collective-permute-start.9
  123.7 1.2 collective-permute-start.8
  124.9 0.0 collective-permute-start.7
  124.9 2.9 %collective-permute-done.9.three = bf16[928,128]{1,0:T(8,128)(2,1)S(1)} collective-permute-done((bf16[928,128]{1,0:T(8,128)(2,1)S(1)}, bf16[928,128]{1,0:T(8,128)(2,1)S(1)}, u32[]{:S(2)}, u32[]{:S(2)}) %collective-permute-start.9) | collective-permute-done | bytes 237600 | tf_op jit(solution)/shard_map/ppermute | solution.py:175
  127.8 2.5 %collective-permute-done.8.two = bf16[928,128]{1,0:T(8,128)(2,1)S(1)} collective-permute-done((bf16[928,128]{1,0:T(8,128)(2,1)S(1)}, bf16[928,128]{1,0:T(8,128)(2,1)S(1)}, u32[]{:S(2)}, u32[]{:S(2)}) %collective-permute-start.8) | collective-permute-done | bytes 237600 | tf_op jit(solution)/shard_map/ppermute | solution.py:175
  130.3 2.7 %collective-permute-done.7.one = bf16[928,128]{1,0:T(8,128)(2,1)S(1)} collective-permute-done((bf16[928,128]{1,0:T(8,128)(2,1)S(1)}, bf16[928,128]{1,0:T(8,128)(2,1)S(1)}, u32[]{:S(2)}, u32[]{:S(2)}) %collective-permute-start.7) | collective-permute-done | bytes 237600 | tf_op jit(solution)/shard_map/ppermute | solution.py:175
  133.0 0.3 shard_map.129.own
  133.3 2.4 %collective-permute-start.12 = (bf16[928,128]{1,0:T(8,128)(2,1)S(1)}, bf16[928,128]{1,0:T(8,128)(2,1)S(1)}, u32[]{:S(2)}, u32[]{:S(2)}) collective-permute-start(bf16[928,128]{1,0:T(8,128)(2,1)S(1)} %shard_map.129.own), channel_id=1, source_target_pairs={{0,96},{4,7},{8,104},{12,15},{16,112},{20,23},{24,120},{28,31},{1,... | collective-permute-start | bytes 712712 | tf_op jit(solution)/shard_map/ppermute | solution.py:177
  135.6 0.3 collective-permute-start.11
  135.9 0.4 collective-permute-start.10
  136.3 4.9 %collective-permute-done.12.three = bf16[928,128]{1,0:T(8,128)(2,1)S(1)} collective-permute-done((bf16[928,128]{1,0:T(8,128)(2,1)S(1)}, bf16[928,128]{1,0:T(8,128)(2,1)S(1)}, u32[]{:S(2)}, u32[]{:S(2)}) %collective-permute-start.12) | collective-permute-done | bytes 237600 | tf_op jit(solution)/shard_map/ppermute | solution.py:177
  141.2 1.0 collective-permute-done.11.two
  142.2 2.7 %collective-permute-done.10.one = bf16[928,128]{1,0:T(8,128)(2,1)S(1)} collective-permute-done((bf16[928,128]{1,0:T(8,128)(2,1)S(1)}, bf16[928,128]{1,0:T(8,128)(2,1)S(1)}, u32[]{:S(2)}, u32[]{:S(2)}) %collective-permute-start.10) | collective-permute-done | bytes 237600 | tf_op jit(solution)/shard_map/ppermute | solution.py:177
  144.9 0.3 shard_map.130.own
  145.2 4.9 %collective-permute-start.13 = (bf16[928,512]{1,0:T(8,128)(2,1)S(1)}, bf16[928,512]{1,0:T(8,128)(2,1)S(1)}, u32[]{:S(2)}, u32[]{:S(2)}) collective-permute-start(bf16[928,512]{1,0:T(8,128)(2,1)S(1)} %shard_map.130.own), channel_id=1, source_target_pairs={{0,4},{4,0},{8,12},{12,8},{16,20},{20,16},{24,28},{28,24},{1,5},{5... | collective-permute-start | bytes 2850824 | tf_op jit(solution)/shard_map/ppermute | solution.py:181
  150.1 1.3 shard_map.131
  151.4 0.8 collective-permute-done.13.other
  152.2 1.8 %shard_map.132 = (f32[768,1024]{1,0:T(8,128)}, f32[153,1024]{1,0:T(8,128)}, f32[1,1]{1,0:T(1,128)}) custom-call(s32[1]{0:T(128)} %bitcast.core, bf16[928,512]{1,0:T(8,128)(2,1)S(1)} %shard_map.130.own, bf16[928,512]{1,0:T(8,128)(2,1)S(1)} %collective-permute-done.13.other, ...), custom_call_target="tpu_custom_call", output_to_operand_aliasing={{0}: (3, {}), {1}: (4, {})} | custom-call | tf_op jit(solution)/shard_map/pallas_call | solution.py:204
  (1 shorter events, 0.0 us)
Async XLA Ops:
  33.3 5.6 %copy-start.9 = (s32[1024]{0:T(1024)S(1)}, s32[1024]{0:T(1024)}, u32[]{:S(2)}) copy-start(s32[1024]{0:T(1024)} %param.17) | copy-start | bytes 12292
  33.3 6.6 %copy-start.8 = (bf16[1024,153]{0,1:T(8,128)(2,1)S(1)}, bf16[1024,153]{0,1:T(8,128)(2,1)}, u32[]{:S(2)}) copy-start(bf16[1024,153]{0,1:T(8,128)(2,1)} %param.19) | copy-start | bytes 940036
  33.3 7.5 %copy-start.1 = (bf16[48,128,128]{2,1,0:T(8,128)(2,1)S(1)}, bf16[48,128,128]{2,1,0:T(8,128)(2,1)}, u32[]{:S(2)}) copy-start(bf16[48,128,128]{2,1,0:T(8,128)(2,1)} %tiles.1) | copy-start | bytes 4718596
  33.3 7.5 %copy-start.2 = (s32[1,1024]{1,0:T(1,128)S(1)}, s32[1,1024]{1,0:T(1,128)}, u32[]{:S(2)}) copy-start(s32[1,1024]{1,0:T(1,128)} %get-tuple-element.20.position) | copy-start | bytes 12292
  33.3 7.5 %copy-start.3 = (s32[48]{0:T(128)S(1)}, s32[48]{0:T(128)}, u32[]{:S(2)}) copy-start(s32[48]{0:T(128)} %row.1) | copy-start | bytes 580
  33.3 7.5 %copy-start.4 = (s32[48]{0:T(128)S(1)}, s32[48]{0:T(128)}, u32[]{:S(2)}) copy-start(s32[48]{0:T(128)} %column.1) | copy-start | bytes 580
  33.4 46.7 %all-to-all-start.1 = ((bf16[128,16,768]{2,1,0:T(8,128)(2,1)}), bf16[128,16,768]{2,1,0:T(8,128)(2,1)}, u32[]{:S(2)}, u32[]{:S(2)}) async-start(bf16[128,16,768]{2,1,0:T(8,128)(2,1)} %bitcast.14), calls=%async_computation.1 | async-start | bytes 6291456 | tf_op jit(solution)/shard_map/all_to_all | solution.py:512
  49.9 2.0 %copy-start.5 = (bf16[1024,2048]{1,0:T(8,128)(2,1)}, bf16[1024,2048]{1,0:T(8,128)(2,1)S(1)}, u32[]{:S(2)}) copy-start(bf16[1024,2048]{1,0:T(8,128)(2,1)S(1)} %get-tuple-element.21.moved_far) | copy-start | bytes 12582916
  51.9 1.4 copy-start.6
  53.3 1.3 copy-start.7
  99.8 2.8 %collective-permute-start = (bf16[928,512]{1,0:T(8,128)(2,1)}, bf16[928,512]{1,0:T(8,128)(2,1)S(1)}, u32[]{:S(2)}, u32[]{:S(2)}) collective-permute-start(bf16[928,512]{1,0:T(8,128)(2,1)} %get-tuple-element.25), channel_id=1, source_target_pairs={{0,4},{4,0},{8,12},{12,8},{16,20},{20,16},{24,28},{28,24},{1,5},{5... | collective-permute-start | bytes 2850824 | tf_op jit(solution)/shard_map/ppermute | solution.py:162
  100.1 1.2 copy-start
  103.1 9.1 %collective-permute-start.1 = (bf16[928,128]{1,0:T(8,128)(2,1)S(1)}, bf16[928,128]{1,0:T(8,128)(2,1)S(1)}, u32[]{:S(2)}, u32[]{:S(2)}) collective-permute-start(bf16[928,128]{1,0:T(8,128)(2,1)S(1)} %get-tuple-element.27), channel_id=1, source_target_pairs={{0,32},{4,5},{8,40},{12,13},{16,48},{20,21},{24,56},{28,29},{1,33}... | collective-permute-start | bytes 712712 | tf_op jit(solution)/shard_map/ppermute | solution.py:172
  103.5 8.7 %collective-permute-start.2 = (bf16[928,128]{1,0:T(8,128)(2,1)S(1)}, bf16[928,128]{1,0:T(8,128)(2,1)S(1)}, u32[]{:S(2)}, u32[]{:S(2)}) collective-permute-start(bf16[928,128]{1,0:T(8,128)(2,1)S(1)} %get-tuple-element.28), channel_id=1, source_target_pairs={{0,64},{4,6},{8,72},{12,14},{16,80},{20,22},{24,88},{28,30},{1,65}... | collective-permute-start | bytes 712712 | tf_op jit(solution)/shard_map/ppermute | solution.py:172
  105.5 7.3 %collective-permute-start.3 = (bf16[928,128]{1,0:T(8,128)(2,1)S(1)}, bf16[928,128]{1,0:T(8,128)(2,1)S(1)}, u32[]{:S(2)}, u32[]{:S(2)}) collective-permute-start(bf16[928,128]{1,0:T(8,128)(2,1)S(1)} %get-tuple-element.29), channel_id=1, source_target_pairs={{0,96},{4,7},{8,104},{12,15},{16,112},{20,23},{24,120},{28,31},{1,... | collective-permute-start | bytes 712712 | tf_op jit(solution)/shard_map/ppermute | solution.py:172
  113.1 5.3 %collective-permute-start.6 = (bf16[928,128]{1,0:T(8,128)(2,1)S(1)}, bf16[928,128]{1,0:T(8,128)(2,1)S(1)}, u32[]{:S(2)}, u32[]{:S(2)}) collective-permute-start(bf16[928,128]{1,0:T(8,128)(2,1)S(1)} %shard_map.127.own), channel_id=1, source_target_pairs={{0,3},{4,28},{8,11},{12,4},{16,19},{20,12},{24,27},{28,20},{1,0},{... | collective-permute-start | bytes 712712 | tf_op jit(solution)/shard_map/ppermute | solution.py:175
  113.2 6.6 %collective-permute-start.5 = (bf16[928,128]{1,0:T(8,128)(2,1)S(1)}, bf16[928,128]{1,0:T(8,128)(2,1)S(1)}, u32[]{:S(2)}, u32[]{:S(2)}) collective-permute-start(bf16[928,128]{1,0:T(8,128)(2,1)S(1)} %shard_map.127.own), channel_id=1, source_target_pairs={{0,2},{4,20},{8,10},{12,28},{16,18},{20,4},{24,26},{28,12},{1,3},{... | collective-permute-start | bytes 712712 | tf_op jit(solution)/shard_map/ppermute | solution.py:175
  114.8 7.7 %collective-permute-start.4 = (bf16[928,128]{1,0:T(8,128)(2,1)S(1)}, bf16[928,128]{1,0:T(8,128)(2,1)S(1)}, u32[]{:S(2)}, u32[]{:S(2)}) collective-permute-start(bf16[928,128]{1,0:T(8,128)(2,1)S(1)} %shard_map.127.own), channel_id=1, source_target_pairs={{0,1},{4,12},{8,9},{12,20},{16,17},{20,28},{24,25},{28,4},{1,2},{5... | collective-permute-start | bytes 712712 | tf_op jit(solution)/shard_map/ppermute | solution.py:175
  122.8 5.0 %collective-permute-start.9 = (bf16[928,128]{1,0:T(8,128)(2,1)S(1)}, bf16[928,128]{1,0:T(8,128)(2,1)S(1)}, u32[]{:S(2)}, u32[]{:S(2)}) collective-permute-start(bf16[928,128]{1,0:T(8,128)(2,1)S(1)} %shard_map.128.own), channel_id=1, source_target_pairs={{0,24},{4,100},{8,0},{12,108},{16,8},{20,116},{24,16},{28,124},{1,... | collective-permute-start | bytes 712712 | tf_op jit(solution)/shard_map/ppermute | solution.py:175
  123.7 6.6 %collective-permute-start.8 = (bf16[928,128]{1,0:T(8,128)(2,1)S(1)}, bf16[928,128]{1,0:T(8,128)(2,1)S(1)}, u32[]{:S(2)}, u32[]{:S(2)}) collective-permute-start(bf16[928,128]{1,0:T(8,128)(2,1)S(1)} %shard_map.128.own), channel_id=1, source_target_pairs={{0,16},{4,68},{8,24},{12,76},{16,0},{20,84},{24,8},{28,92},{1,17},... | collective-permute-start | bytes 712712 | tf_op jit(solution)/shard_map/ppermute | solution.py:175
  124.9 8.1 %collective-permute-start.7 = (bf16[928,128]{1,0:T(8,128)(2,1)S(1)}, bf16[928,128]{1,0:T(8,128)(2,1)S(1)}, u32[]{:S(2)}, u32[]{:S(2)}) collective-permute-start(bf16[928,128]{1,0:T(8,128)(2,1)S(1)} %shard_map.128.own), channel_id=1, source_target_pairs={{0,8},{4,36},{8,16},{12,44},{16,24},{20,52},{24,0},{28,60},{1,9},{... | collective-permute-start | bytes 712712 | tf_op jit(solution)/shard_map/ppermute | solution.py:175
  133.3 8.0 %collective-permute-start.12 = (bf16[928,128]{1,0:T(8,128)(2,1)S(1)}, bf16[928,128]{1,0:T(8,128)(2,1)S(1)}, u32[]{:S(2)}, u32[]{:S(2)}) collective-permute-start(bf16[928,128]{1,0:T(8,128)(2,1)S(1)} %shard_map.129.own), channel_id=1, source_target_pairs={{0,96},{4,7},{8,104},{12,15},{16,112},{20,23},{24,120},{28,31},{1,... | collective-permute-start | bytes 712712 | tf_op jit(solution)/shard_map/ppermute | solution.py:177
  135.6 6.6 %collective-permute-start.11 = (bf16[928,128]{1,0:T(8,128)(2,1)S(1)}, bf16[928,128]{1,0:T(8,128)(2,1)S(1)}, u32[]{:S(2)}, u32[]{:S(2)}) collective-permute-start(bf16[928,128]{1,0:T(8,128)(2,1)S(1)} %shard_map.129.own), channel_id=1, source_target_pairs={{0,64},{4,6},{8,72},{12,14},{16,80},{20,22},{24,88},{28,30},{1,65}... | collective-permute-start | bytes 712712 | tf_op jit(solution)/shard_map/ppermute | solution.py:177
  135.9 9.0 %collective-permute-start.10 = (bf16[928,128]{1,0:T(8,128)(2,1)S(1)}, bf16[928,128]{1,0:T(8,128)(2,1)S(1)}, u32[]{:S(2)}, u32[]{:S(2)}) collective-permute-start(bf16[928,128]{1,0:T(8,128)(2,1)S(1)} %shard_map.129.own), channel_id=1, source_target_pairs={{0,32},{4,5},{8,40},{12,13},{16,48},{20,21},{24,56},{28,29},{1,33}... | collective-permute-start | bytes 712712 | tf_op jit(solution)/shard_map/ppermute | solution.py:177
  145.2 7.0 %collective-permute-start.13 = (bf16[928,512]{1,0:T(8,128)(2,1)S(1)}, bf16[928,512]{1,0:T(8,128)(2,1)S(1)}, u32[]{:S(2)}, u32[]{:S(2)}) collective-permute-start(bf16[928,512]{1,0:T(8,128)(2,1)S(1)} %shard_map.130.own), channel_id=1, source_target_pairs={{0,4},{4,0},{8,12},{12,8},{16,20},{20,16},{24,28},{28,24},{1,5},{5... | collective-permute-start | bytes 2850824 | tf_op jit(solution)/shard_map/ppermute | solution.py:181

commit v6 on v5

--- a/solution.py
+++ b/solution.py
@@ -12,6 +12,7 @@
 WIDTH = 128
 LOSS_ROW = 921
 ROWS = 928
+PITCH = 7
 
 
 def flat(x, y, z, core):
@@ -245,6 +246,7 @@
 
 def fetch_rows(wanted_far, table, far, wanted, narrow, wide, some, out, listed, arrival, leaving):
     stored, width = table.shape
+    pieces = width // 128
     step = stored // arrival.shape[0]
 
     def load(block):
@@ -257,26 +259,39 @@
         load(block).start()
     for block in range(arrival.shape[0]):
         load(block).wait()
-        for start in range(block * step, (block + 1) * step, 128):
-            rows = slice(start, start + 128)
-            wide[rows, :] = narrow[rows, :].astype(jnp.float32)
+
+        @pl.loop(0, step // 64)
+        def _(part):
+            start = pl.multiple_of(block * step + part * 64, 64)
+            values = narrow[pl.ds(start, 64), :].astype(jnp.float32)
+            for line in range(0, 64, 8):
+                for piece in range(pieces):
+                    lines = pl.ds((start + line) * PITCH + piece, 8, stride=PITCH)
+                    wide[lines, :] = values[line : line + 8, piece * 128 : (piece + 1) * 128]
 
     listing.wait()
     devices, capacity = wanted.shape
-    owners = some.shape[0] // capacity
+    group = out.shape[0] // leaving.shape[0]
+    owners = group // capacity
 
     def send(block):
-        rows = pl.ds(pl.multiple_of(block * some.shape[0], some.shape[0]), some.shape[0])
+        rows = pl.ds(pl.multiple_of(block * group, group), group)
         return pltpu.make_async_copy(out.at[rows, :], far.at[rows, :], leaving.at[block])
 
     @pl.loop(0, devices // owners)
     def _(block):
-        for owner in range(owners):
-            for slot in range(capacity):
-                row = wanted[block * owners + owner, slot]
-                some[pl.ds(owner * capacity + slot, 1), :] = wide[pl.ds(row, 1), :]
-        rows = pl.ds(pl.multiple_of(block * some.shape[0], some.shape[0]), some.shape[0])
-        out[rows, :] = some[...].astype(jnp.bfloat16)
+        for line in range(group):
+            row = wanted[block * owners + line // capacity, line % capacity]
+            some[pl.ds(line * PITCH, pieces), :] = wide[pl.ds(row * PITCH, pieces), :]
+        for line in range(0, group, 16):
+            rows = pl.ds(pl.multiple_of(block * group + line, 16), 16)
+            for piece in range(pieces):
+                halves = [
+                    some[pl.ds((line + half) * PITCH + piece, 8, stride=PITCH), :] for half in (0, 8)
+                ]
+                out[rows, piece * 128 : (piece + 1) * 128] = jnp.concatenate(halves, axis=0).astype(
+                    jnp.bfloat16
+                )
         send(block).start()
 
     @pl.loop(0, devices // owners)
@@ -500,12 +515,12 @@
         scratch_shapes=[
             pltpu.SMEM(wanted.shape, jnp.int32),
             pltpu.VMEM(features.shape, bf),
-            pltpu.VMEM(features.shape, jnp.float32),
-            pltpu.VMEM((64, width), jnp.float32),
+            pltpu.VMEM((features.shape[0] * PITCH + 64, 128), jnp.float32),
+            pltpu.VMEM((128 * PITCH + 64, 128), jnp.float32),
             pltpu.VMEM((slots, width), bf),
             pltpu.SemaphoreType.DMA,
             pltpu.SemaphoreType.DMA((8,)),
-            pltpu.SemaphoreType.DMA((slots // 64,)),
+            pltpu.SemaphoreType.DMA((slots // 128,)),
         ],
         compiler_params=pltpu.CompilerParams(vmem_limit_bytes=56 << 20),
     )(wanted, features)

time: 154 us -> 152 us (0.987)
  Pallas kernels: 44.5 us -> 42.4 us
    pallas_call x1, Pallas kernels: 8.92 us -> 6.48 us  [on_device(): pl.pallas_call(fetch_rows, out_shape=jax.ShapeDtypeStruct((slots, width),...]
where the time goes in v6:
time: 152 us
  waiting for transfers between devices  58.2 us (38%)
  Pallas kernels  42.4 us (28%)
  blocking collectives  21.9 us (14%)
  starting transfers between devices  19.8 us (13%)
  local copies, waits for them, and re-layouts  7.82 us (5%)
  between operations  1.61 us (1%)
    all_to_all x1, waiting for transfers between devices, on_device(): lax.all_to_all(found, AXES, split_axis=0, concat_axis=0, tiled=True)  25.1 us
    all_to_all x1, blocking collectives, on_device(): lax.all_to_all(requests, AXES, split_axis=0, concat_axis=0, tiled=True)  21.9 us
    pallas_call x1, Pallas kernels, on_device(): pl.pallas_call(partial(train, classes=classes), out_shape=[jax.ShapeDtype...  19.7 us
    ppermute x6, waiting for transfers between devices, sum_over_devices(): got = [lax.ppermute(total, AXES, shift_pairs(axes, k)) for k in (1, 2, 3)]  15.8 us
    pallas_call x1, Pallas kernels, on_device(): call(build_spread, [jax.ShapeDtypeStruct((nodes, nodes), bf), jax.ShapeDt...  9.48 us
    ppermute x3, waiting for transfers between devices, sum_over_devices(): got = [lax.ppermute(total, AXES, shift_pairs(FIRST, k)) for k in (1, 2, 3)]  8.59 us
    ppermute x3, waiting for transfers between devices, sum_over_devices(): lax.ppermute(part, AXES, shift_pairs(FIRST, k + 1))  6.79 us
    pallas_call x1, Pallas kernels, on_device(): pl.pallas_call(fetch_rows, out_shape=jax.ShapeDtypeStruct((slots, width),...  6.48 us
  transfers between devices with their start and end apart: 15, of which 14 were waited for; matrix products, arithmetic and copies ran while one was open for 1% of the time, Pallas kernels for 7%

profile of v6, /device:TPU:1, one launch (start us, length us, event | category | flops | bytes accessed | tf_op | source)
XLA Modules:
  0.0 151.8 jit_solution(5230332955164619141)
XLA Ops:
  0.6 1.8 %shard_map.121 = (s32[128,16]{1,0:T(8,128)}, s32[1,1024]{1,0:T(1,128)}) custom-call(s32[1,1024]{1,0:T(1,128)} %bitcast.20, s32[1,1024]{1,0:T(1,128)} %bitcast.21), custom_call_target="tpu_custom_call" | custom-call | tf_op jit(solution)/shard_map/pallas_call | solution.py:496
  2.5 21.9 %all_to_all.22 = s32[128,1,16]{2,1,0:T(1,128)} all-to-all(s32[128,1,16]{2,1,0:T(1,128)} %bitcast.18), channel_id=1, replica_groups=mesh['store'=32,'batch'=4] {'store','batch'}, dimensions={0} | all-to-all | bytes 16384 | tf_op jit(solution)/shard_map/all_to_all | solution.py:506
  24.3 6.5 %shard_map.122 = bf16[2048,768]{1,0:T(8,128)(2,1)} custom-call(s32[128,16]{1,0:T(8,128)} %bitcast.17, bf16[4096,768]{1,0:T(8,128)(2,1)} %table.1), custom_call_target="tpu_custom_call" | custom-call | tf_op jit(solution)/shard_map/pallas_call | solution.py:510
  30.8 0.0 copy-start.9
  30.9 0.0 copy-start.8
  30.9 0.0 copy-start.1
  30.9 0.0 copy-start.2
  30.9 0.0 copy-start.3
  30.9 0.0 copy-start.4
  30.9 4.8 %all-to-all-start.1 = ((bf16[128,16,768]{2,1,0:T(8,128)(2,1)}), bf16[128,16,768]{2,1,0:T(8,128)(2,1)}, u32[]{:S(2)}, u32[]{:S(2)}) async-start(bf16[128,16,768]{2,1,0:T(8,128)(2,1)} %bitcast.14), calls=%async_computation.1 | async-start | bytes 6291456 | tf_op jit(solution)/shard_map/all_to_all | solution.py:527
  36.4 0.0 copy-done.9
  36.4 1.1 copy.17.labels_far
  37.5 0.0 copy-done.8
  37.5 0.8 pad.4.two_far
  38.3 0.0 copy-done.1
  38.4 0.0 copy-done.2
  38.4 0.0 copy-done.3
  38.4 0.0 copy-done.4
  38.4 9.5 %shard_map.123 = (bf16[1024,1024]{1,0:T(8,128)(2,1)S(1)}, bf16[1024,1024]{1,0:T(8,128)(2,1)S(1)}, bf16[1024,2048]{1,0:T(8,128)(2,1)S(1)}) custom-call(s32[48]{0:T(128)S(1)} %copy-done.3, s32[48]{0:T(128)S(1)} %copy-done.4, s32[1]{0:T(128)S(6)} %copy.20.count, bf16[48,128,128]{2,1,0:T(8,128)(2,1)S(1)} %copy-done.1, s32[1,1024]{1,0:T(1,128)S(1)} %copy-done.2), custom_call_target="tpu_custom_call" | custom-call | flops 4294967296 | bytes 12582912 | tf_op jit(solution)/shard_map/pallas_call | solution.py:528
  47.8 0.0 copy-start.5
  47.9 2.0 %copy-done.5 = bf16[1024,2048]{1,0:T(8,128)(2,1)} copy-done((bf16[1024,2048]{1,0:T(8,128)(2,1)}, bf16[1024,2048]{1,0:T(8,128)(2,1)S(1)}, u32[]{:S(2)}) %copy-start.5) | copy-done | bytes 4194328
  49.8 0.0 copy-start.6
  49.8 1.4 copy-done.6
  51.2 0.0 copy-start.7
  51.2 1.3 copy-done.7
  52.5 25.1 %all-to-all-done.1 = bf16[128,16,768]{2,1,0:T(8,128)(2,1)} async-done(((bf16[128,16,768]{2,1,0:T(8,128)(2,1)}), bf16[128,16,768]{2,1,0:T(8,128)(2,1)}, u32[]{:S(2)}, u32[]{:S(2)}) %all-to-all-start.1) | async-done | bytes 3145760 | tf_op jit(solution)/shard_map/all_to_all | solution.py:527
  77.7 19.7 %shard_map.124 = (bf16[928,512]{1,0:T(8,128)(2,1)}, bf16[928,512]{1,0:T(8,128)(2,1)}) custom-call(s32[1]{0:T(128)} %bitcast.core, bf16[2048,768]{1,0:T(8,128)(2,1)} %bitcast.8.arrived_far, bf16[1024,2048]{1,0:T(8,128)(2,1)} %copy-done.5, bf16[1024,1024]{1,0:T(8,128)(2,1)} %copy-done.6, bf16[1024,1024]{1,0:T(8,128)(2,1)} %copy-done.7, ...), custom_call_target="tpu_custom_call" | custom-call | flops 12884901888 | bytes 16777216 | tf_op jit(solution)/shard_map/pallas_call | solution.py:544
  97.4 0.3 collective-permute-start
  97.7 1.2 copy-done
  98.9 0.2 shard_map.125.own
  99.1 1.1 collective-permute-done.arrived
  100.2 0.5 shard_map.126
  100.7 0.4 collective-permute-start.1
  101.1 2.0 %collective-permute-start.2 = (bf16[928,128]{1,0:T(8,128)(2,1)S(1)}, bf16[928,128]{1,0:T(8,128)(2,1)S(1)}, u32[]{:S(2)}, u32[]{:S(2)}) collective-permute-start(bf16[928,128]{1,0:T(8,128)(2,1)S(1)} %get-tuple-element.28), channel_id=1, source_target_pairs={{0,64},{4,6},{8,72},{12,14},{16,80},{20,22},{24,88},{28,30},{1,65}... | collective-permute-start | bytes 712712 | tf_op jit(solution)/shard_map/ppermute | solution.py:173
  103.1 0.5 collective-permute-start.3
  103.6 6.2 %collective-permute-done.1.one = bf16[928,128]{1,0:T(8,128)(2,1)S(1)} collective-permute-done((bf16[928,128]{1,0:T(8,128)(2,1)S(1)}, bf16[928,128]{1,0:T(8,128)(2,1)S(1)}, u32[]{:S(2)}, u32[]{:S(2)}) %collective-permute-start.1) | collective-permute-done | bytes 237600 | tf_op jit(solution)/shard_map/ppermute | solution.py:173
  109.7 0.0 collective-permute-done.2.two
  109.7 0.6 collective-permute-done.3.three
  110.4 0.3 shard_map.127.own
  110.7 0.1 collective-permute-start.6
  110.8 1.6 %collective-permute-start.5 = (bf16[928,128]{1,0:T(8,128)(2,1)S(1)}, bf16[928,128]{1,0:T(8,128)(2,1)S(1)}, u32[]{:S(2)}, u32[]{:S(2)}) collective-permute-start(bf16[928,128]{1,0:T(8,128)(2,1)S(1)} %shard_map.127.own), channel_id=1, source_target_pairs={{0,2},{4,20},{8,10},{12,28},{16,18},{20,4},{24,26},{28,12},{1,3},{... | collective-permute-start | bytes 712712 | tf_op jit(solution)/shard_map/ppermute | solution.py:176
  112.3 0.0 collective-permute-start.4
  112.4 3.6 %collective-permute-done.6.three = bf16[928,128]{1,0:T(8,128)(2,1)S(1)} collective-permute-done((bf16[928,128]{1,0:T(8,128)(2,1)S(1)}, bf16[928,128]{1,0:T(8,128)(2,1)S(1)}, u32[]{:S(2)}, u32[]{:S(2)}) %collective-permute-start.6) | collective-permute-done | bytes 237600 | tf_op jit(solution)/shard_map/ppermute | solution.py:176
  115.9 1.4 collective-permute-done.5.two
  117.3 2.7 %collective-permute-done.4.one = bf16[928,128]{1,0:T(8,128)(2,1)S(1)} collective-permute-done((bf16[928,128]{1,0:T(8,128)(2,1)S(1)}, bf16[928,128]{1,0:T(8,128)(2,1)S(1)}, u32[]{:S(2)}, u32[]{:S(2)}) %collective-permute-start.4) | collective-permute-done | bytes 237600 | tf_op jit(solution)/shard_map/ppermute | solution.py:176
  120.1 0.3 shard_map.128.own
  120.4 0.9 collective-permute-start.9
  121.3 1.2 collective-permute-start.8
  122.4 0.0 collective-permute-start.7
  122.5 2.9 %collective-permute-done.9.three = bf16[928,128]{1,0:T(8,128)(2,1)S(1)} collective-permute-done((bf16[928,128]{1,0:T(8,128)(2,1)S(1)}, bf16[928,128]{1,0:T(8,128)(2,1)S(1)}, u32[]{:S(2)}, u32[]{:S(2)}) %collective-permute-start.9) | collective-permute-done | bytes 237600 | tf_op jit(solution)/shard_map/ppermute | solution.py:176
  125.3 2.5 %collective-permute-done.8.two = bf16[928,128]{1,0:T(8,128)(2,1)S(1)} collective-permute-done((bf16[928,128]{1,0:T(8,128)(2,1)S(1)}, bf16[928,128]{1,0:T(8,128)(2,1)S(1)}, u32[]{:S(2)}, u32[]{:S(2)}) %collective-permute-start.8) | collective-permute-done | bytes 237600 | tf_op jit(solution)/shard_map/ppermute | solution.py:176
  127.8 2.7 %collective-permute-done.7.one = bf16[928,128]{1,0:T(8,128)(2,1)S(1)} collective-permute-done((bf16[928,128]{1,0:T(8,128)(2,1)S(1)}, bf16[928,128]{1,0:T(8,128)(2,1)S(1)}, u32[]{:S(2)}, u32[]{:S(2)}) %collective-permute-start.7) | collective-permute-done | bytes 237600 | tf_op jit(solution)/shard_map/ppermute | solution.py:176
  130.6 0.3 shard_map.129.own
  130.8 2.4 %collective-permute-start.12 = (bf16[928,128]{1,0:T(8,128)(2,1)S(1)}, bf16[928,128]{1,0:T(8,128)(2,1)S(1)}, u32[]{:S(2)}, u32[]{:S(2)}) collective-permute-start(bf16[928,128]{1,0:T(8,128)(2,1)S(1)} %shard_map.129.own), channel_id=1, source_target_pairs={{0,96},{4,7},{8,104},{12,15},{16,112},{20,23},{24,120},{28,31},{1,... | collective-permute-start | bytes 712712 | tf_op jit(solution)/shard_map/ppermute | solution.py:178
  133.2 0.3 collective-permute-start.11
  133.5 0.4 collective-permute-start.10
  133.9 4.9 %collective-permute-done.12.three = bf16[928,128]{1,0:T(8,128)(2,1)S(1)} collective-permute-done((bf16[928,128]{1,0:T(8,128)(2,1)S(1)}, bf16[928,128]{1,0:T(8,128)(2,1)S(1)}, u32[]{:S(2)}, u32[]{:S(2)}) %collective-permute-start.12) | collective-permute-done | bytes 237600 | tf_op jit(solution)/shard_map/ppermute | solution.py:178
  138.8 1.0 collective-permute-done.11.two
  139.8 2.7 %collective-permute-done.10.one = bf16[928,128]{1,0:T(8,128)(2,1)S(1)} collective-permute-done((bf16[928,128]{1,0:T(8,128)(2,1)S(1)}, bf16[928,128]{1,0:T(8,128)(2,1)S(1)}, u32[]{:S(2)}, u32[]{:S(2)}) %collective-permute-start.10) | collective-permute-done | bytes 237600 | tf_op jit(solution)/shard_map/ppermute | solution.py:178
  142.5 0.3 shard_map.130.own
  142.7 4.9 %collective-permute-start.13 = (bf16[928,512]{1,0:T(8,128)(2,1)S(1)}, bf16[928,512]{1,0:T(8,128)(2,1)S(1)}, u32[]{:S(2)}, u32[]{:S(2)}) collective-permute-start(bf16[928,512]{1,0:T(8,128)(2,1)S(1)} %shard_map.130.own), channel_id=1, source_target_pairs={{0,4},{4,0},{8,12},{12,8},{16,20},{20,16},{24,28},{28,24},{1,5},{5... | collective-permute-start | bytes 2850824 | tf_op jit(solution)/shard_map/ppermute | solution.py:182
  147.6 1.3 shard_map.131
  148.9 0.8 collective-permute-done.13.other
  149.8 1.8 %shard_map.132 = (f32[768,1024]{1,0:T(8,128)}, f32[153,1024]{1,0:T(8,128)}, f32[1,1]{1,0:T(1,128)}) custom-call(s32[1]{0:T(128)} %bitcast.core, bf16[928,512]{1,0:T(8,128)(2,1)S(1)} %shard_map.130.own, bf16[928,512]{1,0:T(8,128)(2,1)S(1)} %collective-permute-done.13.other, ...), custom_call_target="tpu_custom_call", output_to_operand_aliasing={{0}: (3, {}), {1}: (4, {})} | custom-call | tf_op jit(solution)/shard_map/pallas_call | solution.py:205
  (1 shorter events, 0.0 us)
Async XLA Ops:
  30.8 5.6 %copy-start.9 = (s32[1024]{0:T(1024)S(1)}, s32[1024]{0:T(1024)}, u32[]{:S(2)}) copy-start(s32[1024]{0:T(1024)} %param.17) | copy-start | bytes 12292
  30.9 6.6 %copy-start.8 = (bf16[1024,153]{0,1:T(8,128)(2,1)S(1)}, bf16[1024,153]{0,1:T(8,128)(2,1)}, u32[]{:S(2)}) copy-start(bf16[1024,153]{0,1:T(8,128)(2,1)} %param.19) | copy-start | bytes 940036
  30.9 7.5 %copy-start.1 = (bf16[48,128,128]{2,1,0:T(8,128)(2,1)S(1)}, bf16[48,128,128]{2,1,0:T(8,128)(2,1)}, u32[]{:S(2)}) copy-start(bf16[48,128,128]{2,1,0:T(8,128)(2,1)} %tiles.1) | copy-start | bytes 4718596
  30.9 7.5 %copy-start.2 = (s32[1,1024]{1,0:T(1,128)S(1)}, s32[1,1024]{1,0:T(1,128)}, u32[]{:S(2)}) copy-start(s32[1,1024]{1,0:T(1,128)} %get-tuple-element.20.position) | copy-start | bytes 12292
  30.9 7.5 %copy-start.3 = (s32[48]{0:T(128)S(1)}, s32[48]{0:T(128)}, u32[]{:S(2)}) copy-start(s32[48]{0:T(128)} %row.1) | copy-start | bytes 580
  30.9 7.5 %copy-start.4 = (s32[48]{0:T(128)S(1)}, s32[48]{0:T(128)}, u32[]{:S(2)}) copy-start(s32[48]{0:T(128)} %column.1) | copy-start | bytes 580
  30.9 46.7 %all-to-all-start.1 = ((bf16[128,16,768]{2,1,0:T(8,128)(2,1)}), bf16[128,16,768]{2,1,0:T(8,128)(2,1)}, u32[]{:S(2)}, u32[]{:S(2)}) async-start(bf16[128,16,768]{2,1,0:T(8,128)(2,1)} %bitcast.14), calls=%async_computation.1 | async-start | bytes 6291456 | tf_op jit(solution)/shard_map/all_to_all | solution.py:527
  47.8 2.0 %copy-start.5 = (bf16[1024,2048]{1,0:T(8,128)(2,1)}, bf16[1024,2048]{1,0:T(8,128)(2,1)S(1)}, u32[]{:S(2)}) copy-start(bf16[1024,2048]{1,0:T(8,128)(2,1)S(1)} %get-tuple-element.21.moved_far) | copy-start | bytes 12582916
  49.8 1.4 copy-start.6
  51.2 1.3 copy-start.7
  97.4 2.8 %collective-permute-start = (bf16[928,512]{1,0:T(8,128)(2,1)}, bf16[928,512]{1,0:T(8,128)(2,1)S(1)}, u32[]{:S(2)}, u32[]{:S(2)}) collective-permute-start(bf16[928,512]{1,0:T(8,128)(2,1)} %get-tuple-element.25), channel_id=1, source_target_pairs={{0,4},{4,0},{8,12},{12,8},{16,20},{20,16},{24,28},{28,24},{1,5},{5... | collective-permute-start | bytes 2850824 | tf_op jit(solution)/shard_map/ppermute | solution.py:163
  97.7 1.2 copy-start
  100.7 9.1 %collective-permute-start.1 = (bf16[928,128]{1,0:T(8,128)(2,1)S(1)}, bf16[928,128]{1,0:T(8,128)(2,1)S(1)}, u32[]{:S(2)}, u32[]{:S(2)}) collective-permute-start(bf16[928,128]{1,0:T(8,128)(2,1)S(1)} %get-tuple-element.27), channel_id=1, source_target_pairs={{0,32},{4,5},{8,40},{12,13},{16,48},{20,21},{24,56},{28,29},{1,33}... | collective-permute-start | bytes 712712 | tf_op jit(solution)/shard_map/ppermute | solution.py:173
  101.1 8.7 %collective-permute-start.2 = (bf16[928,128]{1,0:T(8,128)(2,1)S(1)}, bf16[928,128]{1,0:T(8,128)(2,1)S(1)}, u32[]{:S(2)}, u32[]{:S(2)}) collective-permute-start(bf16[928,128]{1,0:T(8,128)(2,1)S(1)} %get-tuple-element.28), channel_id=1, source_target_pairs={{0,64},{4,6},{8,72},{12,14},{16,80},{20,22},{24,88},{28,30},{1,65}... | collective-permute-start | bytes 712712 | tf_op jit(solution)/shard_map/ppermute | solution.py:173
  103.1 7.3 %collective-permute-start.3 = (bf16[928,128]{1,0:T(8,128)(2,1)S(1)}, bf16[928,128]{1,0:T(8,128)(2,1)S(1)}, u32[]{:S(2)}, u32[]{:S(2)}) collective-permute-start(bf16[928,128]{1,0:T(8,128)(2,1)S(1)} %get-tuple-element.29), channel_id=1, source_target_pairs={{0,96},{4,7},{8,104},{12,15},{16,112},{20,23},{24,120},{28,31},{1,... | collective-permute-start | bytes 712712 | tf_op jit(solution)/shard_map/ppermute | solution.py:173
  110.7 5.3 %collective-permute-start.6 = (bf16[928,128]{1,0:T(8,128)(2,1)S(1)}, bf16[928,128]{1,0:T(8,128)(2,1)S(1)}, u32[]{:S(2)}, u32[]{:S(2)}) collective-permute-start(bf16[928,128]{1,0:T(8,128)(2,1)S(1)} %shard_map.127.own), channel_id=1, source_target_pairs={{0,3},{4,28},{8,11},{12,4},{16,19},{20,12},{24,27},{28,20},{1,0},{... | collective-permute-start | bytes 712712 | tf_op jit(solution)/shard_map/ppermute | solution.py:176
  110.8 6.6 %collective-permute-start.5 = (bf16[928,128]{1,0:T(8,128)(2,1)S(1)}, bf16[928,128]{1,0:T(8,128)(2,1)S(1)}, u32[]{:S(2)}, u32[]{:S(2)}) collective-permute-start(bf16[928,128]{1,0:T(8,128)(2,1)S(1)} %shard_map.127.own), channel_id=1, source_target_pairs={{0,2},{4,20},{8,10},{12,28},{16,18},{20,4},{24,26},{28,12},{1,3},{... | collective-permute-start | bytes 712712 | tf_op jit(solution)/shard_map/ppermute | solution.py:176
  112.3 7.7 %collective-permute-start.4 = (bf16[928,128]{1,0:T(8,128)(2,1)S(1)}, bf16[928,128]{1,0:T(8,128)(2,1)S(1)}, u32[]{:S(2)}, u32[]{:S(2)}) collective-permute-start(bf16[928,128]{1,0:T(8,128)(2,1)S(1)} %shard_map.127.own), channel_id=1, source_target_pairs={{0,1},{4,12},{8,9},{12,20},{16,17},{20,28},{24,25},{28,4},{1,2},{5... | collective-permute-start | bytes 712712 | tf_op jit(solution)/shard_map/ppermute | solution.py:176
  120.4 5.0 %collective-permute-start.9 = (bf16[928,128]{1,0:T(8,128)(2,1)S(1)}, bf16[928,128]{1,0:T(8,128)(2,1)S(1)}, u32[]{:S(2)}, u32[]{:S(2)}) collective-permute-start(bf16[928,128]{1,0:T(8,128)(2,1)S(1)} %shard_map.128.own), channel_id=1, source_target_pairs={{0,24},{4,100},{8,0},{12,108},{16,8},{20,116},{24,16},{28,124},{1,... | collective-permute-start | bytes 712712 | tf_op jit(solution)/shard_map/ppermute | solution.py:176
  121.3 6.6 %collective-permute-start.8 = (bf16[928,128]{1,0:T(8,128)(2,1)S(1)}, bf16[928,128]{1,0:T(8,128)(2,1)S(1)}, u32[]{:S(2)}, u32[]{:S(2)}) collective-permute-start(bf16[928,128]{1,0:T(8,128)(2,1)S(1)} %shard_map.128.own), channel_id=1, source_target_pairs={{0,16},{4,68},{8,24},{12,76},{16,0},{20,84},{24,8},{28,92},{1,17},... | collective-permute-start | bytes 712712 | tf_op jit(solution)/shard_map/ppermute | solution.py:176
  122.4 8.1 %collective-permute-start.7 = (bf16[928,128]{1,0:T(8,128)(2,1)S(1)}, bf16[928,128]{1,0:T(8,128)(2,1)S(1)}, u32[]{:S(2)}, u32[]{:S(2)}) collective-permute-start(bf16[928,128]{1,0:T(8,128)(2,1)S(1)} %shard_map.128.own), channel_id=1, source_target_pairs={{0,8},{4,36},{8,16},{12,44},{16,24},{20,52},{24,0},{28,60},{1,9},{... | collective-permute-start | bytes 712712 | tf_op jit(solution)/shard_map/ppermute | solution.py:176
  130.8 8.0 %collective-permute-start.12 = (bf16[928,128]{1,0:T(8,128)(2,1)S(1)}, bf16[928,128]{1,0:T(8,128)(2,1)S(1)}, u32[]{:S(2)}, u32[]{:S(2)}) collective-permute-start(bf16[928,128]{1,0:T(8,128)(2,1)S(1)} %shard_map.129.own), channel_id=1, source_target_pairs={{0,96},{4,7},{8,104},{12,15},{16,112},{20,23},{24,120},{28,31},{1,... | collective-permute-start | bytes 712712 | tf_op jit(solution)/shard_map/ppermute | solution.py:178
  133.2 6.6 %collective-permute-start.11 = (bf16[928,128]{1,0:T(8,128)(2,1)S(1)}, bf16[928,128]{1,0:T(8,128)(2,1)S(1)}, u32[]{:S(2)}, u32[]{:S(2)}) collective-permute-start(bf16[928,128]{1,0:T(8,128)(2,1)S(1)} %shard_map.129.own), channel_id=1, source_target_pairs={{0,64},{4,6},{8,72},{12,14},{16,80},{20,22},{24,88},{28,30},{1,65}... | collective-permute-start | bytes 712712 | tf_op jit(solution)/shard_map/ppermute | solution.py:178
  133.5 9.0 %collective-permute-start.10 = (bf16[928,128]{1,0:T(8,128)(2,1)S(1)}, bf16[928,128]{1,0:T(8,128)(2,1)S(1)}, u32[]{:S(2)}, u32[]{:S(2)}) collective-permute-start(bf16[928,128]{1,0:T(8,128)(2,1)S(1)} %shard_map.129.own), channel_id=1, source_target_pairs={{0,32},{4,5},{8,40},{12,13},{16,48},{20,21},{24,56},{28,29},{1,33}... | collective-permute-start | bytes 712712 | tf_op jit(solution)/shard_map/ppermute | solution.py:178
  142.7 7.0 %collective-permute-start.13 = (bf16[928,512]{1,0:T(8,128)(2,1)S(1)}, bf16[928,512]{1,0:T(8,128)(2,1)S(1)}, u32[]{:S(2)}, u32[]{:S(2)}) collective-permute-start(bf16[928,512]{1,0:T(8,128)(2,1)S(1)} %shard_map.130.own), channel_id=1, source_target_pairs={{0,4},{4,0},{8,12},{12,8},{16,20},{20,16},{24,28},{28,24},{1,5},{5... | collective-permute-start | bytes 2850824 | tf_op jit(solution)/shard_map/ppermute | solution.py:182

commit v7 on v6

--- a/solution.py
+++ b/solution.py
@@ -299,19 +299,16 @@
         send(block).wait()
 
 
-def build_spread(row, column, count, tiles, position, dense, turned, moved):
+def build_spread(row, column, count, tiles, position, dense, moved):
     nodes = dense.shape[0]
     tile = tiles.shape[1]
     dense[...] = jnp.zeros_like(dense)
-    turned[...] = jnp.zeros_like(turned)
 
     @pl.loop(0, count[0])
     def _(t):
         at_row = pl.ds(pl.multiple_of(row[t] * tile, tile), tile)
         at_column = pl.ds(pl.multiple_of(column[t] * tile, tile), tile)
-        values = tiles[t]
-        dense[at_row, at_column] = values
-        turned[at_column, at_row] = values.T
+        dense[at_row, at_column] = tiles[t]
 
     width = 256
 
@@ -330,7 +327,6 @@
     arrived_far,
     moved_far,
     dense_far,
-    turned_far,
     one_far,
     two_far,
     labels_far,
@@ -339,7 +335,6 @@
     arrived,
     moved,
     dense,
-    turned,
     layer_one,
     layer_two,
     labels,
@@ -348,9 +343,9 @@
     mixed_turned,
     slope,
     hidden,
-    smooth,
-    upstream,
+    scored,
     upstream_turned,
+    back_turned,
     arrival,
     leaving,
     *,
@@ -373,15 +368,15 @@
     get_dense = load(5, dense_far, dense)
     get_two = load(6, two_far, layer_two)
     get_labels = load(7, labels_far, labels)
-    get_turned = load(8, turned_far, turned)
     get_moved = [
-        load(9 + at, moved_far.at[pl.ds(start, step), :], moved.at[pl.ds(start, step), :])
+        load(8 + at, moved_far.at[pl.ds(start, step), :], moved.at[pl.ds(start, step), :])
         for at, start in enumerate(tiles)
     ]
     get_moved[0].start()
     for copy in get_arrived:
         copy.start()
     get_one.start()
+    get_two.start()
     get_moved[0].wait()
     for at, start in enumerate(tiles):
         rows = slice(start, start + step)
@@ -402,32 +397,28 @@
         mixed_turned[:, rows] = mixed.T
         if at == 0:
             get_one.wait()
+            get_two.wait()
             get_dense.start()
-            get_two.start()
             get_labels.start()
-            get_turned.start()
         before = jnp.dot(mixed, layer_one[...], preferred_element_type=jnp.float32)
         square = before * before
         rate = 0.7978845608028654
         bend = jnp.tanh(rate * before * (1.0 + 0.044715 * square))
         rise = 0.5 * (1.0 + bend)
-        hidden[rows, :] = (before * rise).astype(jnp.bfloat16)
+        active = (before * rise).astype(jnp.bfloat16)
+        hidden[rows, :] = active
         slope[rows, :] = rise + 0.5 * before * (1.0 - bend * bend) * (
             rate + (3.0 * 0.044715 * rate) * square
         )
+        scored[rows, :] = lax.dot_general(
+            active, layer_two[...], (((1,), (1,)), ((), ())), preferred_element_type=jnp.float32
+        ).astype(jnp.bfloat16)
     get_dense.wait()
-    get_two.wait()
     get_labels.wait()
     loss = jnp.zeros((1, 1), jnp.float32)
     for start in tiles:
         rows = slice(start, start + step)
-        spread = jnp.dot(dense[rows, :], hidden[...], preferred_element_type=jnp.float32).astype(
-            jnp.bfloat16
-        )
-        smooth[rows, :] = spread
-        logits = lax.dot_general(
-            spread, layer_two[...], (((1,), (1,)), ((), ())), preferred_element_type=jnp.float32
-        )
+        logits = jnp.dot(dense[rows, :], scored[...], preferred_element_type=jnp.float32)
         lane = lax.broadcasted_iota(jnp.int32, logits.shape, 1)
         logits = jnp.where(lane < classes, logits, -jnp.inf)
         largest = jnp.max(logits, axis=1, keepdims=True)
@@ -436,37 +427,34 @@
         picked = jnp.sum(jnp.where(truth, logits, 0.0), axis=1, keepdims=True)
         loss += jnp.sum(logsum - picked, axis=0, keepdims=True)
         gap = (jnp.exp(logits - logsum) - jnp.where(truth, 1.0, 0.0)) * (1.0 / nodes)
-        upstream[rows, :] = gap.astype(jnp.bfloat16)
         upstream_turned[:, rows] = gap.astype(jnp.bfloat16).T
     loss = loss * (1.0 / nodes)
     high = loss.astype(jnp.bfloat16).astype(jnp.float32)
     middle = (loss - high).astype(jnp.bfloat16).astype(jnp.float32)
     low = loss - high - middle
     half = SIDE * WIDTH
-    get_turned.wait()
+    back_turned[...] = jnp.dot(
+        upstream_turned[...], dense[...], preferred_element_type=jnp.float32
+    ).astype(jnp.bfloat16)
+    back = back_turned[...].T
     stores = []
     for offset, out, far in ((1, sent, sent_far), (0, own, own_far)):
-        part = lax.rem(core[0] + offset, 2)
-        columns = pl.ds(pl.multiple_of(part * half, half), half)
+        side = lax.rem(core[0] + offset, 2)
+        columns = pl.ds(pl.multiple_of(side * half, half), half)
         second = jnp.dot(
-            upstream_turned[: ROWS - features, :],
-            smooth[:, columns],
-            preferred_element_type=jnp.float32,
+            back_turned[: ROWS - features, :], hidden[:, columns], preferred_element_type=jnp.float32
         )
         row = lax.broadcasted_iota(jnp.int32, second.shape, 0)
         lane = lax.broadcasted_iota(jnp.int32, second.shape, 1)
-        here = (row == LOSS_ROW - features) & (part == 0)
+        here = (row == LOSS_ROW - features) & (side == 0)
         second += jnp.where(here & (lane == 0), high, 0.0)
         second += jnp.where(here & (lane == 1), middle, 0.0)
         second += jnp.where(here & (lane == 2), low, 0.0)
         out[features:, :] = second.astype(out.dtype)
-        back = jnp.dot(
-            upstream[...], layer_two[:, columns], preferred_element_type=jnp.float32
-        ).astype(jnp.bfloat16)
-        back = jnp.dot(turned[...], back, preferred_element_type=jnp.float32)
-        back = (slope[:, columns] * back).astype(jnp.bfloat16)
+        back_hidden = jnp.dot(back, layer_two[:, columns], preferred_element_type=jnp.float32)
+        back_before = (slope[:, columns] * back_hidden).astype(jnp.bfloat16)
         out[:features, :] = jnp.dot(
-            mixed_turned[...], back, preferred_element_type=jnp.float32
+            mixed_turned[...], back_before, preferred_element_type=jnp.float32
         ).astype(out.dtype)
         stores.append(pltpu.make_async_copy(out, far, leaving.at[len(stores)]))
         stores[-1].start()
@@ -525,10 +513,9 @@
         compiler_params=pltpu.CompilerParams(vmem_limit_bytes=56 << 20),
     )(wanted, features)
     arrived = lax.all_to_all(found, AXES, split_axis=0, concat_axis=0, tiled=True)
-    dense, turned, moved = call(
+    dense, moved = call(
         build_spread,
         [
-            jax.ShapeDtypeStruct((nodes, nodes), bf),
             jax.ShapeDtypeStruct((nodes, nodes), bf),
             jax.ShapeDtypeStruct((nodes, slots), bf),
         ],
@@ -547,12 +534,11 @@
             jax.ShapeDtypeStruct((ROWS, half), bf),
             jax.ShapeDtypeStruct((ROWS, half), bf),
         ],
-        in_specs=[smem] + [anywhere] * 7,
+        in_specs=[smem] + [anywhere] * 6,
         out_specs=[anywhere] * 2,
         scratch_shapes=[
             pltpu.VMEM((slots, width), bf),
             pltpu.VMEM((nodes, slots), bf),
-            pltpu.VMEM((nodes, nodes), bf),
             pltpu.VMEM((nodes, nodes), bf),
             pltpu.VMEM((width, hidden), bf),
             pltpu.VMEM((256, hidden), bf),
@@ -562,10 +548,10 @@
             pltpu.VMEM((width, nodes), bf),
             pltpu.VMEM((nodes, hidden), jnp.float32),
             pltpu.VMEM((nodes, hidden), bf),
-            pltpu.VMEM((nodes, hidden), bf),
             pltpu.VMEM((nodes, 256), bf),
             pltpu.VMEM((256, nodes), bf),
-            pltpu.SemaphoreType.DMA((13,)),
+            pltpu.VMEM((256, nodes), bf),
+            pltpu.SemaphoreType.DMA((12,)),
             pltpu.SemaphoreType.DMA((2,)),
         ],
         compiler_params=pltpu.CompilerParams(vmem_limit_bytes=56 << 20),
@@ -577,7 +563,6 @@
         arrived.reshape(slots, width),
         moved,
         dense,
-        turned,
         layer_one,
         padded,
         labels.reshape(nodes, 1),

time: 152 us -> 150 us (0.987)
  Pallas kernels: 42.4 us -> 37.5 us
  waiting for transfers between devices: 58.2 us -> 61.9 us
    all_to_all x1, waiting for transfers between devices: 25.1 us -> 28.8 us  [on_device(): lax.all_to_all(found, AXES, split_axis=0, concat_axis=0, tiled=True)]
    pallas_call x1, Pallas kernels: 19.7 us -> 17 us  [on_device(): pl.pallas_call(partial(train, classes=classes), out_shape=[jax.ShapeDtype...]
    pallas_call x1, Pallas kernels: 9.48 us -> 7.28 us  [on_device(): call(build_spread, [jax.ShapeDtypeStruct((nodes, nodes), bf), jax.ShapeDt...]
    unnamed x20 -> x18, local copies, waits for them, and re-layouts: 5.89 us -> 4.57 us
  transfers between devices with their start and end apart: 15 -> 15, of which waited for: 14 -> 14; matrix products, arithmetic and copies ran while one was open for 1% -> 1% of each run, Pallas kernels for 7% -> 6%
where the time goes in v7:
time: 150 us; the launch traced here: 149 us
  waiting for transfers between devices  61.9 us (41%)
  Pallas kernels  37.5 us (25%)
  blocking collectives  21.9 us (15%)
  starting transfers between devices  20 us (13%)
  local copies, waits for them, and re-layouts  6.45 us (4%)
  between operations  1.61 us (1%)
    all_to_all x1, waiting for transfers between devices, on_device(): lax.all_to_all(found, AXES, split_axis=0, concat_axis=0, tiled=True)  28.8 us
    all_to_all x1, blocking collectives, on_device(): lax.all_to_all(requests, AXES, split_axis=0, concat_axis=0, tiled=True)  21.9 us
    pallas_call x1, Pallas kernels, on_device(): pl.pallas_call(partial(train, classes=classes), out_shape=[jax.ShapeDtype...  17 us
    ppermute x6, waiting for transfers between devices, sum_over_devices(): got = [lax.ppermute(total, AXES, shift_pairs(axes, k)) for k in (1, 2, 3)]  15.8 us
    ppermute x3, waiting for transfers between devices, sum_over_devices(): got = [lax.ppermute(total, AXES, shift_pairs(FIRST, k)) for k in (1, 2, 3)]  8.58 us
    pallas_call x1, Pallas kernels, on_device(): call(build_spread, [jax.ShapeDtypeStruct((nodes, nodes), bf), jax.ShapeDt...  7.28 us
    ppermute x3, waiting for transfers between devices, sum_over_devices(): lax.ppermute(part, AXES, shift_pairs(FIRST, k + 1))  6.79 us
    pallas_call x1, Pallas kernels, on_device(): pl.pallas_call(fetch_rows, out_shape=jax.ShapeDtypeStruct((slots, width),...  6.48 us
  transfers between devices with their start and end apart: 15, of which 14 were waited for; matrix products, arithmetic and copies ran while one was open for 1% of the time, Pallas kernels for 6%

profile of v7, /device:TPU:1, one launch (start us, length us, event | category | flops | bytes accessed | tf_op | source)
XLA Modules:
  0.0 149.3 jit_solution(11206764390636322773)
XLA Ops:
  0.6 1.8 %shard_map.121 = (s32[128,16]{1,0:T(8,128)}, s32[1,1024]{1,0:T(1,128)}) custom-call(s32[1,1024]{1,0:T(1,128)} %bitcast.20, s32[1,1024]{1,0:T(1,128)} %bitcast.21), custom_call_target="tpu_custom_call" | custom-call | tf_op jit(solution)/shard_map/pallas_call | solution.py:484
  2.5 21.9 %all_to_all.22 = s32[128,1,16]{2,1,0:T(1,128)} all-to-all(s32[128,1,16]{2,1,0:T(1,128)} %bitcast.18), channel_id=1, replica_groups=mesh['store'=32,'batch'=4] {'store','batch'}, dimensions={0} | all-to-all | bytes 16384 | tf_op jit(solution)/shard_map/all_to_all | solution.py:494
  24.3 6.5 %shard_map.122 = bf16[2048,768]{1,0:T(8,128)(2,1)} custom-call(s32[128,16]{1,0:T(8,128)} %bitcast.17, bf16[4096,768]{1,0:T(8,128)(2,1)} %table.1), custom_call_target="tpu_custom_call" | custom-call | tf_op jit(solution)/shard_map/pallas_call | solution.py:498
  30.8 0.0 copy-start.8
  30.9 0.0 copy-start.7
  30.9 0.0 copy-start.1
  30.9 0.0 copy-start.2
  30.9 0.0 copy-start.3
  30.9 0.0 copy-start.4
  30.9 4.8 %all-to-all-start.1 = ((bf16[128,16,768]{2,1,0:T(8,128)(2,1)}), bf16[128,16,768]{2,1,0:T(8,128)(2,1)}, u32[]{:S(2)}, u32[]{:S(2)}) async-start(bf16[128,16,768]{2,1,0:T(8,128)(2,1)} %bitcast.14), calls=%async_computation.1 | async-start | bytes 6291456 | tf_op jit(solution)/shard_map/all_to_all | solution.py:515
  36.4 0.0 copy-done.8
  36.4 1.0 copy.17.labels_far
  37.4 0.0 copy-done.7
  37.4 0.8 pad.4.two_far
  38.3 0.0 copy-done.1
  38.3 0.0 copy-done.2
  38.3 0.0 copy-done.3
  38.3 0.0 copy-done.4
  38.3 7.3 %shard_map.123 = (bf16[1024,1024]{1,0:T(8,128)(2,1)S(1)}, bf16[1024,2048]{1,0:T(8,128)(2,1)S(1)}) custom-call(s32[48]{0:T(128)S(1)} %copy-done.3, s32[48]{0:T(128)S(1)} %copy-done.4, s32[1]{0:T(128)S(6)} %copy.20.count, bf16[48,128,128]{2,1,0:T(8,128)(2,1)S(1)} %copy-done.1, s32[1,1024]{1,0:T(1,128)S(1)} %copy-done.2), custom_call_target="tpu_custom_call" | custom-call | flops 4294967296 | bytes 12582912 | tf_op jit(solution)/shard_map/pallas_call | solution.py:516
  45.6 0.0 copy-start.5
  45.6 1.9 %copy-done.5 = bf16[1024,2048]{1,0:T(8,128)(2,1)} copy-done((bf16[1024,2048]{1,0:T(8,128)(2,1)}, bf16[1024,2048]{1,0:T(8,128)(2,1)S(1)}, u32[]{:S(2)}) %copy-start.5) | copy-done | bytes 4194328
  47.5 0.0 copy-start.6
  47.5 1.4 copy-done.6
  48.9 28.8 %all-to-all-done.1 = bf16[128,16,768]{2,1,0:T(8,128)(2,1)} async-done(((bf16[128,16,768]{2,1,0:T(8,128)(2,1)}), bf16[128,16,768]{2,1,0:T(8,128)(2,1)}, u32[]{:S(2)}, u32[]{:S(2)}) %all-to-all-start.1) | async-done | bytes 3145760 | tf_op jit(solution)/shard_map/all_to_all | solution.py:515
  77.7 17.0 %shard_map.124 = (bf16[928,512]{1,0:T(8,128)(2,1)}, bf16[928,512]{1,0:T(8,128)(2,1)}) custom-call(s32[1]{0:T(128)} %bitcast.core, bf16[2048,768]{1,0:T(8,128)(2,1)} %bitcast.8.arrived_far, bf16[1024,2048]{1,0:T(8,128)(2,1)} %copy-done.5, bf16[1024,1024]{1,0:T(8,128)(2,1)} %copy-done.6, bf16[768,1024]{1,0:T(8,128)(2,1)} %one_far.1, ...), custom_call_target="tpu_custom_call" | custom-call | flops 12884901888 | bytes 16777216 | tf_op jit(solution)/shard_map/pallas_call | solution.py:531
  94.7 0.6 collective-permute-start
  95.3 0.0 copy-start
  95.3 1.2 copy-done
  96.5 0.2 shard_map.125.own
  96.7 1.0 collective-permute-done.arrived
  97.7 0.5 shard_map.126
  98.2 0.4 collective-permute-start.1
  98.6 2.0 %collective-permute-start.2 = (bf16[928,128]{1,0:T(8,128)(2,1)S(1)}, bf16[928,128]{1,0:T(8,128)(2,1)S(1)}, u32[]{:S(2)}, u32[]{:S(2)}) collective-permute-start(bf16[928,128]{1,0:T(8,128)(2,1)S(1)} %get-tuple-element.26), channel_id=1, source_target_pairs={{0,64},{4,6},{8,72},{12,14},{16,80},{20,22},{24,88},{28,30},{1,65}... | collective-permute-start | bytes 712712 | tf_op jit(solution)/shard_map/ppermute | solution.py:173
  100.6 0.5 collective-permute-start.3
  101.1 6.2 %collective-permute-done.1.one = bf16[928,128]{1,0:T(8,128)(2,1)S(1)} collective-permute-done((bf16[928,128]{1,0:T(8,128)(2,1)S(1)}, bf16[928,128]{1,0:T(8,128)(2,1)S(1)}, u32[]{:S(2)}, u32[]{:S(2)}) %collective-permute-start.1) | collective-permute-done | bytes 237600 | tf_op jit(solution)/shard_map/ppermute | solution.py:173
  107.3 0.0 collective-permute-done.2.two
  107.3 0.6 collective-permute-done.3.three
  107.9 0.3 shard_map.127.own
  108.2 0.1 collective-permute-start.6
  108.3 1.6 %collective-permute-start.5 = (bf16[928,128]{1,0:T(8,128)(2,1)S(1)}, bf16[928,128]{1,0:T(8,128)(2,1)S(1)}, u32[]{:S(2)}, u32[]{:S(2)}) collective-permute-start(bf16[928,128]{1,0:T(8,128)(2,1)S(1)} %shard_map.127.own), channel_id=1, source_target_pairs={{0,2},{4,20},{8,10},{12,28},{16,18},{20,4},{24,26},{28,12},{1,3},{... | collective-permute-start | bytes 712712 | tf_op jit(solution)/shard_map/ppermute | solution.py:176
  109.9 0.0 collective-permute-start.4
  109.9 3.5 %collective-permute-done.6.three = bf16[928,128]{1,0:T(8,128)(2,1)S(1)} collective-permute-done((bf16[928,128]{1,0:T(8,128)(2,1)S(1)}, bf16[928,128]{1,0:T(8,128)(2,1)S(1)}, u32[]{:S(2)}, u32[]{:S(2)}) %collective-permute-start.6) | collective-permute-done | bytes 237600 | tf_op jit(solution)/shard_map/ppermute | solution.py:176
  113.5 1.4 collective-permute-done.5.two
  114.9 2.7 %collective-permute-done.4.one = bf16[928,128]{1,0:T(8,128)(2,1)S(1)} collective-permute-done((bf16[928,128]{1,0:T(8,128)(2,1)S(1)}, bf16[928,128]{1,0:T(8,128)(2,1)S(1)}, u32[]{:S(2)}, u32[]{:S(2)}) %collective-permute-start.4) | collective-permute-done | bytes 237600 | tf_op jit(solution)/shard_map/ppermute | solution.py:176
  117.6 0.3 shard_map.128.own
  117.9 0.9 collective-permute-start.9
  118.8 1.2 collective-permute-start.8
  120.0 0.0 collective-permute-start.7
  120.0 2.9 %collective-permute-done.9.three = bf16[928,128]{1,0:T(8,128)(2,1)S(1)} collective-permute-done((bf16[928,128]{1,0:T(8,128)(2,1)S(1)}, bf16[928,128]{1,0:T(8,128)(2,1)S(1)}, u32[]{:S(2)}, u32[]{:S(2)}) %collective-permute-start.9) | collective-permute-done | bytes 237600 | tf_op jit(solution)/shard_map/ppermute | solution.py:176
  122.9 2.5 %collective-permute-done.8.two = bf16[928,128]{1,0:T(8,128)(2,1)S(1)} collective-permute-done((bf16[928,128]{1,0:T(8,128)(2,1)S(1)}, bf16[928,128]{1,0:T(8,128)(2,1)S(1)}, u32[]{:S(2)}, u32[]{:S(2)}) %collective-permute-start.8) | collective-permute-done | bytes 237600 | tf_op jit(solution)/shard_map/ppermute | solution.py:176
  125.4 2.7 %collective-permute-done.7.one = bf16[928,128]{1,0:T(8,128)(2,1)S(1)} collective-permute-done((bf16[928,128]{1,0:T(8,128)(2,1)S(1)}, bf16[928,128]{1,0:T(8,128)(2,1)S(1)}, u32[]{:S(2)}, u32[]{:S(2)}) %collective-permute-start.7) | collective-permute-done | bytes 237600 | tf_op jit(solution)/shard_map/ppermute | solution.py:176
  128.1 0.3 shard_map.129.own
  128.4 2.4 %collective-permute-start.12 = (bf16[928,128]{1,0:T(8,128)(2,1)S(1)}, bf16[928,128]{1,0:T(8,128)(2,1)S(1)}, u32[]{:S(2)}, u32[]{:S(2)}) collective-permute-start(bf16[928,128]{1,0:T(8,128)(2,1)S(1)} %shard_map.129.own), channel_id=1, source_target_pairs={{0,96},{4,7},{8,104},{12,15},{16,112},{20,23},{24,120},{28,31},{1,... | collective-permute-start | bytes 712712 | tf_op jit(solution)/shard_map/ppermute | solution.py:178
  130.8 0.2 collective-permute-start.11
  131.0 0.4 collective-permute-start.10
  131.5 4.9 %collective-permute-done.12.three = bf16[928,128]{1,0:T(8,128)(2,1)S(1)} collective-permute-done((bf16[928,128]{1,0:T(8,128)(2,1)S(1)}, bf16[928,128]{1,0:T(8,128)(2,1)S(1)}, u32[]{:S(2)}, u32[]{:S(2)}) %collective-permute-start.12) | collective-permute-done | bytes 237600 | tf_op jit(solution)/shard_map/ppermute | solution.py:178
  136.4 1.0 collective-permute-done.11.two
  137.3 2.7 %collective-permute-done.10.one = bf16[928,128]{1,0:T(8,128)(2,1)S(1)} collective-permute-done((bf16[928,128]{1,0:T(8,128)(2,1)S(1)}, bf16[928,128]{1,0:T(8,128)(2,1)S(1)}, u32[]{:S(2)}, u32[]{:S(2)}) %collective-permute-start.10) | collective-permute-done | bytes 237600 | tf_op jit(solution)/shard_map/ppermute | solution.py:178
  140.0 0.3 shard_map.130.own
  140.3 4.9 %collective-permute-start.13 = (bf16[928,512]{1,0:T(8,128)(2,1)S(1)}, bf16[928,512]{1,0:T(8,128)(2,1)S(1)}, u32[]{:S(2)}, u32[]{:S(2)}) collective-permute-start(bf16[928,512]{1,0:T(8,128)(2,1)S(1)} %shard_map.130.own), channel_id=1, source_target_pairs={{0,4},{4,0},{8,12},{12,8},{16,20},{20,16},{24,28},{28,24},{1,5},{5... | collective-permute-start | bytes 2850824 | tf_op jit(solution)/shard_map/ppermute | solution.py:182
  145.2 1.3 shard_map.131
  146.5 0.8 collective-permute-done.13.other
  147.3 1.8 %shard_map.132 = (f32[768,1024]{1,0:T(8,128)}, f32[153,1024]{1,0:T(8,128)}, f32[1,1]{1,0:T(1,128)}) custom-call(s32[1]{0:T(128)} %bitcast.core, bf16[928,512]{1,0:T(8,128)(2,1)S(1)} %shard_map.130.own, bf16[928,512]{1,0:T(8,128)(2,1)S(1)} %collective-permute-done.13.other, ...), custom_call_target="tpu_custom_call", output_to_operand_aliasing={{0}: (3, {}), {1}: (4, {})} | custom-call | tf_op jit(solution)/shard_map/pallas_call | solution.py:205
Async XLA Ops:
  30.8 5.6 %copy-start.8 = (s32[1024]{0:T(1024)S(1)}, s32[1024]{0:T(1024)}, u32[]{:S(2)}) copy-start(s32[1024]{0:T(1024)} %param.17) | copy-start | bytes 12292
  30.9 6.6 %copy-start.7 = (bf16[1024,153]{0,1:T(8,128)(2,1)S(1)}, bf16[1024,153]{0,1:T(8,128)(2,1)}, u32[]{:S(2)}) copy-start(bf16[1024,153]{0,1:T(8,128)(2,1)} %param.19) | copy-start | bytes 940036
  30.9 7.4 %copy-start.1 = (bf16[48,128,128]{2,1,0:T(8,128)(2,1)S(1)}, bf16[48,128,128]{2,1,0:T(8,128)(2,1)}, u32[]{:S(2)}) copy-start(bf16[48,128,128]{2,1,0:T(8,128)(2,1)} %tiles.1) | copy-start | bytes 4718596
  30.9 7.4 %copy-start.2 = (s32[1,1024]{1,0:T(1,128)S(1)}, s32[1,1024]{1,0:T(1,128)}, u32[]{:S(2)}) copy-start(s32[1,1024]{1,0:T(1,128)} %get-tuple-element.19.position) | copy-start | bytes 12292
  30.9 7.4 %copy-start.3 = (s32[48]{0:T(128)S(1)}, s32[48]{0:T(128)}, u32[]{:S(2)}) copy-start(s32[48]{0:T(128)} %row.1) | copy-start | bytes 580
  30.9 7.4 %copy-start.4 = (s32[48]{0:T(128)S(1)}, s32[48]{0:T(128)}, u32[]{:S(2)}) copy-start(s32[48]{0:T(128)} %column.1) | copy-start | bytes 580
  30.9 46.8 %all-to-all-start.1 = ((bf16[128,16,768]{2,1,0:T(8,128)(2,1)}), bf16[128,16,768]{2,1,0:T(8,128)(2,1)}, u32[]{:S(2)}, u32[]{:S(2)}) async-start(bf16[128,16,768]{2,1,0:T(8,128)(2,1)} %bitcast.14), calls=%async_computation.1 | async-start | bytes 6291456 | tf_op jit(solution)/shard_map/all_to_all | solution.py:515
  45.6 2.0 %copy-start.5 = (bf16[1024,2048]{1,0:T(8,128)(2,1)}, bf16[1024,2048]{1,0:T(8,128)(2,1)S(1)}, u32[]{:S(2)}) copy-start(bf16[1024,2048]{1,0:T(8,128)(2,1)S(1)} %get-tuple-element.20.moved_far) | copy-start | bytes 12582916
  47.5 1.4 copy-start.6
  94.7 3.0 %collective-permute-start = (bf16[928,512]{1,0:T(8,128)(2,1)}, bf16[928,512]{1,0:T(8,128)(2,1)S(1)}, u32[]{:S(2)}, u32[]{:S(2)}) collective-permute-start(bf16[928,512]{1,0:T(8,128)(2,1)} %get-tuple-element.23), channel_id=1, source_target_pairs={{0,4},{4,0},{8,12},{12,8},{16,20},{20,16},{24,28},{28,24},{1,5},{5... | collective-permute-start | bytes 2850824 | tf_op jit(solution)/shard_map/ppermute | solution.py:163
  95.3 1.2 copy-start
  98.2 9.1 %collective-permute-start.1 = (bf16[928,128]{1,0:T(8,128)(2,1)S(1)}, bf16[928,128]{1,0:T(8,128)(2,1)S(1)}, u32[]{:S(2)}, u32[]{:S(2)}) collective-permute-start(bf16[928,128]{1,0:T(8,128)(2,1)S(1)} %get-tuple-element.25), channel_id=1, source_target_pairs={{0,32},{4,5},{8,40},{12,13},{16,48},{20,21},{24,56},{28,29},{1,33}... | collective-permute-start | bytes 712712 | tf_op jit(solution)/shard_map/ppermute | solution.py:173
  98.6 8.7 %collective-permute-start.2 = (bf16[928,128]{1,0:T(8,128)(2,1)S(1)}, bf16[928,128]{1,0:T(8,128)(2,1)S(1)}, u32[]{:S(2)}, u32[]{:S(2)}) collective-permute-start(bf16[928,128]{1,0:T(8,128)(2,1)S(1)} %get-tuple-element.26), channel_id=1, source_target_pairs={{0,64},{4,6},{8,72},{12,14},{16,80},{20,22},{24,88},{28,30},{1,65}... | collective-permute-start | bytes 712712 | tf_op jit(solution)/shard_map/ppermute | solution.py:173
  100.6 7.3 %collective-permute-start.3 = (bf16[928,128]{1,0:T(8,128)(2,1)S(1)}, bf16[928,128]{1,0:T(8,128)(2,1)S(1)}, u32[]{:S(2)}, u32[]{:S(2)}) collective-permute-start(bf16[928,128]{1,0:T(8,128)(2,1)S(1)} %get-tuple-element.27), channel_id=1, source_target_pairs={{0,96},{4,7},{8,104},{12,15},{16,112},{20,23},{24,120},{28,31},{1,... | collective-permute-start | bytes 712712 | tf_op jit(solution)/shard_map/ppermute | solution.py:173
  108.2 5.3 %collective-permute-start.6 = (bf16[928,128]{1,0:T(8,128)(2,1)S(1)}, bf16[928,128]{1,0:T(8,128)(2,1)S(1)}, u32[]{:S(2)}, u32[]{:S(2)}) collective-permute-start(bf16[928,128]{1,0:T(8,128)(2,1)S(1)} %shard_map.127.own), channel_id=1, source_target_pairs={{0,3},{4,28},{8,11},{12,4},{16,19},{20,12},{24,27},{28,20},{1,0},{... | collective-permute-start | bytes 712712 | tf_op jit(solution)/shard_map/ppermute | solution.py:176
  108.3 6.6 %collective-permute-start.5 = (bf16[928,128]{1,0:T(8,128)(2,1)S(1)}, bf16[928,128]{1,0:T(8,128)(2,1)S(1)}, u32[]{:S(2)}, u32[]{:S(2)}) collective-permute-start(bf16[928,128]{1,0:T(8,128)(2,1)S(1)} %shard_map.127.own), channel_id=1, source_target_pairs={{0,2},{4,20},{8,10},{12,28},{16,18},{20,4},{24,26},{28,12},{1,3},{... | collective-permute-start | bytes 712712 | tf_op jit(solution)/shard_map/ppermute | solution.py:176
  109.9 7.7 %collective-permute-start.4 = (bf16[928,128]{1,0:T(8,128)(2,1)S(1)}, bf16[928,128]{1,0:T(8,128)(2,1)S(1)}, u32[]{:S(2)}, u32[]{:S(2)}) collective-permute-start(bf16[928,128]{1,0:T(8,128)(2,1)S(1)} %shard_map.127.own), channel_id=1, source_target_pairs={{0,1},{4,12},{8,9},{12,20},{16,17},{20,28},{24,25},{28,4},{1,2},{5... | collective-permute-start | bytes 712712 | tf_op jit(solution)/shard_map/ppermute | solution.py:176
  117.9 5.0 %collective-permute-start.9 = (bf16[928,128]{1,0:T(8,128)(2,1)S(1)}, bf16[928,128]{1,0:T(8,128)(2,1)S(1)}, u32[]{:S(2)}, u32[]{:S(2)}) collective-permute-start(bf16[928,128]{1,0:T(8,128)(2,1)S(1)} %shard_map.128.own), channel_id=1, source_target_pairs={{0,24},{4,100},{8,0},{12,108},{16,8},{20,116},{24,16},{28,124},{1,... | collective-permute-start | bytes 712712 | tf_op jit(solution)/shard_map/ppermute | solution.py:176
  118.8 6.6 %collective-permute-start.8 = (bf16[928,128]{1,0:T(8,128)(2,1)S(1)}, bf16[928,128]{1,0:T(8,128)(2,1)S(1)}, u32[]{:S(2)}, u32[]{:S(2)}) collective-permute-start(bf16[928,128]{1,0:T(8,128)(2,1)S(1)} %shard_map.128.own), channel_id=1, source_target_pairs={{0,16},{4,68},{8,24},{12,76},{16,0},{20,84},{24,8},{28,92},{1,17},... | collective-permute-start | bytes 712712 | tf_op jit(solution)/shard_map/ppermute | solution.py:176
  120.0 8.1 %collective-permute-start.7 = (bf16[928,128]{1,0:T(8,128)(2,1)S(1)}, bf16[928,128]{1,0:T(8,128)(2,1)S(1)}, u32[]{:S(2)}, u32[]{:S(2)}) collective-permute-start(bf16[928,128]{1,0:T(8,128)(2,1)S(1)} %shard_map.128.own), channel_id=1, source_target_pairs={{0,8},{4,36},{8,16},{12,44},{16,24},{20,52},{24,0},{28,60},{1,9},{... | collective-permute-start | bytes 712712 | tf_op jit(solution)/shard_map/ppermute | solution.py:176
  128.4 8.0 %collective-permute-start.12 = (bf16[928,128]{1,0:T(8,128)(2,1)S(1)}, bf16[928,128]{1,0:T(8,128)(2,1)S(1)}, u32[]{:S(2)}, u32[]{:S(2)}) collective-permute-start(bf16[928,128]{1,0:T(8,128)(2,1)S(1)} %shard_map.129.own), channel_id=1, source_target_pairs={{0,96},{4,7},{8,104},{12,15},{16,112},{20,23},{24,120},{28,31},{1,... | collective-permute-start | bytes 712712 | tf_op jit(solution)/shard_map/ppermute | solution.py:178
  130.8 6.6 %collective-permute-start.11 = (bf16[928,128]{1,0:T(8,128)(2,1)S(1)}, bf16[928,128]{1,0:T(8,128)(2,1)S(1)}, u32[]{:S(2)}, u32[]{:S(2)}) collective-permute-start(bf16[928,128]{1,0:T(8,128)(2,1)S(1)} %shard_map.129.own), channel_id=1, source_target_pairs={{0,64},{4,6},{8,72},{12,14},{16,80},{20,22},{24,88},{28,30},{1,65}... | collective-permute-start | bytes 712712 | tf_op jit(solution)/shard_map/ppermute | solution.py:178
  131.0 9.0 %collective-permute-start.10 = (bf16[928,128]{1,0:T(8,128)(2,1)S(1)}, bf16[928,128]{1,0:T(8,128)(2,1)S(1)}, u32[]{:S(2)}, u32[]{:S(2)}) collective-permute-start(bf16[928,128]{1,0:T(8,128)(2,1)S(1)} %shard_map.129.own), channel_id=1, source_target_pairs={{0,32},{4,5},{8,40},{12,13},{16,48},{20,21},{24,56},{28,29},{1,33}... | collective-permute-start | bytes 712712 | tf_op jit(solution)/shard_map/ppermute | solution.py:178
  140.3 7.0 %collective-permute-start.13 = (bf16[928,512]{1,0:T(8,128)(2,1)S(1)}, bf16[928,512]{1,0:T(8,128)(2,1)S(1)}, u32[]{:S(2)}, u32[]{:S(2)}) collective-permute-start(bf16[928,512]{1,0:T(8,128)(2,1)S(1)} %shard_map.130.own), channel_id=1, source_target_pairs={{0,4},{4,0},{8,12},{12,8},{16,20},{20,16},{24,28},{28,24},{1,5},{5... | collective-permute-start | bytes 2850824 | tf_op jit(solution)/shard_map/ppermute | solution.py:182

commit v8 on v7

--- a/solution.py
+++ b/solution.py
@@ -63,24 +63,11 @@
     out[ROWS - 16 :, columns] = last.astype(jnp.bfloat16)
 
 
-def pick_blocks(place, far, near, arrival):
-    copies = []
-    for index, offset in enumerate((1, 2, 3, 0)):
+def first_add(place, own, arrived, keep, one, two, three):
+    for offset, out in ((1, one), (2, two), (3, three), (0, keep)):
         block = lax.rem(place[0] + offset, SIDE)
         columns = pl.ds(pl.multiple_of(block * WIDTH, WIDTH), WIDTH)
-        copies.append(
-            pltpu.make_async_copy(far.at[:, columns], near.at[index], arrival.at[index])
-        )
-        copies[-1].start()
-    for copy in copies:
-        copy.wait()
-
-
-def first_add(place, own, arrived, keep, one, two, three):
-    for index, (offset, out) in enumerate(((1, one), (2, two), (3, three), (0, keep))):
-        block = lax.rem(place[0] + offset, SIDE)
-        columns = pl.ds(pl.multiple_of(block * WIDTH, WIDTH), WIDTH)
-        total = own[index].astype(jnp.float32) + arrived[:, columns].astype(jnp.float32)
+        total = own[:, columns].astype(jnp.float32) + arrived[:, columns].astype(jnp.float32)
         store_total(out, slice(None), total)
 
 
@@ -161,15 +148,7 @@
     bf = jnp.bfloat16
     block = jax.ShapeDtypeStruct((ROWS, WIDTH), bf)
     arrived = lax.ppermute(sent, AXES, swap_pairs())
-    picked = pl.pallas_call(
-        pick_blocks,
-        out_shape=jax.ShapeDtypeStruct((SIDE, ROWS, WIDTH), bf),
-        in_specs=[pl.BlockSpec(memory_space=pltpu.SMEM), pl.BlockSpec(memory_space=pl.ANY)],
-        out_specs=pl.BlockSpec(memory_space=pltpu.VMEM),
-        scratch_shapes=[pltpu.SemaphoreType.DMA((SIDE,))],
-        compiler_params=pltpu.CompilerParams(vmem_limit_bytes=16 << 20),
-    )(place, own)
-    keep, *parts = call(first_add, [block] * 4, 1, 2)(place, picked, arrived)
+    keep, *parts = call(first_add, [block] * 4, 1, 2)(place, own, arrived)
     got = [lax.ppermute(part, AXES, shift_pairs(FIRST, k + 1)) for k, part in enumerate(parts)]
     total = call(four_add, block, 0, 4)(keep, *got)
     for axes in (SECOND, THIRD):
@@ -330,16 +309,14 @@
     one_far,
     two_far,
     labels_far,
-    sent_far,
-    own_far,
+    sent,
+    own,
     arrived,
     moved,
     dense,
     layer_one,
     layer_two,
     labels,
-    sent,
-    own,
     mixed_turned,
     slope,
     hidden,
@@ -347,7 +324,6 @@
     upstream_turned,
     back_turned,
     arrival,
-    leaving,
     *,
     classes,
 ):
@@ -437,8 +413,7 @@
         upstream_turned[...], dense[...], preferred_element_type=jnp.float32
     ).astype(jnp.bfloat16)
     back = back_turned[...].T
-    stores = []
-    for offset, out, far in ((1, sent, sent_far), (0, own, own_far)):
+    for offset, out in ((1, sent), (0, own)):
         side = lax.rem(core[0] + offset, 2)
         columns = pl.ds(pl.multiple_of(side * half, half), half)
         second = jnp.dot(
@@ -456,10 +431,6 @@
         out[:features, :] = jnp.dot(
             mixed_turned[...], back_before, preferred_element_type=jnp.float32
         ).astype(out.dtype)
-        stores.append(pltpu.make_async_copy(out, far, leaving.at[len(stores)]))
-        stores[-1].start()
-    for copy in stores:
-        copy.wait()
 
 
 def on_device(
@@ -535,7 +506,7 @@
             jax.ShapeDtypeStruct((ROWS, half), bf),
         ],
         in_specs=[smem] + [anywhere] * 6,
-        out_specs=[anywhere] * 2,
+        out_specs=[vmem] * 2,
         scratch_shapes=[
             pltpu.VMEM((slots, width), bf),
             pltpu.VMEM((nodes, slots), bf),
@@ -543,8 +514,6 @@
             pltpu.VMEM((width, hidden), bf),
             pltpu.VMEM((256, hidden), bf),
             pltpu.VMEM((nodes, 1), jnp.int32),
-            pltpu.VMEM((ROWS, half), bf),
-            pltpu.VMEM((ROWS, half), bf),
             pltpu.VMEM((width, nodes), bf),
             pltpu.VMEM((nodes, hidden), jnp.float32),
             pltpu.VMEM((nodes, hidden), bf),
@@ -552,9 +521,8 @@
             pltpu.VMEM((256, nodes), bf),
             pltpu.VMEM((256, nodes), bf),
             pltpu.SemaphoreType.DMA((12,)),
-            pltpu.SemaphoreType.DMA((2,)),
         ],
-        compiler_params=pltpu.CompilerParams(vmem_limit_bytes=56 << 20),
+        compiler_params=pltpu.CompilerParams(vmem_limit_bytes=50 << 20),
         cost_estimate=pl.CostEstimate(
             flops=12 * nodes * nodes * hidden, bytes_accessed=16 << 20, transcendentals=nodes * hidden
         ),

time: 150 us -> 149 us (level)
  waiting for transfers between devices: 61.9 us -> 63.6 us
    unnamed x18 -> x16, local copies, waits for them, and re-layouts: 4.57 us -> 4.79 us
  transfers between devices with their start and end apart: 15 -> 15, of which waited for: 14 -> 14; matrix products, arithmetic and copies ran while one was open for 1% -> 0% of each run, Pallas kernels for 6% -> 6%
where the time goes in v8:
time: 149 us; the launch traced here: 148 us
  waiting for transfers between devices  63.6 us (43%)
  Pallas kernels  36.4 us (24%)
  blocking collectives  21.7 us (15%)
  starting transfers between devices  19.9 us (13%)
  local copies, waits for them, and re-layouts  5.05 us (3%)
  between operations  1.64 us (1%)
    all_to_all x1, waiting for transfers between devices, on_device(): lax.all_to_all(found, AXES, split_axis=0, concat_axis=0, tiled=True)  29.3 us
    all_to_all x1, blocking collectives, on_device(): lax.all_to_all(requests, AXES, split_axis=0, concat_axis=0, tiled=True)  21.7 us
    pallas_call x1, Pallas kernels, on_device(): pl.pallas_call(partial(train, classes=classes), out_shape=[jax.ShapeDtype...  16.2 us
    ppermute x6, waiting for transfers between devices, sum_over_devices(): got = [lax.ppermute(total, AXES, shift_pairs(axes, k)) for k in (1, 2, 3)]  15.9 us
    ppermute x3, waiting for transfers between devices, sum_over_devices(): got = [lax.ppermute(total, AXES, shift_pairs(FIRST, k)) for k in (1, 2, 3)]  8.61 us
    pallas_call x1, Pallas kernels, on_device(): call(build_spread, [jax.ShapeDtypeStruct((nodes, nodes), bf), jax.ShapeDt...  7.03 us
    ppermute x3, waiting for transfers between devices, sum_over_devices(): lax.ppermute(part, AXES, shift_pairs(FIRST, k + 1))  6.8 us
    pallas_call x1, Pallas kernels, on_device(): pl.pallas_call(fetch_rows, out_shape=jax.ShapeDtypeStruct((slots, width),...  6.48 us
  transfers between devices with their start and end apart: 15, of which 14 were waited for; matrix products, arithmetic and copies ran while one was open for 0% of the time, Pallas kernels for 6%

profile of v8, /device:TPU:1, one launch (start us, length us, event | category | flops | bytes accessed | tf_op | source)
XLA Modules:
  0.0 148.3 jit_solution(16550166583333652034)
XLA Ops:
  0.6 1.8 %shard_map.121 = (s32[128,16]{1,0:T(8,128)}, s32[1,1024]{1,0:T(1,128)}) custom-call(s32[1,1024]{1,0:T(1,128)} %bitcast.20, s32[1,1024]{1,0:T(1,128)} %bitcast.21), custom_call_target="tpu_custom_call" | custom-call | tf_op jit(solution)/shard_map/pallas_call | solution.py:455
  2.5 21.7 %all_to_all.22 = s32[128,1,16]{2,1,0:T(1,128)} all-to-all(s32[128,1,16]{2,1,0:T(1,128)} %bitcast.18), channel_id=1, replica_groups=mesh['store'=32,'batch'=4] {'store','batch'}, dimensions={0} | all-to-all | bytes 16384 | tf_op jit(solution)/shard_map/all_to_all | solution.py:465
  24.2 6.5 %shard_map.122 = bf16[2048,768]{1,0:T(8,128)(2,1)} custom-call(s32[128,16]{1,0:T(8,128)} %bitcast.17, bf16[4096,768]{1,0:T(8,128)(2,1)} %table.1), custom_call_target="tpu_custom_call" | custom-call | tf_op jit(solution)/shard_map/pallas_call | solution.py:469
  30.7 0.0 copy-start.7
  30.7 0.0 copy-start.6
  30.7 0.0 copy-start.1
  30.7 0.0 copy-start.2
  30.7 0.0 copy-start.3
  30.7 5.0 %all-to-all-start.1 = ((bf16[128,16,768]{2,1,0:T(8,128)(2,1)}), bf16[128,16,768]{2,1,0:T(8,128)(2,1)}, u32[]{:S(2)}, u32[]{:S(2)}) async-start(bf16[128,16,768]{2,1,0:T(8,128)(2,1)} %bitcast.14), calls=%async_computation.1 | async-start | bytes 6291456 | tf_op jit(solution)/shard_map/all_to_all | solution.py:486
  36.4 0.0 copy-done.7
  36.4 0.2 copy.17.labels_far
  36.6 0.0 copy-done.6
  36.7 0.0 copy-done.1
  36.7 0.0 copy-done.2
  36.7 0.0 copy-done.3
  36.7 0.0 copy-start
  36.7 1.4 copy-done
  38.1 7.0 %shard_map.123 = (bf16[1024,1024]{1,0:T(8,128)(2,1)S(1)}, bf16[1024,2048]{1,0:T(8,128)(2,1)S(1)}) custom-call(s32[48]{0:T(128)S(1)} %copy-done.2, s32[48]{0:T(128)S(1)} %copy-done.3, s32[1]{0:T(128)S(6)} %copy.20.count, bf16[48,128,128]{2,1,0:T(8,128)(2,1)S(1)} %copy-done, s32[1,1024]{1,0:T(1,128)S(1)} %copy-done.1), custom_call_target="tpu_custom_call" | custom-call | flops 4294967296 | bytes 12582912 | tf_op jit(solution)/shard_map/pallas_call | solution.py:487
  45.2 0.0 copy-start.4
  45.2 1.9 %copy-done.4 = bf16[1024,2048]{1,0:T(8,128)(2,1)} copy-done((bf16[1024,2048]{1,0:T(8,128)(2,1)}, bf16[1024,2048]{1,0:T(8,128)(2,1)S(1)}, u32[]{:S(2)}) %copy-start.4) | copy-done | bytes 4194328
  47.1 0.0 copy-start.5
  47.1 1.4 copy-done.5
  48.5 29.3 %all-to-all-done.1 = bf16[128,16,768]{2,1,0:T(8,128)(2,1)} async-done(((bf16[128,16,768]{2,1,0:T(8,128)(2,1)}), bf16[128,16,768]{2,1,0:T(8,128)(2,1)}, u32[]{:S(2)}, u32[]{:S(2)}) %all-to-all-start.1) | async-done | bytes 3145760 | tf_op jit(solution)/shard_map/all_to_all | solution.py:486
  77.8 16.2 %shard_map.124 = (bf16[928,512]{1,0:T(8,128)(2,1)S(1)}, bf16[928,512]{1,0:T(8,128)(2,1)S(1)}) custom-call(s32[1]{0:T(128)} %bitcast.core, bf16[2048,768]{1,0:T(8,128)(2,1)} %bitcast.8.arrived_far, bf16[1024,2048]{1,0:T(8,128)(2,1)} %copy-done.4, bf16[1024,1024]{1,0:T(8,128)(2,1)} %copy-done.5, bf16[768,1024]{1,0:T(8,128)(2,1)} %one_far.1, ...), custom_call_target="tpu_custom_call" | custom-call | flops 12884901888 | bytes 16777216 | tf_op jit(solution)/shard_map/pallas_call | solution.py:502
  94.1 0.3 collective-permute-start
  94.4 2.3 %collective-permute-done.arrived = bf16[928,512]{1,0:T(8,128)(2,1)S(1)} collective-permute-done((bf16[928,512]{1,0:T(8,128)(2,1)S(1)}, bf16[928,512]{1,0:T(8,128)(2,1)S(1)}, u32[]{:S(2)}, u32[]{:S(2)}) %collective-permute-start) | collective-permute-done | bytes 950304 | tf_op jit(solution)/shard_map/ppermute | solution.py:150
  96.7 0.5 shard_map.125
  97.2 0.4 collective-permute-start.1
  97.6 2.0 %collective-permute-start.2 = (bf16[928,128]{1,0:T(8,128)(2,1)S(1)}, bf16[928,128]{1,0:T(8,128)(2,1)S(1)}, u32[]{:S(2)}, u32[]{:S(2)}) collective-permute-start(bf16[928,128]{1,0:T(8,128)(2,1)S(1)} %get-tuple-element.26), channel_id=1, source_target_pairs={{0,64},{4,6},{8,72},{12,14},{16,80},{20,22},{24,88},{28,30},{1,65}... | collective-permute-start | bytes 712712 | tf_op jit(solution)/shard_map/ppermute | solution.py:152
  99.6 0.5 collective-permute-start.3
  100.1 6.2 %collective-permute-done.1.one = bf16[928,128]{1,0:T(8,128)(2,1)S(1)} collective-permute-done((bf16[928,128]{1,0:T(8,128)(2,1)S(1)}, bf16[928,128]{1,0:T(8,128)(2,1)S(1)}, u32[]{:S(2)}, u32[]{:S(2)}) %collective-permute-start.1) | collective-permute-done | bytes 237600 | tf_op jit(solution)/shard_map/ppermute | solution.py:152
  106.3 0.0 collective-permute-done.2.two
  106.3 0.6 collective-permute-done.3.three
  106.9 0.3 shard_map.126.own
  107.2 0.1 collective-permute-start.6
  107.3 1.6 %collective-permute-start.5 = (bf16[928,128]{1,0:T(8,128)(2,1)S(1)}, bf16[928,128]{1,0:T(8,128)(2,1)S(1)}, u32[]{:S(2)}, u32[]{:S(2)}) collective-permute-start(bf16[928,128]{1,0:T(8,128)(2,1)S(1)} %shard_map.126.own), channel_id=1, source_target_pairs={{0,2},{4,20},{8,10},{12,28},{16,18},{20,4},{24,26},{28,12},{1,3},{... | collective-permute-start | bytes 712712 | tf_op jit(solution)/shard_map/ppermute | solution.py:155
  108.9 0.0 collective-permute-start.4
  108.9 3.6 %collective-permute-done.6.three = bf16[928,128]{1,0:T(8,128)(2,1)S(1)} collective-permute-done((bf16[928,128]{1,0:T(8,128)(2,1)S(1)}, bf16[928,128]{1,0:T(8,128)(2,1)S(1)}, u32[]{:S(2)}, u32[]{:S(2)}) %collective-permute-start.6) | collective-permute-done | bytes 237600 | tf_op jit(solution)/shard_map/ppermute | solution.py:155
  112.5 1.4 collective-permute-done.5.two
  113.9 2.7 %collective-permute-done.4.one = bf16[928,128]{1,0:T(8,128)(2,1)S(1)} collective-permute-done((bf16[928,128]{1,0:T(8,128)(2,1)S(1)}, bf16[928,128]{1,0:T(8,128)(2,1)S(1)}, u32[]{:S(2)}, u32[]{:S(2)}) %collective-permute-start.4) | collective-permute-done | bytes 237600 | tf_op jit(solution)/shard_map/ppermute | solution.py:155
  116.6 0.3 shard_map.127.own
  116.9 0.9 collective-permute-start.9
  117.8 1.2 collective-permute-start.8
  119.0 0.0 collective-permute-start.7
  119.0 2.9 %collective-permute-done.9.three = bf16[928,128]{1,0:T(8,128)(2,1)S(1)} collective-permute-done((bf16[928,128]{1,0:T(8,128)(2,1)S(1)}, bf16[928,128]{1,0:T(8,128)(2,1)S(1)}, u32[]{:S(2)}, u32[]{:S(2)}) %collective-permute-start.9) | collective-permute-done | bytes 237600 | tf_op jit(solution)/shard_map/ppermute | solution.py:155
  121.9 2.5 %collective-permute-done.8.two = bf16[928,128]{1,0:T(8,128)(2,1)S(1)} collective-permute-done((bf16[928,128]{1,0:T(8,128)(2,1)S(1)}, bf16[928,128]{1,0:T(8,128)(2,1)S(1)}, u32[]{:S(2)}, u32[]{:S(2)}) %collective-permute-start.8) | collective-permute-done | bytes 237600 | tf_op jit(solution)/shard_map/ppermute | solution.py:155
  124.4 2.7 %collective-permute-done.7.one = bf16[928,128]{1,0:T(8,128)(2,1)S(1)} collective-permute-done((bf16[928,128]{1,0:T(8,128)(2,1)S(1)}, bf16[928,128]{1,0:T(8,128)(2,1)S(1)}, u32[]{:S(2)}, u32[]{:S(2)}) %collective-permute-start.7) | collective-permute-done | bytes 237600 | tf_op jit(solution)/shard_map/ppermute | solution.py:155
  127.1 0.3 shard_map.128.own
  127.4 2.4 %collective-permute-start.12 = (bf16[928,128]{1,0:T(8,128)(2,1)S(1)}, bf16[928,128]{1,0:T(8,128)(2,1)S(1)}, u32[]{:S(2)}, u32[]{:S(2)}) collective-permute-start(bf16[928,128]{1,0:T(8,128)(2,1)S(1)} %shard_map.128.own), channel_id=1, source_target_pairs={{0,96},{4,7},{8,104},{12,15},{16,112},{20,23},{24,120},{28,31},{1,... | collective-permute-start | bytes 712712 | tf_op jit(solution)/shard_map/ppermute | solution.py:157
  129.8 0.3 collective-permute-start.11
  130.0 0.4 collective-permute-start.10
  130.4 4.9 %collective-permute-done.12.three = bf16[928,128]{1,0:T(8,128)(2,1)S(1)} collective-permute-done((bf16[928,128]{1,0:T(8,128)(2,1)S(1)}, bf16[928,128]{1,0:T(8,128)(2,1)S(1)}, u32[]{:S(2)}, u32[]{:S(2)}) %collective-permute-start.12) | collective-permute-done | bytes 237600 | tf_op jit(solution)/shard_map/ppermute | solution.py:157
  135.4 1.0 collective-permute-done.11.two
  136.3 2.7 %collective-permute-done.10.one = bf16[928,128]{1,0:T(8,128)(2,1)S(1)} collective-permute-done((bf16[928,128]{1,0:T(8,128)(2,1)S(1)}, bf16[928,128]{1,0:T(8,128)(2,1)S(1)}, u32[]{:S(2)}, u32[]{:S(2)}) %collective-permute-start.10) | collective-permute-done | bytes 237600 | tf_op jit(solution)/shard_map/ppermute | solution.py:157
  139.0 0.3 shard_map.129.own
  139.3 4.9 %collective-permute-start.13 = (bf16[928,512]{1,0:T(8,128)(2,1)S(1)}, bf16[928,512]{1,0:T(8,128)(2,1)S(1)}, u32[]{:S(2)}, u32[]{:S(2)}) collective-permute-start(bf16[928,512]{1,0:T(8,128)(2,1)S(1)} %shard_map.129.own), channel_id=1, source_target_pairs={{0,4},{4,0},{8,12},{12,8},{16,20},{20,16},{24,28},{28,24},{1,5},{5... | collective-permute-start | bytes 2850824 | tf_op jit(solution)/shard_map/ppermute | solution.py:161
  144.2 1.3 shard_map.130
  145.5 0.8 collective-permute-done.13.other
  146.3 1.8 %shard_map.131 = (f32[768,1024]{1,0:T(8,128)}, f32[153,1024]{1,0:T(8,128)}, f32[1,1]{1,0:T(1,128)}) custom-call(s32[1]{0:T(128)} %bitcast.core, bf16[928,512]{1,0:T(8,128)(2,1)S(1)} %shard_map.129.own, bf16[928,512]{1,0:T(8,128)(2,1)S(1)} %collective-permute-done.13.other, ...), custom_call_target="tpu_custom_call", output_to_operand_aliasing={{0}: (3, {}), {1}: (4, {})} | custom-call | tf_op jit(solution)/shard_map/pallas_call | solution.py:184
  (1 shorter events, 0.0 us)
Async XLA Ops:
  30.7 5.7 %copy-start.7 = (s32[1024]{0:T(1024)S(1)}, s32[1024]{0:T(1024)}, u32[]{:S(2)}) copy-start(s32[1024]{0:T(1024)} %param.17) | copy-start | bytes 12292
  30.7 5.9 %copy-start.6 = (bf16[1024,153]{0,1:T(8,128)(2,1)S(1)}, bf16[1024,153]{0,1:T(8,128)(2,1)}, u32[]{:S(2)}) copy-start(bf16[1024,153]{0,1:T(8,128)(2,1)} %param.19) | copy-start | bytes 940036
  30.7 6.0 %copy-start.1 = (s32[1,1024]{1,0:T(1,128)S(1)}, s32[1,1024]{1,0:T(1,128)}, u32[]{:S(2)}) copy-start(s32[1,1024]{1,0:T(1,128)} %get-tuple-element.19.position) | copy-start | bytes 12292
  30.7 6.0 %copy-start.2 = (s32[48]{0:T(128)S(1)}, s32[48]{0:T(128)}, u32[]{:S(2)}) copy-start(s32[48]{0:T(128)} %row.1) | copy-start | bytes 580
  30.7 6.0 %copy-start.3 = (s32[48]{0:T(128)S(1)}, s32[48]{0:T(128)}, u32[]{:S(2)}) copy-start(s32[48]{0:T(128)} %column.1) | copy-start | bytes 580
  30.7 47.1 %all-to-all-start.1 = ((bf16[128,16,768]{2,1,0:T(8,128)(2,1)}), bf16[128,16,768]{2,1,0:T(8,128)(2,1)}, u32[]{:S(2)}, u32[]{:S(2)}) async-start(bf16[128,16,768]{2,1,0:T(8,128)(2,1)} %bitcast.14), calls=%async_computation.1 | async-start | bytes 6291456 | tf_op jit(solution)/shard_map/all_to_all | solution.py:486
  36.7 1.4 copy-start
  45.2 2.0 %copy-start.4 = (bf16[1024,2048]{1,0:T(8,128)(2,1)}, bf16[1024,2048]{1,0:T(8,128)(2,1)S(1)}, u32[]{:S(2)}) copy-start(bf16[1024,2048]{1,0:T(8,128)(2,1)S(1)} %get-tuple-element.20.moved_far) | copy-start | bytes 12582916
  47.1 1.4 copy-start.5
  94.1 2.6 %collective-permute-start = (bf16[928,512]{1,0:T(8,128)(2,1)S(1)}, bf16[928,512]{1,0:T(8,128)(2,1)S(1)}, u32[]{:S(2)}, u32[]{:S(2)}) collective-permute-start(bf16[928,512]{1,0:T(8,128)(2,1)S(1)} %get-tuple-element.23), channel_id=1, source_target_pairs={{0,4},{4,0},{8,12},{12,8},{16,20},{20,16},{24,28},{28,24},{1,5},{5... | collective-permute-start | bytes 2850824 | tf_op jit(solution)/shard_map/ppermute | solution.py:150
  97.2 9.1 %collective-permute-start.1 = (bf16[928,128]{1,0:T(8,128)(2,1)S(1)}, bf16[928,128]{1,0:T(8,128)(2,1)S(1)}, u32[]{:S(2)}, u32[]{:S(2)}) collective-permute-start(bf16[928,128]{1,0:T(8,128)(2,1)S(1)} %get-tuple-element.25), channel_id=1, source_target_pairs={{0,32},{4,5},{8,40},{12,13},{16,48},{20,21},{24,56},{28,29},{1,33}... | collective-permute-start | bytes 712712 | tf_op jit(solution)/shard_map/ppermute | solution.py:152
  97.6 8.7 %collective-permute-start.2 = (bf16[928,128]{1,0:T(8,128)(2,1)S(1)}, bf16[928,128]{1,0:T(8,128)(2,1)S(1)}, u32[]{:S(2)}, u32[]{:S(2)}) collective-permute-start(bf16[928,128]{1,0:T(8,128)(2,1)S(1)} %get-tuple-element.26), channel_id=1, source_target_pairs={{0,64},{4,6},{8,72},{12,14},{16,80},{20,22},{24,88},{28,30},{1,65}... | collective-permute-start | bytes 712712 | tf_op jit(solution)/shard_map/ppermute | solution.py:152
  99.6 7.3 %collective-permute-start.3 = (bf16[928,128]{1,0:T(8,128)(2,1)S(1)}, bf16[928,128]{1,0:T(8,128)(2,1)S(1)}, u32[]{:S(2)}, u32[]{:S(2)}) collective-permute-start(bf16[928,128]{1,0:T(8,128)(2,1)S(1)} %get-tuple-element.27), channel_id=1, source_target_pairs={{0,96},{4,7},{8,104},{12,15},{16,112},{20,23},{24,120},{28,31},{1,... | collective-permute-start | bytes 712712 | tf_op jit(solution)/shard_map/ppermute | solution.py:152
  107.2 5.3 %collective-permute-start.6 = (bf16[928,128]{1,0:T(8,128)(2,1)S(1)}, bf16[928,128]{1,0:T(8,128)(2,1)S(1)}, u32[]{:S(2)}, u32[]{:S(2)}) collective-permute-start(bf16[928,128]{1,0:T(8,128)(2,1)S(1)} %shard_map.126.own), channel_id=1, source_target_pairs={{0,3},{4,28},{8,11},{12,4},{16,19},{20,12},{24,27},{28,20},{1,0},{... | collective-permute-start | bytes 712712 | tf_op jit(solution)/shard_map/ppermute | solution.py:155
  107.3 6.6 %collective-permute-start.5 = (bf16[928,128]{1,0:T(8,128)(2,1)S(1)}, bf16[928,128]{1,0:T(8,128)(2,1)S(1)}, u32[]{:S(2)}, u32[]{:S(2)}) collective-permute-start(bf16[928,128]{1,0:T(8,128)(2,1)S(1)} %shard_map.126.own), channel_id=1, source_target_pairs={{0,2},{4,20},{8,10},{12,28},{16,18},{20,4},{24,26},{28,12},{1,3},{... | collective-permute-start | bytes 712712 | tf_op jit(solution)/shard_map/ppermute | solution.py:155
  108.9 7.7 %collective-permute-start.4 = (bf16[928,128]{1,0:T(8,128)(2,1)S(1)}, bf16[928,128]{1,0:T(8,128)(2,1)S(1)}, u32[]{:S(2)}, u32[]{:S(2)}) collective-permute-start(bf16[928,128]{1,0:T(8,128)(2,1)S(1)} %shard_map.126.own), channel_id=1, source_target_pairs={{0,1},{4,12},{8,9},{12,20},{16,17},{20,28},{24,25},{28,4},{1,2},{5... | collective-permute-start | bytes 712712 | tf_op jit(solution)/shard_map/ppermute | solution.py:155
  116.9 5.0 %collective-permute-start.9 = (bf16[928,128]{1,0:T(8,128)(2,1)S(1)}, bf16[928,128]{1,0:T(8,128)(2,1)S(1)}, u32[]{:S(2)}, u32[]{:S(2)}) collective-permute-start(bf16[928,128]{1,0:T(8,128)(2,1)S(1)} %shard_map.127.own), channel_id=1, source_target_pairs={{0,24},{4,100},{8,0},{12,108},{16,8},{20,116},{24,16},{28,124},{1,... | collective-permute-start | bytes 712712 | tf_op jit(solution)/shard_map/ppermute | solution.py:155
  117.8 6.6 %collective-permute-start.8 = (bf16[928,128]{1,0:T(8,128)(2,1)S(1)}, bf16[928,128]{1,0:T(8,128)(2,1)S(1)}, u32[]{:S(2)}, u32[]{:S(2)}) collective-permute-start(bf16[928,128]{1,0:T(8,128)(2,1)S(1)} %shard_map.127.own), channel_id=1, source_target_pairs={{0,16},{4,68},{8,24},{12,76},{16,0},{20,84},{24,8},{28,92},{1,17},... | collective-permute-start | bytes 712712 | tf_op jit(solution)/shard_map/ppermute | solution.py:155
  119.0 8.1 %collective-permute-start.7 = (bf16[928,128]{1,0:T(8,128)(2,1)S(1)}, bf16[928,128]{1,0:T(8,128)(2,1)S(1)}, u32[]{:S(2)}, u32[]{:S(2)}) collective-permute-start(bf16[928,128]{1,0:T(8,128)(2,1)S(1)} %shard_map.127.own), channel_id=1, source_target_pairs={{0,8},{4,36},{8,16},{12,44},{16,24},{20,52},{24,0},{28,60},{1,9},{... | collective-permute-start | bytes 712712 | tf_op jit(solution)/shard_map/ppermute | solution.py:155
  127.4 8.0 %collective-permute-start.12 = (bf16[928,128]{1,0:T(8,128)(2,1)S(1)}, bf16[928,128]{1,0:T(8,128)(2,1)S(1)}, u32[]{:S(2)}, u32[]{:S(2)}) collective-permute-start(bf16[928,128]{1,0:T(8,128)(2,1)S(1)} %shard_map.128.own), channel_id=1, source_target_pairs={{0,96},{4,7},{8,104},{12,15},{16,112},{20,23},{24,120},{28,31},{1,... | collective-permute-start | bytes 712712 | tf_op jit(solution)/shard_map/ppermute | solution.py:157
  129.8 6.6 %collective-permute-start.11 = (bf16[928,128]{1,0:T(8,128)(2,1)S(1)}, bf16[928,128]{1,0:T(8,128)(2,1)S(1)}, u32[]{:S(2)}, u32[]{:S(2)}) collective-permute-start(bf16[928,128]{1,0:T(8,128)(2,1)S(1)} %shard_map.128.own), channel_id=1, source_target_pairs={{0,64},{4,6},{8,72},{12,14},{16,80},{20,22},{24,88},{28,30},{1,65}... | collective-permute-start | bytes 712712 | tf_op jit(solution)/shard_map/ppermute | solution.py:157
  130.0 9.0 %collective-permute-start.10 = (bf16[928,128]{1,0:T(8,128)(2,1)S(1)}, bf16[928,128]{1,0:T(8,128)(2,1)S(1)}, u32[]{:S(2)}, u32[]{:S(2)}) collective-permute-start(bf16[928,128]{1,0:T(8,128)(2,1)S(1)} %shard_map.128.own), channel_id=1, source_target_pairs={{0,32},{4,5},{8,40},{12,13},{16,48},{20,21},{24,56},{28,29},{1,33}... | collective-permute-start | bytes 712712 | tf_op jit(solution)/shard_map/ppermute | solution.py:157
  139.3 7.0 %collective-permute-start.13 = (bf16[928,512]{1,0:T(8,128)(2,1)S(1)}, bf16[928,512]{1,0:T(8,128)(2,1)S(1)}, u32[]{:S(2)}, u32[]{:S(2)}) collective-permute-start(bf16[928,512]{1,0:T(8,128)(2,1)S(1)} %shard_map.129.own), channel_id=1, source_target_pairs={{0,4},{4,0},{8,12},{12,8},{16,20},{20,16},{24,28},{28,24},{1,5},{5... | collective-permute-start | bytes 2850824 | tf_op jit(solution)/shard_map/ppermute | solution.py:161

commit v9 on v8

--- a/solution.py
+++ b/solution.py
@@ -379,8 +379,8 @@
         before = jnp.dot(mixed, layer_one[...], preferred_element_type=jnp.float32)
         square = before * before
         rate = 0.7978845608028654
-        bend = jnp.tanh(rate * before * (1.0 + 0.044715 * square))
-        rise = 0.5 * (1.0 + bend)
+        bend = jnp.tanh(before * (rate + (rate * 0.044715) * square))
+        rise = 0.5 + 0.5 * bend
         active = (before * rise).astype(jnp.bfloat16)
         hidden[rows, :] = active
         slope[rows, :] = rise + 0.5 * before * (1.0 - bend * bend) * (
@@ -475,11 +475,11 @@
             pltpu.SMEM(wanted.shape, jnp.int32),
             pltpu.VMEM(features.shape, bf),
             pltpu.VMEM((features.shape[0] * PITCH + 64, 128), jnp.float32),
-            pltpu.VMEM((128 * PITCH + 64, 128), jnp.float32),
+            pltpu.VMEM((256 * PITCH + 64, 128), jnp.float32),
             pltpu.VMEM((slots, width), bf),
             pltpu.SemaphoreType.DMA,
             pltpu.SemaphoreType.DMA((8,)),
-            pltpu.SemaphoreType.DMA((slots // 128,)),
+            pltpu.SemaphoreType.DMA((slots // 256,)),
         ],
         compiler_params=pltpu.CompilerParams(vmem_limit_bytes=56 << 20),
     )(wanted, features)

time: 149 us -> 149 us (level)
  no operation moved by 1% of the time
where the time goes in v9:
time: 149 us; the launch traced here: 148 us
  waiting for transfers between devices  63.4 us (43%)
  Pallas kernels  36.3 us (24%)
  blocking collectives  21.7 us (15%)
  starting transfers between devices  20.2 us (14%)
  local copies, waits for them, and re-layouts  5.05 us (3%)
  between operations  1.64 us (1%)
    all_to_all x1, waiting for transfers between devices, on_device(): lax.all_to_all(found, AXES, split_axis=0, concat_axis=0, tiled=True)  29.1 us
    all_to_all x1, blocking collectives, on_device(): lax.all_to_all(requests, AXES, split_axis=0, concat_axis=0, tiled=True)  21.7 us
    pallas_call x1, Pallas kernels, on_device(): pl.pallas_call(partial(train, classes=classes), out_shape=[jax.ShapeDtype...  16 us
    ppermute x6, waiting for transfers between devices, sum_over_devices(): got = [lax.ppermute(total, AXES, shift_pairs(axes, k)) for k in (1, 2, 3)]  15.9 us
    ppermute x3, waiting for transfers between devices, sum_over_devices(): got = [lax.ppermute(total, AXES, shift_pairs(FIRST, k)) for k in (1, 2, 3)]  8.6 us
    pallas_call x1, Pallas kernels, on_device(): call(build_spread, [jax.ShapeDtypeStruct((nodes, nodes), bf), jax.ShapeDt...  7.2 us
    ppermute x3, waiting for transfers between devices, sum_over_devices(): lax.ppermute(part, AXES, shift_pairs(FIRST, k + 1))  6.79 us
    pallas_call x1, Pallas kernels, on_device(): pl.pallas_call(fetch_rows, out_shape=jax.ShapeDtypeStruct((slots, width),...  6.53 us
  transfers between devices with their start and end apart: 15, of which 14 were waited for; matrix products, arithmetic and copies ran while one was open for 0% of the time, Pallas kernels for 6%

profile of v9, /device:TPU:1, one launch (start us, length us, event | category | flops | bytes accessed | tf_op | source)
XLA Modules:
  0.0 148.3 jit_solution(7650530344422903217)
XLA Ops:
  0.6 1.8 %shard_map.121 = (s32[128,16]{1,0:T(8,128)}, s32[1,1024]{1,0:T(1,128)}) custom-call(s32[1,1024]{1,0:T(1,128)} %bitcast.20, s32[1,1024]{1,0:T(1,128)} %bitcast.21), custom_call_target="tpu_custom_call" | custom-call | tf_op jit(solution)/shard_map/pallas_call | solution.py:455
  2.5 21.7 %all_to_all.22 = s32[128,1,16]{2,1,0:T(1,128)} all-to-all(s32[128,1,16]{2,1,0:T(1,128)} %bitcast.18), channel_id=1, replica_groups=mesh['store'=32,'batch'=4] {'store','batch'}, dimensions={0} | all-to-all | bytes 16384 | tf_op jit(solution)/shard_map/all_to_all | solution.py:465
  24.2 6.5 %shard_map.122 = bf16[2048,768]{1,0:T(8,128)(2,1)} custom-call(s32[128,16]{1,0:T(8,128)} %bitcast.17, bf16[4096,768]{1,0:T(8,128)(2,1)} %table.1), custom_call_target="tpu_custom_call" | custom-call | tf_op jit(solution)/shard_map/pallas_call | solution.py:469
  30.7 0.0 copy-start.7
  30.7 0.0 copy-start.6
  30.8 0.0 copy-start.1
  30.8 0.0 copy-start.2
  30.8 0.0 copy-start.3
  30.8 5.0 %all-to-all-start.1 = ((bf16[128,16,768]{2,1,0:T(8,128)(2,1)}), bf16[128,16,768]{2,1,0:T(8,128)(2,1)}, u32[]{:S(2)}, u32[]{:S(2)}) async-start(bf16[128,16,768]{2,1,0:T(8,128)(2,1)} %bitcast.14), calls=%async_computation.1 | async-start | bytes 6291456 | tf_op jit(solution)/shard_map/all_to_all | solution.py:486
  36.4 0.0 copy-done.7
  36.4 0.2 copy.17.labels_far
  36.7 0.0 copy-done.6
  36.7 0.0 copy-done.1
  36.7 0.0 copy-done.2
  36.8 0.0 copy-done.3
  36.8 0.0 copy-start
  36.8 1.4 copy-done
  38.2 7.2 %shard_map.123 = (bf16[1024,1024]{1,0:T(8,128)(2,1)S(1)}, bf16[1024,2048]{1,0:T(8,128)(2,1)S(1)}) custom-call(s32[48]{0:T(128)S(1)} %copy-done.2, s32[48]{0:T(128)S(1)} %copy-done.3, s32[1]{0:T(128)S(6)} %copy.20.count, bf16[48,128,128]{2,1,0:T(8,128)(2,1)S(1)} %copy-done, s32[1,1024]{1,0:T(1,128)S(1)} %copy-done.1), custom_call_target="tpu_custom_call" | custom-call | flops 4294967296 | bytes 12582912 | tf_op jit(solution)/shard_map/pallas_call | solution.py:487
  45.4 0.0 copy-start.4
  45.4 1.9 %copy-done.4 = bf16[1024,2048]{1,0:T(8,128)(2,1)} copy-done((bf16[1024,2048]{1,0:T(8,128)(2,1)}, bf16[1024,2048]{1,0:T(8,128)(2,1)S(1)}, u32[]{:S(2)}) %copy-start.4) | copy-done | bytes 4194328
  47.3 0.0 copy-start.5
  47.3 1.4 copy-done.5
  48.7 29.1 %all-to-all-done.1 = bf16[128,16,768]{2,1,0:T(8,128)(2,1)} async-done(((bf16[128,16,768]{2,1,0:T(8,128)(2,1)}), bf16[128,16,768]{2,1,0:T(8,128)(2,1)}, u32[]{:S(2)}, u32[]{:S(2)}) %all-to-all-start.1) | async-done | bytes 3145760 | tf_op jit(solution)/shard_map/all_to_all | solution.py:486
  77.8 16.0 %shard_map.124 = (bf16[928,512]{1,0:T(8,128)(2,1)S(1)}, bf16[928,512]{1,0:T(8,128)(2,1)S(1)}) custom-call(s32[1]{0:T(128)} %bitcast.core, bf16[2048,768]{1,0:T(8,128)(2,1)} %bitcast.8.arrived_far, bf16[1024,2048]{1,0:T(8,128)(2,1)} %copy-done.4, bf16[1024,1024]{1,0:T(8,128)(2,1)} %copy-done.5, bf16[768,1024]{1,0:T(8,128)(2,1)} %one_far.1, ...), custom_call_target="tpu_custom_call" | custom-call | flops 12884901888 | bytes 16777216 | tf_op jit(solution)/shard_map/pallas_call | solution.py:502
  93.8 0.6 collective-permute-start
  94.4 2.3 %collective-permute-done.arrived = bf16[928,512]{1,0:T(8,128)(2,1)S(1)} collective-permute-done((bf16[928,512]{1,0:T(8,128)(2,1)S(1)}, bf16[928,512]{1,0:T(8,128)(2,1)S(1)}, u32[]{:S(2)}, u32[]{:S(2)}) %collective-permute-start) | collective-permute-done | bytes 950304 | tf_op jit(solution)/shard_map/ppermute | solution.py:150
  96.6 0.5 shard_map.125
  97.2 0.4 collective-permute-start.1
  97.6 2.0 %collective-permute-start.2 = (bf16[928,128]{1,0:T(8,128)(2,1)S(1)}, bf16[928,128]{1,0:T(8,128)(2,1)S(1)}, u32[]{:S(2)}, u32[]{:S(2)}) collective-permute-start(bf16[928,128]{1,0:T(8,128)(2,1)S(1)} %get-tuple-element.26), channel_id=1, source_target_pairs={{0,64},{4,6},{8,72},{12,14},{16,80},{20,22},{24,88},{28,30},{1,65}... | collective-permute-start | bytes 712712 | tf_op jit(solution)/shard_map/ppermute | solution.py:152
  99.6 0.5 collective-permute-start.3
  100.1 6.2 %collective-permute-done.1.one = bf16[928,128]{1,0:T(8,128)(2,1)S(1)} collective-permute-done((bf16[928,128]{1,0:T(8,128)(2,1)S(1)}, bf16[928,128]{1,0:T(8,128)(2,1)S(1)}, u32[]{:S(2)}, u32[]{:S(2)}) %collective-permute-start.1) | collective-permute-done | bytes 237600 | tf_op jit(solution)/shard_map/ppermute | solution.py:152
  106.2 0.0 collective-permute-done.2.two
  106.3 0.6 collective-permute-done.3.three
  106.9 0.3 shard_map.126.own
  107.2 0.1 collective-permute-start.6
  107.3 1.6 %collective-permute-start.5 = (bf16[928,128]{1,0:T(8,128)(2,1)S(1)}, bf16[928,128]{1,0:T(8,128)(2,1)S(1)}, u32[]{:S(2)}, u32[]{:S(2)}) collective-permute-start(bf16[928,128]{1,0:T(8,128)(2,1)S(1)} %shard_map.126.own), channel_id=1, source_target_pairs={{0,2},{4,20},{8,10},{12,28},{16,18},{20,4},{24,26},{28,12},{1,3},{... | collective-permute-start | bytes 712712 | tf_op jit(solution)/shard_map/ppermute | solution.py:155
  108.9 0.0 collective-permute-start.4
  108.9 3.5 %collective-permute-done.6.three = bf16[928,128]{1,0:T(8,128)(2,1)S(1)} collective-permute-done((bf16[928,128]{1,0:T(8,128)(2,1)S(1)}, bf16[928,128]{1,0:T(8,128)(2,1)S(1)}, u32[]{:S(2)}, u32[]{:S(2)}) %collective-permute-start.6) | collective-permute-done | bytes 237600 | tf_op jit(solution)/shard_map/ppermute | solution.py:155
  112.4 1.4 collective-permute-done.5.two
  113.9 2.7 %collective-permute-done.4.one = bf16[928,128]{1,0:T(8,128)(2,1)S(1)} collective-permute-done((bf16[928,128]{1,0:T(8,128)(2,1)S(1)}, bf16[928,128]{1,0:T(8,128)(2,1)S(1)}, u32[]{:S(2)}, u32[]{:S(2)}) %collective-permute-start.4) | collective-permute-done | bytes 237600 | tf_op jit(solution)/shard_map/ppermute | solution.py:155
  116.6 0.3 shard_map.127.own
  116.9 0.9 collective-permute-start.9
  117.8 1.2 collective-permute-start.8
  119.0 0.0 collective-permute-start.7
  119.0 2.9 %collective-permute-done.9.three = bf16[928,128]{1,0:T(8,128)(2,1)S(1)} collective-permute-done((bf16[928,128]{1,0:T(8,128)(2,1)S(1)}, bf16[928,128]{1,0:T(8,128)(2,1)S(1)}, u32[]{:S(2)}, u32[]{:S(2)}) %collective-permute-start.9) | collective-permute-done | bytes 237600 | tf_op jit(solution)/shard_map/ppermute | solution.py:155
  121.9 2.5 %collective-permute-done.8.two = bf16[928,128]{1,0:T(8,128)(2,1)S(1)} collective-permute-done((bf16[928,128]{1,0:T(8,128)(2,1)S(1)}, bf16[928,128]{1,0:T(8,128)(2,1)S(1)}, u32[]{:S(2)}, u32[]{:S(2)}) %collective-permute-start.8) | collective-permute-done | bytes 237600 | tf_op jit(solution)/shard_map/ppermute | solution.py:155
  124.4 2.7 %collective-permute-done.7.one = bf16[928,128]{1,0:T(8,128)(2,1)S(1)} collective-permute-done((bf16[928,128]{1,0:T(8,128)(2,1)S(1)}, bf16[928,128]{1,0:T(8,128)(2,1)S(1)}, u32[]{:S(2)}, u32[]{:S(2)}) %collective-permute-start.7) | collective-permute-done | bytes 237600 | tf_op jit(solution)/shard_map/ppermute | solution.py:155
  127.1 0.3 shard_map.128.own
  127.4 2.4 %collective-permute-start.12 = (bf16[928,128]{1,0:T(8,128)(2,1)S(1)}, bf16[928,128]{1,0:T(8,128)(2,1)S(1)}, u32[]{:S(2)}, u32[]{:S(2)}) collective-permute-start(bf16[928,128]{1,0:T(8,128)(2,1)S(1)} %shard_map.128.own), channel_id=1, source_target_pairs={{0,96},{4,7},{8,104},{12,15},{16,112},{20,23},{24,120},{28,31},{1,... | collective-permute-start | bytes 712712 | tf_op jit(solution)/shard_map/ppermute | solution.py:157
  129.7 0.3 collective-permute-start.11
  130.0 0.4 collective-permute-start.10
  130.4 4.9 %collective-permute-done.12.three = bf16[928,128]{1,0:T(8,128)(2,1)S(1)} collective-permute-done((bf16[928,128]{1,0:T(8,128)(2,1)S(1)}, bf16[928,128]{1,0:T(8,128)(2,1)S(1)}, u32[]{:S(2)}, u32[]{:S(2)}) %collective-permute-start.12) | collective-permute-done | bytes 237600 | tf_op jit(solution)/shard_map/ppermute | solution.py:157
  135.3 1.0 collective-permute-done.11.two
  136.3 2.7 %collective-permute-done.10.one = bf16[928,128]{1,0:T(8,128)(2,1)S(1)} collective-permute-done((bf16[928,128]{1,0:T(8,128)(2,1)S(1)}, bf16[928,128]{1,0:T(8,128)(2,1)S(1)}, u32[]{:S(2)}, u32[]{:S(2)}) %collective-permute-start.10) | collective-permute-done | bytes 237600 | tf_op jit(solution)/shard_map/ppermute | solution.py:157
  139.0 0.3 shard_map.129.own
  139.3 4.9 %collective-permute-start.13 = (bf16[928,512]{1,0:T(8,128)(2,1)S(1)}, bf16[928,512]{1,0:T(8,128)(2,1)S(1)}, u32[]{:S(2)}, u32[]{:S(2)}) collective-permute-start(bf16[928,512]{1,0:T(8,128)(2,1)S(1)} %shard_map.129.own), channel_id=1, source_target_pairs={{0,4},{4,0},{8,12},{12,8},{16,20},{20,16},{24,28},{28,24},{1,5},{5... | collective-permute-start | bytes 2850824 | tf_op jit(solution)/shard_map/ppermute | solution.py:161
  144.2 1.3 shard_map.130
  145.5 0.8 collective-permute-done.13.other
  146.3 1.8 %shard_map.131 = (f32[768,1024]{1,0:T(8,128)}, f32[153,1024]{1,0:T(8,128)}, f32[1,1]{1,0:T(1,128)}) custom-call(s32[1]{0:T(128)} %bitcast.core, bf16[928,512]{1,0:T(8,128)(2,1)S(1)} %shard_map.129.own, bf16[928,512]{1,0:T(8,128)(2,1)S(1)} %collective-permute-done.13.other, ...), custom_call_target="tpu_custom_call", output_to_operand_aliasing={{0}: (3, {}), {1}: (4, {})} | custom-call | tf_op jit(solution)/shard_map/pallas_call | solution.py:184
  (1 shorter events, 0.0 us)
Async XLA Ops:
  30.7 5.7 %copy-start.7 = (s32[1024]{0:T(1024)S(1)}, s32[1024]{0:T(1024)}, u32[]{:S(2)}) copy-start(s32[1024]{0:T(1024)} %param.17) | copy-start | bytes 12292
  30.7 5.9 %copy-start.6 = (bf16[1024,153]{0,1:T(8,128)(2,1)S(1)}, bf16[1024,153]{0,1:T(8,128)(2,1)}, u32[]{:S(2)}) copy-start(bf16[1024,153]{0,1:T(8,128)(2,1)} %param.19) | copy-start | bytes 940036
  30.8 6.0 %copy-start.1 = (s32[1,1024]{1,0:T(1,128)S(1)}, s32[1,1024]{1,0:T(1,128)}, u32[]{:S(2)}) copy-start(s32[1,1024]{1,0:T(1,128)} %get-tuple-element.19.position) | copy-start | bytes 12292
  30.8 6.0 %copy-start.2 = (s32[48]{0:T(128)S(1)}, s32[48]{0:T(128)}, u32[]{:S(2)}) copy-start(s32[48]{0:T(128)} %row.1) | copy-start | bytes 580
  30.8 6.0 %copy-start.3 = (s32[48]{0:T(128)S(1)}, s32[48]{0:T(128)}, u32[]{:S(2)}) copy-start(s32[48]{0:T(128)} %column.1) | copy-start | bytes 580
  30.8 47.1 %all-to-all-start.1 = ((bf16[128,16,768]{2,1,0:T(8,128)(2,1)}), bf16[128,16,768]{2,1,0:T(8,128)(2,1)}, u32[]{:S(2)}, u32[]{:S(2)}) async-start(bf16[128,16,768]{2,1,0:T(8,128)(2,1)} %bitcast.14), calls=%async_computation.1 | async-start | bytes 6291456 | tf_op jit(solution)/shard_map/all_to_all | solution.py:486
  36.8 1.4 copy-start
  45.4 2.0 %copy-start.4 = (bf16[1024,2048]{1,0:T(8,128)(2,1)}, bf16[1024,2048]{1,0:T(8,128)(2,1)S(1)}, u32[]{:S(2)}) copy-start(bf16[1024,2048]{1,0:T(8,128)(2,1)S(1)} %get-tuple-element.20.moved_far) | copy-start | bytes 12582916
  47.3 1.4 copy-start.5
  93.8 2.8 %collective-permute-start = (bf16[928,512]{1,0:T(8,128)(2,1)S(1)}, bf16[928,512]{1,0:T(8,128)(2,1)S(1)}, u32[]{:S(2)}, u32[]{:S(2)}) collective-permute-start(bf16[928,512]{1,0:T(8,128)(2,1)S(1)} %get-tuple-element.23), channel_id=1, source_target_pairs={{0,4},{4,0},{8,12},{12,8},{16,20},{20,16},{24,28},{28,24},{1,5},{5... | collective-permute-start | bytes 2850824 | tf_op jit(solution)/shard_map/ppermute | solution.py:150
  97.2 9.1 %collective-permute-start.1 = (bf16[928,128]{1,0:T(8,128)(2,1)S(1)}, bf16[928,128]{1,0:T(8,128)(2,1)S(1)}, u32[]{:S(2)}, u32[]{:S(2)}) collective-permute-start(bf16[928,128]{1,0:T(8,128)(2,1)S(1)} %get-tuple-element.25), channel_id=1, source_target_pairs={{0,32},{4,5},{8,40},{12,13},{16,48},{20,21},{24,56},{28,29},{1,33}... | collective-permute-start | bytes 712712 | tf_op jit(solution)/shard_map/ppermute | solution.py:152
  97.6 8.7 %collective-permute-start.2 = (bf16[928,128]{1,0:T(8,128)(2,1)S(1)}, bf16[928,128]{1,0:T(8,128)(2,1)S(1)}, u32[]{:S(2)}, u32[]{:S(2)}) collective-permute-start(bf16[928,128]{1,0:T(8,128)(2,1)S(1)} %get-tuple-element.26), channel_id=1, source_target_pairs={{0,64},{4,6},{8,72},{12,14},{16,80},{20,22},{24,88},{28,30},{1,65}... | collective-permute-start | bytes 712712 | tf_op jit(solution)/shard_map/ppermute | solution.py:152
  99.6 7.3 %collective-permute-start.3 = (bf16[928,128]{1,0:T(8,128)(2,1)S(1)}, bf16[928,128]{1,0:T(8,128)(2,1)S(1)}, u32[]{:S(2)}, u32[]{:S(2)}) collective-permute-start(bf16[928,128]{1,0:T(8,128)(2,1)S(1)} %get-tuple-element.27), channel_id=1, source_target_pairs={{0,96},{4,7},{8,104},{12,15},{16,112},{20,23},{24,120},{28,31},{1,... | collective-permute-start | bytes 712712 | tf_op jit(solution)/shard_map/ppermute | solution.py:152
  107.2 5.3 %collective-permute-start.6 = (bf16[928,128]{1,0:T(8,128)(2,1)S(1)}, bf16[928,128]{1,0:T(8,128)(2,1)S(1)}, u32[]{:S(2)}, u32[]{:S(2)}) collective-permute-start(bf16[928,128]{1,0:T(8,128)(2,1)S(1)} %shard_map.126.own), channel_id=1, source_target_pairs={{0,3},{4,28},{8,11},{12,4},{16,19},{20,12},{24,27},{28,20},{1,0},{... | collective-permute-start | bytes 712712 | tf_op jit(solution)/shard_map/ppermute | solution.py:155
  107.3 6.6 %collective-permute-start.5 = (bf16[928,128]{1,0:T(8,128)(2,1)S(1)}, bf16[928,128]{1,0:T(8,128)(2,1)S(1)}, u32[]{:S(2)}, u32[]{:S(2)}) collective-permute-start(bf16[928,128]{1,0:T(8,128)(2,1)S(1)} %shard_map.126.own), channel_id=1, source_target_pairs={{0,2},{4,20},{8,10},{12,28},{16,18},{20,4},{24,26},{28,12},{1,3},{... | collective-permute-start | bytes 712712 | tf_op jit(solution)/shard_map/ppermute | solution.py:155
  108.9 7.7 %collective-permute-start.4 = (bf16[928,128]{1,0:T(8,128)(2,1)S(1)}, bf16[928,128]{1,0:T(8,128)(2,1)S(1)}, u32[]{:S(2)}, u32[]{:S(2)}) collective-permute-start(bf16[928,128]{1,0:T(8,128)(2,1)S(1)} %shard_map.126.own), channel_id=1, source_target_pairs={{0,1},{4,12},{8,9},{12,20},{16,17},{20,28},{24,25},{28,4},{1,2},{5... | collective-permute-start | bytes 712712 | tf_op jit(solution)/shard_map/ppermute | solution.py:155
  116.9 5.0 %collective-permute-start.9 = (bf16[928,128]{1,0:T(8,128)(2,1)S(1)}, bf16[928,128]{1,0:T(8,128)(2,1)S(1)}, u32[]{:S(2)}, u32[]{:S(2)}) collective-permute-start(bf16[928,128]{1,0:T(8,128)(2,1)S(1)} %shard_map.127.own), channel_id=1, source_target_pairs={{0,24},{4,100},{8,0},{12,108},{16,8},{20,116},{24,16},{28,124},{1,... | collective-permute-start | bytes 712712 | tf_op jit(solution)/shard_map/ppermute | solution.py:155
  117.8 6.6 %collective-permute-start.8 = (bf16[928,128]{1,0:T(8,128)(2,1)S(1)}, bf16[928,128]{1,0:T(8,128)(2,1)S(1)}, u32[]{:S(2)}, u32[]{:S(2)}) collective-permute-start(bf16[928,128]{1,0:T(8,128)(2,1)S(1)} %shard_map.127.own), channel_id=1, source_target_pairs={{0,16},{4,68},{8,24},{12,76},{16,0},{20,84},{24,8},{28,92},{1,17},... | collective-permute-start | bytes 712712 | tf_op jit(solution)/shard_map/ppermute | solution.py:155
  119.0 8.1 %collective-permute-start.7 = (bf16[928,128]{1,0:T(8,128)(2,1)S(1)}, bf16[928,128]{1,0:T(8,128)(2,1)S(1)}, u32[]{:S(2)}, u32[]{:S(2)}) collective-permute-start(bf16[928,128]{1,0:T(8,128)(2,1)S(1)} %shard_map.127.own), channel_id=1, source_target_pairs={{0,8},{4,36},{8,16},{12,44},{16,24},{20,52},{24,0},{28,60},{1,9},{... | collective-permute-start | bytes 712712 | tf_op jit(solution)/shard_map/ppermute | solution.py:155
  127.4 8.0 %collective-permute-start.12 = (bf16[928,128]{1,0:T(8,128)(2,1)S(1)}, bf16[928,128]{1,0:T(8,128)(2,1)S(1)}, u32[]{:S(2)}, u32[]{:S(2)}) collective-permute-start(bf16[928,128]{1,0:T(8,128)(2,1)S(1)} %shard_map.128.own), channel_id=1, source_target_pairs={{0,96},{4,7},{8,104},{12,15},{16,112},{20,23},{24,120},{28,31},{1,... | collective-permute-start | bytes 712712 | tf_op jit(solution)/shard_map/ppermute | solution.py:157
  129.7 6.6 %collective-permute-start.11 = (bf16[928,128]{1,0:T(8,128)(2,1)S(1)}, bf16[928,128]{1,0:T(8,128)(2,1)S(1)}, u32[]{:S(2)}, u32[]{:S(2)}) collective-permute-start(bf16[928,128]{1,0:T(8,128)(2,1)S(1)} %shard_map.128.own), channel_id=1, source_target_pairs={{0,64},{4,6},{8,72},{12,14},{16,80},{20,22},{24,88},{28,30},{1,65}... | collective-permute-start | bytes 712712 | tf_op jit(solution)/shard_map/ppermute | solution.py:157
  130.0 9.0 %collective-permute-start.10 = (bf16[928,128]{1,0:T(8,128)(2,1)S(1)}, bf16[928,128]{1,0:T(8,128)(2,1)S(1)}, u32[]{:S(2)}, u32[]{:S(2)}) collective-permute-start(bf16[928,128]{1,0:T(8,128)(2,1)S(1)} %shard_map.128.own), channel_id=1, source_target_pairs={{0,32},{4,5},{8,40},{12,13},{16,48},{20,21},{24,56},{28,29},{1,33}... | collective-permute-start | bytes 712712 | tf_op jit(solution)/shard_map/ppermute | solution.py:157
  139.3 7.0 %collective-permute-start.13 = (bf16[928,512]{1,0:T(8,128)(2,1)S(1)}, bf16[928,512]{1,0:T(8,128)(2,1)S(1)}, u32[]{:S(2)}, u32[]{:S(2)}) collective-permute-start(bf16[928,512]{1,0:T(8,128)(2,1)S(1)} %shard_map.129.own), channel_id=1, source_target_pairs={{0,4},{4,0},{8,12},{12,8},{16,20},{20,16},{24,28},{28,24},{1,5},{5... | collective-permute-start | bytes 2850824 | tf_op jit(solution)/shard_map/ppermute | solution.py:161
